TPU v7x, 256 devices: a whole 4x4x8 slice. The times are simulated.
256 devices in a mesh: tp: 16 (over y, x), pp: 16 (over z, core).
Axes of the slice: x: 4, y: 4, z: 8, core: 2. Of those that a mesh axis runs over, the one named last changes fastest.
Arguments:
- tokens: bfloat16 [16, 512, 8192], P('pp', None, 'tp'), may hold values from -28 to 28
- norm_gain: float32 [16, 8192], P('pp'), may hold values from 0.1 to 1.9
- w_query: bfloat16 [16, 8192, 4096], P('pp', None, 'tp'), may hold values from -2 to 2
- w_key: bfloat16 [16, 8192, 512], P('pp', None, 'tp'), may hold values from -1 to 1
- w_value: bfloat16 [16, 8192, 512], P('pp', None, 'tp'), may hold values from -0.0625 to 0.0625
- w_output: bfloat16 [16, 4096, 8192], P('pp', 'tp'), may hold values from -0.09375 to 0.09375
Outputs:
- handoff: float32 [16, 512, 8192], P('pp', None, 'tp')
All inputs are finite; a program needn't handle non-finite values. Where the computation divides by a largest or mean magnitude, that divisor is 1e-20 or more.
Results may differ from a plain program's by a relative error of at most 0.0065.
Values may be sent and summed in bfloat16 or wider, within the bound.
No kernel may reach another device: no remote copies, remote signals or barrier semaphores. Data moves between devices by JAX's collectives and lax.ppermute only.
A program may use at most 128 MiB of HBM per device.

v0:
```python
import math

import jax
import jax.numpy as jnp
from jax import lax
from jax.sharding import PartitionSpec as P

KVH = 4
HD = 128
BLOCK = 128


def from_partner(block, axis, distance):
    count = lax.axis_size(axis)
    route = []
    for low in range(count):
        high = low | 1 << distance
        if high != low and high < count:
            route += [(low, high), (high, low)]
    return lax.ppermute(block, axis, route)


def from_behind(block, axis, distance):
    devices = range(lax.axis_size(axis))
    route = [((i - distance) % len(devices), i) for i in devices]
    return lax.ppermute(block, axis, route)


def rotate(values, heads, head_size):
    rows = values.shape[0]
    half = head_size // 2
    freq = jnp.exp(jnp.arange(half, dtype=jnp.float32) * (-2.0 * math.log(500000.0) / head_size))
    angle = jnp.arange(rows, dtype=jnp.float32)[:, None] * freq[None, :]
    cosine = jnp.cos(angle)[:, None, :]
    sine = jnp.sin(angle)[:, None, :]
    shaped = values.reshape(rows, heads, head_size)
    first = shaped[..., :half]
    second = shaped[..., half:]
    return jnp.concatenate(
        [first * cosine - second * sine, second * cosine + first * sine], axis=-1
    )


def quantize(values, block):
    rows, cols = values.shape
    blocks = values.reshape(rows, cols // block, block)
    scale = (jnp.max(jnp.abs(blocks), axis=-1) + 1e-06).astype(jnp.bfloat16)
    quant = (blocks / scale.astype(jnp.float32)[..., None]).astype(jnp.bfloat16)
    return (quant.reshape(rows, cols), scale)


def dequantize(quant, scale, block):
    rows, cols = quant.shape
    blocks = quant.astype(jnp.float32).reshape(rows, cols // block, block)
    return (blocks * scale.astype(jnp.float32)[..., None]).reshape(rows, cols)


def join_pair(mine, other, upper):
    low_first = jnp.concatenate([mine, other], axis=1)
    high_first = jnp.concatenate([other, mine], axis=1)
    return jnp.where(upper, high_first, low_first)


def on_device(tokens, norm_gain, w_query, w_key, w_value, w_output):
    rows = tokens.shape[1]
    whole = lax.all_gather(tokens[0], "tp", axis=1, tiled=True)
    xf = whole.astype(jnp.float32)
    normed = (
        xf * lax.rsqrt(jnp.mean(xf * xf, axis=-1, keepdims=True) + 1e-05) * norm_gain[0]
    ).astype(jnp.bfloat16)
    local_heads = w_query.shape[2] // HD
    queries = rotate(
        jnp.dot(normed, w_query[0], preferred_element_type=jnp.float32), local_heads, HD
    ).astype(jnp.bfloat16)
    key_head = jnp.dot(normed, w_key[0], preferred_element_type=jnp.float32).astype(jnp.bfloat16)
    value_head = jnp.dot(normed, w_value[0], preferred_element_type=jnp.float32).astype(
        jnp.bfloat16
    )
    span = lax.axis_size("tp") // KVH
    position = lax.axis_index("tp")
    for level in range(span.bit_length() - 1):
        other_key, other_value = from_partner((key_head, value_head), "tp", level)
        upper = position // 2**level % 2 == 1
        key_head = join_pair(key_head, other_key, upper)
        value_head = join_pair(value_head, other_value, upper)
    keys = rotate(key_head.astype(jnp.float32), 1, HD)[:, 0, :].astype(jnp.bfloat16)
    scores = jnp.einsum(
        "thd,sd->hts", queries, keys, preferred_element_type=jnp.float32
    ) / math.sqrt(HD)
    causal = jnp.arange(rows)[:, None] >= jnp.arange(rows)[None, :]
    scores = jnp.where(causal[None], scores, jnp.float32(-1e30))
    peak = jnp.max(scores, axis=-1, keepdims=True)
    weights = jnp.exp(scores - peak)
    probs = (weights / jnp.sum(weights, axis=-1, keepdims=True)).astype(jnp.bfloat16)
    context = jnp.einsum("hts,sd->thd", probs, value_head, preferred_element_type=jnp.float32)
    context = context.astype(jnp.bfloat16).reshape(rows, local_heads * HD)
    partial_value = jnp.dot(context, w_output[0], preferred_element_type=jnp.float32)
    quant, scale = quantize(partial_value, BLOCK)
    attended = lax.psum_scatter(
        dequantize(quant, scale, BLOCK).astype(jnp.bfloat16), "tp", scatter_dimension=1, tiled=True
    ).astype(jnp.float32)
    merged = tokens[0].astype(jnp.float32) + attended
    out_quant, out_scale = quantize(merged, BLOCK)
    moved, moved_scale = from_behind((out_quant, out_scale), "pp", 1)
    return dequantize(moved, moved_scale, BLOCK)[None]


def solution(mesh):
    return jax.shard_map(
        on_device,
        mesh=mesh,
        in_specs=(
            P("pp", None, "tp"),
            P("pp", None),
            P("pp", None, "tp"),
            P("pp", None, "tp"),
            P("pp", None, "tp"),
            P("pp", "tp", None),
        ),
        out_specs=P("pp", None, "tp"),
        check_vma=False,
    )
```

profile of v0, /device:TPU:128, one launch (start us, length us, event | category | flops | bytes accessed | tf_op | source)
XLA Modules:
  0.0 255.7 jit_solution(7913777723528494557)
XLA Ops:
  6.5 0.0 copy-start
  6.5 0.0 all-gather.3.cloned.1.call-start
  6.5 0.7 all-gather.3.cloned.1.call-update
  7.3 0.0 reduce-scatter.2.cloned.1.call-start
  7.3 6.5 %copy.19 = bf16[256,8192]{1,0:T(8,128)(2,1)} copy(bf16[256,8192]{0,1:T(8,128)(2,1)} %bitcast.85) | data formatting | bytes 8388608 | tf_op jit(solution)/shard_map/dot_general | solution.py:73
  13.8 0.0 copy-start.6
  13.8 6.4 %copy.21 = bf16[8192,256]{1,0:T(8,128)(2,1)} copy(bf16[8192,256]{0,1:T(8,128)(2,1)} %bitcast.86) | data formatting | bytes 8388608 | tf_op jit(solution)/shard_map/dot_general | solution.py:97
  20.2 0.1 iota_compare_fusion
  20.3 0.5 fusion.32
  20.9 73.8 %all-gather.3.cloned.1.call-done = bf16[1,512,8192]{2,1,0:T(8,128)(2,1)} async-done(((bf16[1,512,512]{2,1,0:T(8,128)(2,1)}), bf16[1,512,8192]{2,1,0:T(8,128)(2,1)}) %all-gather.3.cloned.1.call-update) | async-done | bytes 8388624 | tf_op jit(solution)/shard_map/all_gather | solution.py:66
  94.7 0.0 copy-start.2
  94.7 5.3 %fusion.1 = f32[512]{0:T(512)S(1)} fusion(bf16[1,512,8192]{2,1,0:T(8,128)(2,1)} %all-gather.3.cloned.1.call-done), kind=kLoop, calls=%fused_computation.3 | loop fusion | flops 12582400 | bytes 8390656 | tf_op jit(solution)/shard_map/reduce_sum | solution.py:69
  99.9 0.0 copy-start.5
  99.9 0.0 copy-done
  100.0 0.0 copy-done.6
  100.0 0.5 copy-done.2
  100.4 2.8 %convolution_convert_fusion.2 = bf16[512,32]{0,1:T(8,128)(2,1)S(1)} fusion(bf16[1,8192,32]{1,2,0:T(8,128)(2,1)S(1)} %copy-done, bf16[1,512,8192]{2,1,0:T(8,128)(2,1)S(1)} %copy-done.2, f32[8192]{0:T(1024)S(1)} %bitcast.93, f32[512]{0:T(512)S(1)} %add_rsqrt_fusion), kind=kOutput, calls=%fused_computation.17 | convolution fusion | flops 285229056 | bytes 8980480 | tf_op jit(solution)/shard_map/dot_general | solution.py:76
  103.2 0.0 copy-start.4
  103.2 1.2 collective-permute-start
  104.4 0.0 copy-done.5
  104.4 2.7 %convolution_convert_fusion.1 = bf16[512,32]{0,1:T(8,128)(2,1)S(1)} fusion(bf16[1,8192,32]{1,2,0:T(8,128)(2,1)S(1)} %copy-done.5, bf16[1,512,8192]{2,1,0:T(8,128)(2,1)S(1)} %copy-done.2, f32[8192]{0:T(1024)S(1)} %bitcast.94, f32[512]{0:T(512)S(1)} %add_rsqrt_fusion), kind=kOutput, calls=%fused_computation.16 | convolution fusion | flops 285229056 | bytes 8980480 | tf_op jit(solution)/shard_map/dot_general | solution.py:75
  107.2 0.9 collective-permute-start.2
  108.1 0.0 copy-done.4
  108.1 2.6 %fusion.4 = f32[512,2,128]{0,2,1:T(8,128)S(1)} fusion(bf16[2,128,8192]{2,1,0:T(8,128)(2,1)S(1)} %bitcast.87, bf16[1,512,8192]{2,1,0:T(8,128)(2,1)S(1)} %copy-done.2, f32[8192]{0:T(1024)S(1)} %bitcast.95, f32[512]{0:T(512)S(1)} %add_rsqrt_fusion), kind=kOutput, calls=%fused_computation.9 | convolution fusion | flops 2164260864 | bytes 13142016 | tf_op jit(solution)/shard_map/dot_general | solution.py:73
  110.6 0.1 subtract_convert_fusion
  110.7 0.4 collective-permute-done.2
  111.1 2.9 %collective-permute-start.3 = (bf16[512,64]{0,1:T(8,128)(2,1)S(1)}, bf16[512,64]{0,1:T(8,128)(2,1)S(1)}, u32[]{:S(2)}, u32[]{:S(2)}) collective-permute-start(bf16[512,64]{0,1:T(8,128)(2,1)S(1)} %maximum_select_fusion.3), channel_id=1, source_target_pairs={{0,32},{32,0},{16,48},{48,16},{64,96},{96,64},{80,112},{112,80},{1... | collective-permute-start | bytes 196616 | tf_op jit(solution)/shard_map/ppermute | solution.py:20
  114.1 0.0 collective-permute-done
  114.1 0.9 collective-permute-start.1
  115.1 2.1 collective-permute-done.3
  117.2 0.6 subtract_convert_fusion.1
  117.8 0.9 fusion.59
  118.7 1.3 collective-permute-done.1
  120.0 1.2 convolution_convert_fusion
  121.2 5.0 %abs_reduce_fusion = (f32[512,64]{0,1:T(8,128)S(1)}, f32[512,64,128]{0,2,1:T(8,128)S(1)}) fusion(bf16[512,256,1]{0,1,2:T(8,128)(2,1)S(1)} %bitcast.90, bf16[64,128,256]{2,1,0:T(8,128)(2,1)} %bitcast.84), kind=kOutput, calls=%fused_computation.8 | convolution fusion | flops 2155839488 | bytes 21364736 | tf_op jit(solution)/shard_map/dot_general | solution.py:97
  126.3 4.8 %multiply_convert_fusion = bf16[512,64,128]{0,2,1:T(8,128)(2,1)} fusion(f32[512,64]{0,1:T(8,128)S(1)} %fusion.38, f32[512,64,128]{0,2,1:T(8,128)S(1)} %get-tuple-element.12), kind=kLoop, calls=%fused_computation.6 | loop fusion | flops 20971520 | bytes 25296896 | tf_op jit(solution)/shard_map/convert_element_type | solution.py:100
  131.0 12.0 %copy.13 = bf16[512,8192]{1,0:T(8,128)(2,1)} copy(bf16[512,8192]{0,1:T(8,128)(2,1)} %bitcast.83) | data formatting | bytes 16777216 | tf_op jit(solution)/shard_map/convert_element_type | solution.py:100
  143.0 0.0 copy-start.3
  143.0 0.0 reduce-scatter.2.cloned.1.call-update
  143.0 0.0 copy-start.1
  143.0 88.7 %reduce-scatter.2.cloned.1.call-done = bf16[512,512]{1,0:T(8,128)(2,1)} async-done(((bf16[512,8192]{1,0:T(8,128)(2,1)}), bf16[512,512]{1,0:T(8,128)(2,1)}) %reduce-scatter.2.cloned.1.call-update) | async-done | bytes 524304 | tf_op jit(solution)/shard_map/reduce_scatter | solution.py:99
  231.7 0.0 copy-done.3
  231.7 1.2 fusion.12
  232.9 0.4 abs.11
  233.3 0.6 reduce_max.29
  234.0 0.6 div.62
  234.6 1.3 fusion.8
  235.9 0.0 collective-permute-start.4
  235.9 0.8 collective-permute-start.5
  236.7 10.4 %collective-permute-done.5 = bf16[512,4]{1,0:T(8,128)(2,1)S(1)} collective-permute-done((bf16[512,4]{1,0:T(8,128)(2,1)S(1)}, bf16[512,4]{1,0:T(8,128)(2,1)S(1)}, u32[]{:S(2)}, u32[]{:S(2)}) %collective-permute-start.5) | collective-permute-done | bytes 4128 | tf_op jit(solution)/shard_map/ppermute | solution.py:26
  247.1 0.0 collective-permute-done.4
  247.1 0.6 mul.206
  247.7 1.1 fusion.7
  248.9 0.0 copy-done.1
  (7 shorter events, 0.1 us)
Async XLA Ops:
  6.5 93.4 %copy-start = (bf16[1,8192,32]{1,2,0:T(8,128)(2,1)S(1)}, bf16[1,8192,32]{1,2,0:T(8,128)(2,1)}, u32[]{:S(2)}) copy-start(bf16[1,8192,32]{1,2,0:T(8,128)(2,1)} %param.10) | copy-start | bytes 1572868
  6.5 88.1 %all-gather.3.cloned.1.call-start = ((), (), s32[]{:S(2)}) async-start(), calls=%async_computation.2 | async-start | bytes 8912896 | tf_op jit(solution)/shard_map/all_gather | solution.py:66
  7.3 224.5 %reduce-scatter.2.cloned.1.call-start = ((), (), s32[]{:S(2)}) async-start(), calls=%async_computation.1 | async-start | bytes 8912896 | tf_op jit(solution)/shard_map/reduce_scatter | solution.py:99
  13.8 86.2 %copy-start.6 = (f32[1,8192]{1,0:T(1,128)S(1)}, f32[1,8192]{1,0:T(1,128)}, u32[]{:S(2)}) copy-start(f32[1,8192]{1,0:T(1,128)} %param.7) | copy-start | bytes 98308
  94.7 5.8 %copy-start.2 = (bf16[1,512,8192]{2,1,0:T(8,128)(2,1)S(1)}, bf16[1,512,8192]{2,1,0:T(8,128)(2,1)}, u32[]{:S(2)}) copy-start(bf16[1,512,8192]{2,1,0:T(8,128)(2,1)} %all-gather.3.cloned.1.call-done) | copy-start | bytes 25165828
  99.9 4.5 %copy-start.5 = (bf16[1,8192,32]{1,2,0:T(8,128)(2,1)S(1)}, bf16[1,8192,32]{1,2,0:T(8,128)(2,1)}, u32[]{:S(2)}) copy-start(bf16[1,8192,32]{1,2,0:T(8,128)(2,1)} %param.9) | copy-start | bytes 1572868
  103.2 4.8 %copy-start.4 = (bf16[256,8192]{1,0:T(8,128)(2,1)S(1)}, bf16[256,8192]{1,0:T(8,128)(2,1)}, u32[]{:S(2)}) copy-start(bf16[256,8192]{1,0:T(8,128)(2,1)} %copy.19) | copy-start | bytes 12582916
  103.2 10.9 %collective-permute-start = (bf16[512,32]{0,1:T(8,128)(2,1)S(1)}, bf16[512,32]{0,1:T(8,128)(2,1)S(1)}, u32[]{:S(2)}, u32[]{:S(2)}) collective-permute-start(bf16[512,32]{0,1:T(8,128)(2,1)S(1)} %convolution_convert_fusion.2), channel_id=1, source_target_pairs={{0,16},{16,0},{32,48},{48,32},{64,80},{80,64},{96,112},{112,96},{1... | collective-permute-start | bytes 98312 | tf_op jit(solution)/shard_map/ppermute | solution.py:20
  107.2 3.9 %collective-permute-start.2 = (bf16[512,32]{0,1:T(8,128)(2,1)S(1)}, bf16[512,32]{0,1:T(8,128)(2,1)S(1)}, u32[]{:S(2)}, u32[]{:S(2)}) collective-permute-start(bf16[512,32]{0,1:T(8,128)(2,1)S(1)} %convolution_convert_fusion.1), channel_id=1, source_target_pairs={{0,16},{16,0},{32,48},{48,32},{64,80},{80,64},{96,112},{112,96},{1... | collective-permute-start | bytes 98312 | tf_op jit(solution)/shard_map/ppermute | solution.py:20
  111.1 6.0 %collective-permute-start.3 = (bf16[512,64]{0,1:T(8,128)(2,1)S(1)}, bf16[512,64]{0,1:T(8,128)(2,1)S(1)}, u32[]{:S(2)}, u32[]{:S(2)}) collective-permute-start(bf16[512,64]{0,1:T(8,128)(2,1)S(1)} %maximum_select_fusion.3), channel_id=1, source_target_pairs={{0,32},{32,0},{16,48},{48,16},{64,96},{96,64},{80,112},{112,80},{1... | collective-permute-start | bytes 196616 | tf_op jit(solution)/shard_map/ppermute | solution.py:20
  114.1 5.9 %collective-permute-start.1 = (bf16[512,64]{0,1:T(8,128)(2,1)S(1)}, bf16[512,64]{0,1:T(8,128)(2,1)S(1)}, u32[]{:S(2)}, u32[]{:S(2)}) collective-permute-start(bf16[512,64]{0,1:T(8,128)(2,1)S(1)} %maximum_select_fusion.2), channel_id=1, source_target_pairs={{0,32},{32,0},{16,48},{48,16},{64,96},{96,64},{80,112},{112,80},{1... | collective-permute-start | bytes 196616 | tf_op jit(solution)/shard_map/ppermute | solution.py:20
  143.0 88.7 %copy-start.3 = (bf16[1,512,512]{2,1,0:T(8,128)(2,1)S(1)}, bf16[1,512,512]{2,1,0:T(8,128)(2,1)}, u32[]{:S(2)}) copy-start(bf16[1,512,512]{2,1,0:T(8,128)(2,1)} %param.6) | copy-start | bytes 1572868
  143.0 105.8 %copy-start.1 = (bf16[1,8192,32]{1,2,0:T(8,128)(2,1)S(1)}, bf16[1,8192,32]{1,2,0:T(8,128)(2,1)}, u32[]{:S(2)}) copy-start(bf16[1,8192,32]{1,2,0:T(8,128)(2,1)} %param.10) | copy-start | bytes 1572868
  235.9 11.2 %collective-permute-start.4 = (bf16[512,512]{1,0:T(8,128)(2,1)S(1)}, bf16[512,512]{1,0:T(8,128)(2,1)S(1)}, u32[]{:S(2)}, u32[]{:S(2)}) collective-permute-start(bf16[512,512]{1,0:T(8,128)(2,1)S(1)} %fusion.8), channel_id=1, source_target_pairs={{15,0},{0,1},{1,2},{2,3},{3,4},{4,5},{5,6},{6,7},{7,8},{8,9},{9,10... | collective-permute-start | bytes 1572872 | tf_op jit(solution)/shard_map/ppermute | solution.py:26
  235.9 11.2 %collective-permute-start.5 = (bf16[512,4]{1,0:T(8,128)(2,1)S(1)}, bf16[512,4]{1,0:T(8,128)(2,1)S(1)}, u32[]{:S(2)}, u32[]{:S(2)}) collective-permute-start(bf16[512,4]{1,0:T(8,128)(2,1)S(1)} %add_convert_fusion), channel_id=1, source_target_pairs={{15,0},{0,1},{1,2},{2,3},{3,4},{4,5},{5,6},{6,7},{7,8},{8,9},{9,10... | collective-permute-start | bytes 12296 | tf_op jit(solution)/shard_map/ppermute | solution.py:26
Sparse Core Ops, SparseCore 0:
  9.8 84.8 all-gather.2
  143.1 88.5 reduce-scatter.1
where the time goes:
time: 258 us; the launch traced here: 256 us
  waiting for transfers between devices  177 us (69%)
  local copies, waits for them, and re-layouts  26.9 us (10%)
  other arithmetic  15.7 us (6%)
  matrix products  15.3 us (6%)
  between operations  13.6 us (5%)
  starting transfers between devices  6.85 us (3%)
    reduce_scatter x1, waiting for transfers between devices, on_device(): lax.psum_scatter(dequantize(quant, scale, BLOCK).astype(jnp.bfloat16), 't...  88.7 us
    all_gather x1, waiting for transfers between devices, on_device(): whole = lax.all_gather(tokens[0], 'tp', axis=1, tiled=True)  73.8 us
    convert_element_type x1, local copies, waits for them, and re-layouts, on_device(): dequantize(quant, scale, BLOCK).astype(jnp.bfloat16)  12 us
    ppermute x2, waiting for transfers between devices, from_behind(): return lax.ppermute(block, axis, route)  10.4 us
    dot_general x1, local copies, waits for them, and re-layouts, on_device(): jnp.dot(normed, w_query[0], preferred_element_type=jnp.float32)  6.45 us
    dot_general x1, local copies, waits for them, and re-layouts, on_device(): jnp.dot(context, w_output[0], preferred_element_type=jnp.float32)  6.41 us
    ppermute x4, starting transfers between devices, from_partner(): return lax.ppermute(block, axis, route)  5.98 us
    reduce_sum x1, other arithmetic, on_device(): jnp.mean(xf * xf, axis=-1, keepdims=True) + 1e-05  5.25 us
  transfers between devices with their start and end apart: 8, of which 6 were waited for; matrix products, arithmetic and copies ran while one was open for 8% of the time, Pallas kernels for 0%

commit v1 on v0

v1 whole, which is shorter than its diff:
```python
import functools
import math

import jax
import jax.numpy as jnp
from jax import lax
from jax.experimental import pallas as pl
from jax.experimental.pallas import tpu as pltpu
from jax.sharding import Mesh
from jax.sharding import PartitionSpec as P

KVH = 4
HD = 128
SIDE = 4
EPS = 1e-05


def shift(block, axis, step):
    count = lax.axis_size(axis)
    return lax.ppermute(block, axis, [(i, (i + step) % count) for i in range(count)])


def dot(a, b, dims=((1,), (0,))):
    return lax.dot_general(a, b, (dims, ((), ())), preferred_element_type=jnp.float32)


def accumulate_kernel(pieces, first, last, width, table, *refs):
    refs = list(refs)
    take = lambda n: [refs.pop(0) for _ in range(n)]
    x_refs = take(pieces)
    gain, wq, wk, wv = take(4)
    prior = [] if first else take(3)
    tables = take(2) if last else []
    outs = take(2) if last else []
    sums = take(3)
    step = pl.program_id(0)

    @pl.when(step == 0)
    def _():
        for i, held in enumerate(sums):
            held[...] = jnp.zeros_like(held) if first else prior[i][...]

    q_sum, kv_sum, square_sum = sums
    x = jnp.concatenate([ref[...] for ref in x_refs], axis=0).astype(jnp.float32)
    squares = x * x
    total = squares[:, :128]
    for i in range(1, x.shape[1] // 128):
        total = total + squares[:, i * 128 : (i + 1) * 128]
    square_sum[...] += total
    scaled = (x * gain[...]).astype(jnp.bfloat16)
    q_sum[...] += dot(scaled, wq[...])
    kv_weights = jnp.concatenate([wk[...], wv[...]], axis=0)
    kv_sum[...] += dot(scaled, kv_weights, ((1,), (1,)))

    if last:
        cosine, sine = tables
        q_out, kv_out = outs

        @pl.when(step == pl.num_programs(0) - 1)
        def _():
            mean = jnp.sum(square_sum[...], axis=1, keepdims=True) / width
            row = lax.rsqrt(mean + EPS)
            kv_out[...] = (kv_sum[...] * row).astype(jnp.bfloat16)
            for h in range(q_sum.shape[1] // HD):
                one = q_sum[:, h * HD : (h + 1) * HD] * row
                turned = one * cosine[...] + pltpu.roll(one, HD // 2, 1) * sine[...]
                q_out[:, h * HD : (h + 1) * HD] = turned.astype(jnp.bfloat16)


def accumulate(pieces, table, gain, wq, wk, wv, prior=None, tables=None):
    rows = sum(p.shape[0] for p in pieces)
    depth = pieces[0].shape[1] // SIDE
    heads = wq.shape[1]
    narrow = 2 * wk.shape[0]
    first, last = prior is None, tables is not None
    fixed = lambda shape: pl.BlockSpec(shape, lambda k, t: (0, 0))
    in_specs = [pl.BlockSpec((p.shape[0], depth), lambda k, t: (0, k)) for p in pieces]
    in_specs += [
        pl.BlockSpec((1, depth), lambda k, t: (0, t[k])),
        pl.BlockSpec((depth, heads), lambda k, t: (t[k], 0)),
        pl.BlockSpec((wk.shape[0], depth), lambda k, t: (0, t[k])),
        pl.BlockSpec((wv.shape[0], depth), lambda k, t: (0, t[k])),
    ]
    args = list(pieces) + [gain, wq, wk, wv]
    sums = [(rows, heads), (rows, narrow), (rows, 128)]
    if not first:
        in_specs += [fixed(s) for s in sums]
        args += list(prior)
    if last:
        in_specs += [fixed(t.shape) for t in tables]
        args += list(tables)
        outs = [(s, jnp.bfloat16) for s in sums[:2]]
        scratch = [pltpu.VMEM(s, jnp.float32) for s in sums]
    else:
        outs = [(s, jnp.float32) for s in sums]
        scratch = []
    return pl.pallas_call(
        functools.partial(accumulate_kernel, len(pieces), first, last, gain.shape[1]),
        out_shape=[jax.ShapeDtypeStruct(s, d) for s, d in outs],
        grid_spec=pltpu.PrefetchScalarGridSpec(
            num_scalar_prefetch=1,
            grid=(SIDE,),
            in_specs=in_specs,
            out_specs=[fixed(s) for s, _ in outs],
            scratch_shapes=scratch,
        ),
        cost_estimate=pl.CostEstimate(
            flops=2 * rows * depth * SIDE * (heads + narrow),
            bytes_accessed=2 * SIDE * depth * (rows + heads + narrow) + 8 * rows * 448,
            transcendentals=0,
        ),
    )(table, *args)


def attend_kernel(start, place, q, own, right, two, left, cosine, sine, out):
    rows = q.shape[0]
    span = own.shape[0]
    part = own.shape[1] // 2
    line = lax.broadcasted_iota(jnp.int32, (2 * part, 2 * HD), 0)
    column = lax.broadcasted_iota(jnp.int32, (2 * part, 2 * HD), 1)
    home = jnp.where(line < part, line, line - part + HD)
    whole = jnp.zeros((span, 2 * HD), jnp.float32)
    for d, piece in enumerate((own, right, two, left)):
        at = lax.rem(place[0] + d, SIDE) * part
        whole += dot(piece[...], (column == home + at).astype(jnp.bfloat16))
    raw = whole[:, :HD]
    keys = (raw * cosine[...] + pltpu.roll(raw, HD // 2, 1) * sine[...]).astype(jnp.bfloat16)
    values = whole[:, HD:].astype(jnp.bfloat16)
    seen = (
        lax.broadcasted_iota(jnp.int32, (rows, span), 0) + start
        >= lax.broadcasted_iota(jnp.int32, (rows, span), 1)
    )
    for h in range(q.shape[1] // HD):
        scores = dot(q[:, h * HD : (h + 1) * HD], keys, ((1,), (1,))) * (1.0 / math.sqrt(HD))
        scores = jnp.where(seen, scores, jnp.float32(-1e30))
        weights = jnp.exp(scores - jnp.max(scores, axis=1, keepdims=True))
        probs = weights / jnp.sum(weights, axis=1, keepdims=True)
        out[:, h * HD : (h + 1) * HD] = dot(probs.astype(jnp.bfloat16), values).astype(
            jnp.bfloat16
        )


def attend(start, place, q, parts, cosine, sine):
    rows = q.shape[0]
    span = start + rows
    fixed = lambda shape: pl.BlockSpec(shape, lambda i, t: (0, 0))
    part = parts[0].shape[1]
    return pl.pallas_call(
        functools.partial(attend_kernel, start),
        out_shape=jax.ShapeDtypeStruct(q.shape, jnp.bfloat16),
        grid_spec=pltpu.PrefetchScalarGridSpec(
            num_scalar_prefetch=1,
            grid=(1,),
            in_specs=[fixed(q.shape)] + [fixed((span, part))] * 4 + [fixed((span, HD))] * 2,
            out_specs=fixed(q.shape),
        ),
        cost_estimate=pl.CostEstimate(
            flops=8 * rows * span * HD, bytes_accessed=4 * rows * 256, transcendentals=2 * rows * span
        ),
    )(place, q, *parts, cosine, sine)


def project_kernel(n_top, n_low, n_both, split, table, *refs):
    refs = list(refs)
    take = lambda n: [refs.pop(0) for _ in range(n)]
    context, weights = take(2)
    tops, lows, boths = take(n_top), take(n_low), take(n_both)
    half = context.shape[0] // 2
    value = dot(context[...], weights[...])
    top, low = value[:half], value[half:]
    for ref in tops:
        top = top + ref[...].astype(jnp.float32)
    for ref in lows:
        low = low + ref[...].astype(jnp.float32)
    for ref in boths:
        top = top + ref[:half].astype(jnp.float32)
        low = low + ref[half:].astype(jnp.float32)
    if split:
        refs[0][...] = top.astype(refs[0].dtype)
        refs[1][...] = low.astype(refs[1].dtype)
    else:
        refs[0][:half] = top.astype(refs[0].dtype)
        refs[0][half:] = low.astype(refs[0].dtype)


def project(context, weights, table, tops=(), lows=(), boths=(), split=False, kind=jnp.bfloat16):
    rows, depth = context.shape
    width = weights.shape[1] // SIDE**2
    half = rows // 2
    block = lambda r: pl.BlockSpec((r, width), lambda k, t: (0, k))
    shapes = [half, half] if split else [rows]
    result = pl.pallas_call(
        functools.partial(project_kernel, len(tops), len(lows), len(boths), split),
        out_shape=[jax.ShapeDtypeStruct((r, width * SIDE), kind) for r in shapes],
        grid_spec=pltpu.PrefetchScalarGridSpec(
            num_scalar_prefetch=1,
            grid=(SIDE,),
            in_specs=[
                pl.BlockSpec((rows, depth), lambda k, t: (0, 0)),
                pl.BlockSpec((depth, width), lambda k, t: (0, t[k])),
            ]
            + [block(half)] * (len(tops) + len(lows))
            + [block(rows)] * len(boths),
            out_specs=[block(r) for r in shapes],
        ),
        cost_estimate=pl.CostEstimate(
            flops=2 * rows * depth * width * SIDE,
            bytes_accessed=2 * SIDE * width * (depth + rows),
            transcendentals=0,
        ),
    )(table, context, weights, *tops, *lows, *boths)
    return result if split else result[0]


def ring_gather(block, axis):
    half = block.shape[0] // 2
    behind = shift(block, axis, 1)
    ahead = shift(block, axis, -1)
    far = (shift(behind[:half], axis, 1), shift(ahead[half:], axis, -1))
    return behind, ahead, far


def on_device(tokens, norm_gain, w_query, w_key, w_value, w_output):
    own = tokens[0]
    rows = own.shape[0]
    half = rows // 2
    y, x = lax.axis_index("ty"), lax.axis_index("tx")
    wq, wk, wv, wo = w_query[0], w_key[0].T, w_value[0].T, w_output[0]

    freq = jnp.exp(jnp.arange(HD // 2, dtype=jnp.float32) * (-2.0 * math.log(500000.0) / HD))
    angle = jnp.arange(rows, dtype=jnp.float32)[:, None] * freq[None, :]
    cosine = jnp.concatenate([jnp.cos(angle)] * 2, axis=1)
    sine = jnp.concatenate([-jnp.sin(angle), jnp.sin(angle)], axis=1)

    offsets = jnp.array((0, -1, 1, 2), jnp.int32)
    wrap = lambda v: (v + SIDE) % SIDE
    along = (
        lambda far: wrap(y + far) * SIDE + wrap(x + offsets),
        lambda far: wrap(y + offsets) * SIDE + wrap(x + far),
    )
    first_axis, second_axis = ("tx", "ty"), ("ty", "tx")

    blocks = [own[:half], own[half:]]
    near = [ring_gather(blocks[i], first_axis[i]) for i in range(2)]
    lines = [
        jnp.concatenate([blocks[i], near[i][0], near[i][1], jnp.concatenate(near[i][2])], axis=1)
        for i in range(2)
    ]
    distant = [ring_gather(lines[i], second_axis[i]) for i in range(2)]
    common = (norm_gain, wq, wk, wv)
    queries, narrow = [], []
    for i in range(2):
        sums = accumulate([lines[i]], along[i](0), *common)
        sums = accumulate([distant[i][0]], along[i](-1), *common, prior=sums)
        sums = accumulate([distant[i][1]], along[i](1), *common, prior=sums)
        cut = slice(i * half, (i + 1) * half)
        q, kv = accumulate(
            distant[i][2], along[i](2), *common, prior=sums, tables=(cosine[cut], sine[cut])
        )
        queries.append(q)
        narrow.append(kv)
    kv = jnp.concatenate(narrow)
    parts = (kv, shift(kv, "tx", -1), shift(kv, "tx", 2), shift(kv, "tx", 1))
    place = x.astype(jnp.int32)[None]
    merged = []
    contexts = [attend(i * half, place, queries[i], parts, cosine, sine) for i in range(2)]

    strips = []
    for i in range(2):
        axis = second_axis[i]
        run = functools.partial(project, contexts[i], wo)
        far_top, far_low = run(along[i](2), split=True)
        from_behind = shift(far_top, axis, 1)
        from_ahead = shift(far_low, axis, -1)
        onward = shift(run(along[i](1), tops=[from_behind]), axis, 1)
        back = shift(run(along[i](-1), lows=[from_ahead]), axis, -1)
        strips.append(run(along[i](0), boths=[onward, back], kind=jnp.float32))
    for i in range(2):
        axis = first_axis[i]
        width = strips[i].shape[1] // SIDE
        mine, behind, ahead, far = (strips[i][:, k * width : (k + 1) * width] for k in range(SIDE))
        cut = half // 2
        far = far.astype(jnp.bfloat16)
        from_behind = shift(far[:cut], axis, 1).astype(jnp.float32)
        from_ahead = shift(far[cut:], axis, -1).astype(jnp.float32)
        ahead = jnp.concatenate([ahead[:cut] + from_behind, ahead[cut:]]).astype(jnp.bfloat16)
        behind = jnp.concatenate([behind[:cut], behind[cut:] + from_ahead]).astype(jnp.bfloat16)
        onward, back = shift(ahead, axis, 1), shift(behind, axis, -1)
        merged.append(
            blocks[i].astype(jnp.float32)
            + (mine + onward.astype(jnp.float32) + back.astype(jnp.float32))
        )
    result = jnp.concatenate(merged).astype(jnp.bfloat16)
    return shift(result, "pp", 1).astype(jnp.float32)[None]


def solution(mesh):
    shape = mesh.devices.shape
    grid = Mesh(mesh.devices.reshape(SIDE, shape[0] // SIDE, shape[1]), ("ty", "tx", "pp"))
    tp = ("ty", "tx")
    return jax.shard_map(
        on_device,
        mesh=grid,
        in_specs=(
            P("pp", None, tp),
            P("pp", None),
            P("pp", None, tp),
            P("pp", None, tp),
            P("pp", None, tp),
            P("pp", tp, None),
        ),
        out_specs=P("pp", None, tp),
        check_vma=False,
    )
```

time: 258 us -> 220 us (0.85)
  waiting for transfers between devices: 177 us -> 52.6 us
  Pallas kernels: 0 us -> 84.6 us
  starting transfers between devices: 6.85 us -> 53.4 us
  matrix products: 15.3 us -> 0 us
  between operations: 13.6 us -> 0.36 us
  local copies, waits for them, and re-layouts: 26.9 us -> 16.9 us
  other arithmetic: 15.7 us -> 10.4 us
    reduce_scatter x1 -> x0, waiting for transfers between devices: 88.7 us -> none  [on_device(): lax.psum_scatter(dequantize(quant, scale, BLOCK).astype(jnp.bfloat16), 't...]
    pallas_call x0 -> x18, Pallas kernels: none -> 84.6 us  [the longest x8 39.5 us: accumulate(): pl.pallas_call(functools.partial(accumulate_kernel, len(pieces), first, l...]
    all_gather x1 -> x0, waiting for transfers between devices: 73.8 us -> none  [on_device(): whole = lax.all_gather(tokens[0], 'tp', axis=1, tiled=True)]
    ppermute x6 -> x36, starting transfers between devices: 6.81 us -> 53.4 us  [shift(): lax.ppermute(block, axis, [(i, (i + step) % count) for i in range(count)])]
    ppermute x6 -> x36, waiting for transfers between devices: 14.2 us -> 52.6 us  [shift(): lax.ppermute(block, axis, [(i, (i + step) % count) for i in range(count)])]
    dot_general x5 -> x0, matrix products: 14.3 us -> none  [the longest x1 5.04 us: on_device(): jnp.dot(context, w_output[0], preferred_element_type=jnp.float32)]
    dot_general x2 -> x0, local copies, waits for them, and re-layouts: 12.9 us -> none  [the longest x1 6.45 us: on_device(): jnp.dot(normed, w_query[0], preferred_element_type=jnp.float32)]
    convert_element_type x1 -> x0, local copies, waits for them, and re-layouts: 12 us -> none  [on_device(): dequantize(quant, scale, BLOCK).astype(jnp.bfloat16)]
  transfers between devices with their start and end apart: 8 -> 36, of which waited for: 6 -> 13; matrix products, arithmetic and copies ran while one was open for 8% -> 8% of each run, Pallas kernels for 0% -> 33%
where the time goes in v1:
time: 220 us; the launch traced here: 218 us
  Pallas kernels  84.6 us (38%)
  starting transfers between devices  53.4 us (24%)
  waiting for transfers between devices  52.6 us (24%)
  local copies, waits for them, and re-layouts  16.9 us (8%)
  other arithmetic  10.4 us (5%)
    ppermute x36, starting transfers between devices, shift(): lax.ppermute(block, axis, [(i, (i + step) % count) for i in range(count)])  53.4 us
    ppermute x36, waiting for transfers between devices, shift(): lax.ppermute(block, axis, [(i, (i + step) % count) for i in range(count)])  52.6 us
    pallas_call x8, Pallas kernels, accumulate(): pl.pallas_call(functools.partial(accumulate_kernel, len(pieces), first, l...  39.5 us
    pallas_call x8, Pallas kernels, project(): pl.pallas_call(functools.partial(project_kernel, len(tops), len(lows), le...  38.2 us
    unnamed x41, local copies, waits for them, and re-layouts  7.49 us
    pallas_call x2, Pallas kernels, attend(): pl.pallas_call(functools.partial(attend_kernel, start), out_shape=jax.Sha...  6.99 us
    slice x8, local copies, waits for them, and re-layouts, ring_gather(): far = (shift(behind[:half], axis, 1), shift(ahead[half:], axis, -1))  6.8 us
  transfers between devices with their start and end apart: 36, of which 13 were waited for; matrix products, arithmetic and copies ran while one was open for 8% of the time, Pallas kernels for 33%

profile of v1, /device:TPU:128, one launch (start us, length us, event | category | flops | bytes accessed | tf_op | source)
XLA Modules:
  0.0 218.2 jit_solution(9618714699182341368)
XLA Ops:
  0.0 1.1 slice_bitcast_fusion.1
  1.1 2.8 %collective-permute-start.1 = (bf16[256,512]{1,0:T(8,128)(2,1)S(1)}, bf16[256,512]{1,0:T(8,128)(2,1)S(1)}, u32[]{:S(2)}, u32[]{:S(2)}) collective-permute-start(bf16[256,512]{1,0:T(8,128)(2,1)S(1)} %get-tuple-element.77), channel_id=1, source_target_pairs={{0,48},{16,0},{32,16},{48,32},{1,49},{17,1},{33,17},{49,33},{2,50}... | collective-permute-start | bytes 786440 | tf_op jit(solution)/shard_map/ppermute | solution.py:20
  3.9 3.0 %collective-permute-start.9 = (bf16[256,512]{1,0:T(8,128)(2,1)S(1)}, bf16[256,512]{1,0:T(8,128)(2,1)S(1)}, u32[]{:S(2)}, u32[]{:S(2)}) collective-permute-start(bf16[256,512]{1,0:T(8,128)(2,1)S(1)} %get-tuple-element.78), channel_id=1, source_target_pairs={{0,192},{64,0},{128,64},{192,128},{1,193},{65,1},{129,65},{193,129... | collective-permute-start | bytes 786440 | tf_op jit(solution)/shard_map/ppermute | solution.py:20
  6.9 2.5 %collective-permute-done.1 = bf16[256,512]{1,0:T(8,128)(2,1)S(1)} collective-permute-done((bf16[256,512]{1,0:T(8,128)(2,1)S(1)}, bf16[256,512]{1,0:T(8,128)(2,1)S(1)}, u32[]{:S(2)}, u32[]{:S(2)}) %collective-permute-start.1) | collective-permute-done | bytes 262176 | tf_op jit(solution)/shard_map/ppermute | solution.py:20
  9.5 3.8 %collective-permute-start.3 = (bf16[128,512]{1,0:T(8,128)(2,1)S(1)}, bf16[128,512]{1,0:T(8,128)(2,1)S(1)}, u32[]{:S(2)}, u32[]{:S(2)}) collective-permute-start(bf16[128,512]{1,0:T(8,128)(2,1)S(1)} %slice.145), channel_id=1, source_target_pairs={{0,48},{16,0},{32,16},{48,32},{1,49},{17,1},{33,17},{49,33},{2,50}... | collective-permute-start | bytes 393224 | tf_op jit(solution)/shard_map/ppermute | solution.py:20
  13.4 3.1 %collective-permute-start.11 = (bf16[128,512]{1,0:T(8,128)(2,1)S(1)}, bf16[128,512]{1,0:T(8,128)(2,1)S(1)}, u32[]{:S(2)}, u32[]{:S(2)}) collective-permute-start(bf16[128,512]{1,0:T(8,128)(2,1)S(1)} %slice.153), channel_id=1, source_target_pairs={{0,192},{64,0},{128,64},{192,128},{1,193},{65,1},{129,65},{193,129... | collective-permute-start | bytes 393224 | tf_op jit(solution)/shard_map/ppermute | solution.py:20
  16.6 2.9 %collective-permute-done.2 = bf16[128,512]{1,0:T(8,128)(2,1)S(1)} collective-permute-done((bf16[128,512]{1,0:T(8,128)(2,1)S(1)}, bf16[128,512]{1,0:T(8,128)(2,1)S(1)}, u32[]{:S(2)}, u32[]{:S(2)}) %collective-permute-start.2) | collective-permute-done | bytes 131104 | tf_op jit(solution)/shard_map/ppermute | solution.py:20
  19.7 3.1 %collective-permute-start.6 = (bf16[256,2048]{1,0:T(8,128)(2,1)S(1)}, bf16[256,2048]{1,0:T(8,128)(2,1)}, u32[]{:S(2)}, u32[]{:S(2)}) collective-permute-start(bf16[256,2048]{1,0:T(8,128)(2,1)S(1)} %maximum_maximum_fusion.refs_0_), channel_id=1, source_target_pairs={{0,192},{64,0},{128,64},{192,128},{1,193},{65,1},{129,65},{193,129... | collective-permute-start | bytes 3145736 | tf_op jit(solution)/shard_map/ppermute | solution.py:20
  22.9 4.6 %collective-permute-start.14 = (bf16[256,2048]{1,0:T(8,128)(2,1)S(1)}, bf16[256,2048]{1,0:T(8,128)(2,1)}, u32[]{:S(2)}, u32[]{:S(2)}) collective-permute-start(bf16[256,2048]{1,0:T(8,128)(2,1)S(1)} %maximum_maximum_fusion.1.refs_0_), channel_id=1, source_target_pairs={{0,48},{16,0},{32,16},{48,32},{1,49},{17,1},{33,17},{49,33},{2,50}... | collective-permute-start | bytes 3145736 | tf_op jit(solution)/shard_map/ppermute | solution.py:20
  28.7 1.0 fusion.10
  29.7 13.1 %collective-permute-done.6.refs_0_ = bf16[256,2048]{1,0:T(8,128)(2,1)} collective-permute-done((bf16[256,2048]{1,0:T(8,128)(2,1)S(1)}, bf16[256,2048]{1,0:T(8,128)(2,1)}, u32[]{:S(2)}, u32[]{:S(2)}) %collective-permute-start.6) | collective-permute-done | bytes 1048608 | tf_op jit(solution)/shard_map/ppermute | solution.py:20
  42.9 1.9 slice.147
  44.8 3.8 %collective-permute-start.7 = (bf16[128,2048]{1,0:T(8,128)(2,1)}, bf16[128,2048]{1,0:T(8,128)(2,1)S(1)}, u32[]{:S(2)}, u32[]{:S(2)}) collective-permute-start(bf16[128,2048]{1,0:T(8,128)(2,1)} %slice.147), channel_id=1, source_target_pairs={{0,192},{64,0},{128,64},{192,128},{1,193},{65,1},{129,65},{193,129... | collective-permute-start | bytes 1572872 | tf_op jit(solution)/shard_map/ppermute | solution.py:20
  48.6 1.9 slice.146
  50.5 1.0 fusion.12
  51.5 1.9 slice.155
  53.4 1.8 collective-permute-start.15
  55.2 1.1 slice.154
  57.2 4.7 %shard_map.77 = (f32[256,256]{1,0:T(8,128)}, f32[256,64]{1,0:T(8,128)}, f32[256,128]{1,0:T(8,128)}) custom-call(s32[4]{0:T(128)} %get-tuple-element.90.table, bf16[256,2048]{1,0:T(8,128)(2,1)} %copy-done.3, f32[1,8192]{1,0:T(1,128)} %refs_2_.3, bf16[8192,256]{1,0:T(8,128)(2,1)} %bitcast.20, bf16[32,8192]{1,0:T(8,128)(2,1)} %bitcast.36, bf16[32,8192]{1,0:T(8,128)(2,1)} %bitcast.44), custom_call_target="tpu_custom_call" | custom-call | flops 335544320 | bytes 3276800 | tf_op jit(solution)/shard_map/pallas_call | solution.py:97
  61.9 4.7 %shard_map.73 = (f32[256,256]{1,0:T(8,128)}, f32[256,64]{1,0:T(8,128)}, f32[256,128]{1,0:T(8,128)}) custom-call(s32[4]{0:T(128)} %get-tuple-element.57.table, bf16[256,2048]{1,0:T(8,128)(2,1)} %copy-done.2, f32[1,8192]{1,0:T(1,128)} %refs_2_.3, bf16[8192,256]{1,0:T(8,128)(2,1)} %bitcast.21, bf16[32,8192]{1,0:T(8,128)(2,1)} %bitcast.37, bf16[32,8192]{1,0:T(8,128)(2,1)} %bitcast.45), custom_call_target="tpu_custom_call" | custom-call | flops 335544320 | bytes 3276800 | tf_op jit(solution)/shard_map/pallas_call | solution.py:97
  66.6 4.9 %shard_map.78 = (f32[256,256]{1,0:T(8,128)}, f32[256,64]{1,0:T(8,128)}, f32[256,128]{1,0:T(8,128)}) custom-call(s32[4]{0:T(128)} %get-tuple-element.84.table, bf16[256,2048]{1,0:T(8,128)(2,1)} %collective-permute-done.12.refs_0_, f32[1,8192]{1,0:T(1,128)} %refs_2_.3, bf16[8192,256]{1,0:T(8,128)(2,1)} %bitcast.22, bf16[32,8192]{1,0:T(8,128)(2,1)} %bitcast.38, ...), custom_call_target="tpu_custom_call" | custom-call | flops 335544320 | bytes 3276800 | tf_op jit(solution)/shard_map/pallas_call | solution.py:97
  71.5 4.9 %shard_map.79 = (f32[256,256]{1,0:T(8,128)}, f32[256,64]{1,0:T(8,128)}, f32[256,128]{1,0:T(8,128)}) custom-call(s32[4]{0:T(128)} %get-tuple-element.89.table, bf16[256,2048]{1,0:T(8,128)(2,1)} %collective-permute-done.14.refs_0_, f32[1,8192]{1,0:T(1,128)} %refs_2_.3, bf16[8192,256]{1,0:T(8,128)(2,1)} %bitcast.23, bf16[32,8192]{1,0:T(8,128)(2,1)} %bitcast.39, ...), custom_call_target="tpu_custom_call" | custom-call | flops 335544320 | bytes 3276800 | tf_op jit(solution)/shard_map/pallas_call | solution.py:97
  76.4 4.9 %shard_map.74 = (f32[256,256]{1,0:T(8,128)}, f32[256,64]{1,0:T(8,128)}, f32[256,128]{1,0:T(8,128)}) custom-call(s32[4]{0:T(128)} %get-tuple-element.81.table, bf16[256,2048]{1,0:T(8,128)(2,1)} %collective-permute-done.4.refs_0_, f32[1,8192]{1,0:T(1,128)} %refs_2_.3, bf16[8192,256]{1,0:T(8,128)(2,1)} %bitcast.24, bf16[32,8192]{1,0:T(8,128)(2,1)} %bitcast.40, ...), custom_call_target="tpu_custom_call" | custom-call | flops 335544320 | bytes 3276800 | tf_op jit(solution)/shard_map/pallas_call | solution.py:97
  81.3 4.9 %shard_map.75 = (f32[256,256]{1,0:T(8,128)}, f32[256,64]{1,0:T(8,128)}, f32[256,128]{1,0:T(8,128)}) custom-call(s32[4]{0:T(128)} %get-tuple-element.82.table, bf16[256,2048]{1,0:T(8,128)(2,1)} %collective-permute-done.6.refs_0_, f32[1,8192]{1,0:T(1,128)} %refs_2_.3, bf16[8192,256]{1,0:T(8,128)(2,1)} %bitcast.25, bf16[32,8192]{1,0:T(8,128)(2,1)} %bitcast.41, ...), custom_call_target="tpu_custom_call" | custom-call | flops 335544320 | bytes 3276800 | tf_op jit(solution)/shard_map/pallas_call | solution.py:97
  87.0 5.2 %shard_map.76 = (bf16[256,256]{1,0:T(8,128)(2,1)}, bf16[256,64]{1,0:T(8,128)(2,1)}) custom-call(s32[4]{0:T(128)} %get-tuple-element.83.table, bf16[128,2048]{1,0:T(8,128)(2,1)} %collective-permute-done.5.refs_0_, bf16[128,2048]{1,0:T(8,128)(2,1)} %copy-done.10, f32[1,8192]{1,0:T(1,128)} %refs_2_.3, bf16[8192,256]{1,0:T(8,128)(2,1)} %bitcast.26, ...), custom_call_target="tpu_custom_call" | custom-call | flops 335544320 | bytes 3276800 | tf_op jit(solution)/shard_map/pallas_call | solution.py:97
  92.2 0.8 constant_dynamic-update-slice_fusion.1
  93.1 0.8 copy-done.9
  94.1 5.2 %shard_map.80 = (bf16[256,256]{1,0:T(8,128)(2,1)}, bf16[256,64]{1,0:T(8,128)(2,1)}) custom-call(s32[4]{0:T(128)} %get-tuple-element.91.table, bf16[128,2048]{1,0:T(8,128)(2,1)} %copy-done.11, bf16[128,2048]{1,0:T(8,128)(2,1)} %copy-done.9, f32[1,8192]{1,0:T(1,128)} %refs_2_.3, bf16[8192,256]{1,0:T(8,128)(2,1)} %bitcast.27, bf16[32,8192]{1,0:T(8,128)(2,1)} %bitcast.43, ...), custom_call_target="tpu_custom_call" | custom-call | flops 335544320 | bytes 3276800 | tf_op jit(solution)/shard_map/pallas_call | solution.py:97
  99.3 0.9 constant_dynamic-update-slice_fusion.own
  100.2 4.4 %collective-permute-start.17 = (bf16[512,64]{1,0:T(8,128)(2,1)S(1)}, bf16[512,64]{1,0:T(8,128)(2,1)S(1)}, u32[]{:S(2)}, u32[]{:S(2)}) collective-permute-start(bf16[512,64]{1,0:T(8,128)(2,1)S(1)} %constant_dynamic-update-slice_fusion.own), channel_id=1, source_target_pairs={{0,32},{16,48},{32,0},{48,16},{1,33},{17,49},{33,1},{49,17},{2,34}... | collective-permute-start | bytes 196616 | tf_op jit(solution)/shard_map/ppermute | solution.py:20
  104.7 1.0 pad_maximum_fusion.5
  105.7 0.8 collective-permute-done.18.left
  106.5 2.5 %collective-permute-done.17.two = bf16[512,64]{1,0:T(8,128)(2,1)S(1)} collective-permute-done((bf16[512,64]{1,0:T(8,128)(2,1)S(1)}, bf16[512,64]{1,0:T(8,128)(2,1)S(1)}, u32[]{:S(2)}, u32[]{:S(2)}) %collective-permute-start.17) | collective-permute-done | bytes 65568 | tf_op jit(solution)/shard_map/ppermute | solution.py:20
  110.3 3.8 %shard_map.86.refs_0_ = bf16[256,256]{1,0:T(8,128)(2,1)} custom-call(s32[1]{0:T(128)} %bitcast.1.place, bf16[256,256]{1,0:T(8,128)(2,1)} %get-tuple-element.54.q, bf16[512,64]{1,0:T(8,128)(2,1)} %copy-done.8, bf16[512,64]{1,0:T(8,128)(2,1)} %copy-done.18, bf16[512,64]{1,0:T(8,128)(2,1)} %copy-done.17, bf16[512,64]{1,0:T(8,128)(2,1)} %copy-done.16, ...), custom_call_target="tpu_custom_call" | custom-call | flops 134217728 | bytes 262144 | tf_op jit(solution)/shard_map/pallas_call | solution.py:148
  114.1 4.5 %shard_map.87 = (bf16[128,2048]{1,0:T(8,128)(2,1)}, bf16[128,2048]{1,0:T(8,128)(2,1)}) custom-call(s32[4]{0:T(128)} %get-tuple-element.91.table, bf16[256,256]{1,0:T(8,128)(2,1)} %shard_map.86.refs_0_, bf16[256,8192]{1,0:T(8,128)(2,1)} %bitcast.28), custom_call_target="tpu_custom_call" | custom-call | flops 268435456 | bytes 2097152 | tf_op jit(solution)/shard_map/pallas_call | solution.py:192
  118.6 1.7 collective-permute-start.29
  120.6 3.2 %shard_map.81.refs_0_ = bf16[256,256]{1,0:T(8,128)(2,1)} custom-call(s32[1]{0:T(128)} %bitcast.1.place, bf16[256,256]{1,0:T(8,128)(2,1)} %get-tuple-element.40.q, bf16[512,64]{1,0:T(8,128)(2,1)} %copy-done.8, bf16[512,64]{1,0:T(8,128)(2,1)} %copy-done.18, bf16[512,64]{1,0:T(8,128)(2,1)} %copy-done.17, bf16[512,64]{1,0:T(8,128)(2,1)} %copy-done.16, ...), custom_call_target="tpu_custom_call" | custom-call | flops 67108864 | bytes 262144 | tf_op jit(solution)/shard_map/pallas_call | solution.py:148
  123.8 4.5 %shard_map.82 = (bf16[128,2048]{1,0:T(8,128)(2,1)}, bf16[128,2048]{1,0:T(8,128)(2,1)}) custom-call(s32[4]{0:T(128)} %get-tuple-element.83.table, bf16[256,256]{1,0:T(8,128)(2,1)} %shard_map.81.refs_0_, bf16[256,8192]{1,0:T(8,128)(2,1)} %bitcast.29), custom_call_target="tpu_custom_call" | custom-call | flops 268435456 | bytes 2097152 | tf_op jit(solution)/shard_map/pallas_call | solution.py:192
  128.3 3.2 %collective-permute-start.21 = (bf16[128,2048]{1,0:T(8,128)(2,1)}, bf16[128,2048]{1,0:T(8,128)(2,1)S(1)}, u32[]{:S(2)}, u32[]{:S(2)}) collective-permute-start(bf16[128,2048]{1,0:T(8,128)(2,1)} %get-tuple-element.53), channel_id=1, source_target_pairs={{0,192},{64,0},{128,64},{192,128},{1,193},{65,1},{129,65},{193,129... | collective-permute-start | bytes 1572872 | tf_op jit(solution)/shard_map/ppermute | solution.py:20
  132.3 4.7 %shard_map.89 = bf16[256,2048]{1,0:T(8,128)(2,1)} custom-call(s32[4]{0:T(128)} %get-tuple-element.84.table, bf16[256,256]{1,0:T(8,128)(2,1)} %shard_map.86.refs_0_, bf16[256,8192]{1,0:T(8,128)(2,1)} %bitcast.30, bf16[128,2048]{1,0:T(8,128)(2,1)} %copy-done.14), custom_call_target="tpu_custom_call" | custom-call | flops 268435456 | bytes 2097152 | tf_op jit(solution)/shard_map/pallas_call | solution.py:192
  137.0 2.9 %collective-permute-start.30 = (bf16[256,2048]{1,0:T(8,128)(2,1)}, bf16[256,2048]{1,0:T(8,128)(2,1)S(1)}, u32[]{:S(2)}, u32[]{:S(2)}) collective-permute-start(bf16[256,2048]{1,0:T(8,128)(2,1)} %shard_map.89), channel_id=1, source_target_pairs={{0,48},{16,0},{32,16},{48,32},{1,49},{17,1},{33,17},{49,33},{2,50}... | collective-permute-start | bytes 3145736 | tf_op jit(solution)/shard_map/ppermute | solution.py:20
  140.7 4.7 %shard_map.88 = bf16[256,2048]{1,0:T(8,128)(2,1)} custom-call(s32[4]{0:T(128)} %get-tuple-element.89.table, bf16[256,256]{1,0:T(8,128)(2,1)} %shard_map.86.refs_0_, bf16[256,8192]{1,0:T(8,128)(2,1)} %bitcast.31, bf16[128,2048]{1,0:T(8,128)(2,1)} %copy-done.12), custom_call_target="tpu_custom_call" | custom-call | flops 268435456 | bytes 2097152 | tf_op jit(solution)/shard_map/pallas_call | solution.py:192
  145.5 0.8 copy-done.15
  146.3 4.7 %shard_map.84 = bf16[256,2048]{1,0:T(8,128)(2,1)} custom-call(s32[4]{0:T(128)} %get-tuple-element.81.table, bf16[256,256]{1,0:T(8,128)(2,1)} %shard_map.81.refs_0_, bf16[256,8192]{1,0:T(8,128)(2,1)} %bitcast.32, bf16[128,2048]{1,0:T(8,128)(2,1)} %copy-done.15), custom_call_target="tpu_custom_call" | custom-call | flops 268435456 | bytes 2097152 | tf_op jit(solution)/shard_map/pallas_call | solution.py:192
  151.0 3.3 %collective-permute-start.22 = (bf16[256,2048]{1,0:T(8,128)(2,1)}, bf16[256,2048]{1,0:T(8,128)(2,1)S(1)}, u32[]{:S(2)}, u32[]{:S(2)}) collective-permute-start(bf16[256,2048]{1,0:T(8,128)(2,1)} %shard_map.84), channel_id=1, source_target_pairs={{0,192},{64,0},{128,64},{192,128},{1,193},{65,1},{129,65},{193,129... | collective-permute-start | bytes 3145736 | tf_op jit(solution)/shard_map/ppermute | solution.py:20
  154.2 0.8 copy-done.13
  155.1 4.7 %shard_map.83 = bf16[256,2048]{1,0:T(8,128)(2,1)} custom-call(s32[4]{0:T(128)} %get-tuple-element.82.table, bf16[256,256]{1,0:T(8,128)(2,1)} %shard_map.81.refs_0_, bf16[256,8192]{1,0:T(8,128)(2,1)} %bitcast.33, bf16[128,2048]{1,0:T(8,128)(2,1)} %copy-done.13), custom_call_target="tpu_custom_call" | custom-call | flops 268435456 | bytes 2097152 | tf_op jit(solution)/shard_map/pallas_call | solution.py:192
  159.7 6.6 %collective-permute-done.28.refs_2_ = bf16[256,2048]{1,0:T(8,128)(2,1)} collective-permute-done((bf16[256,2048]{1,0:T(8,128)(2,1)}, bf16[256,2048]{1,0:T(8,128)(2,1)}, u32[]{:S(2)}, u32[]{:S(2)}) %collective-permute-start.28) | collective-permute-done | bytes 1048608 | tf_op jit(solution)/shard_map/ppermute | solution.py:20
  166.4 5.2 %shard_map.90 = f32[256,2048]{1,0:T(8,128)} custom-call(s32[4]{0:T(128)} %get-tuple-element.90.table, bf16[256,256]{1,0:T(8,128)(2,1)} %shard_map.86.refs_0_, bf16[256,8192]{1,0:T(8,128)(2,1)} %bitcast.34, bf16[256,2048]{1,0:T(8,128)(2,1)} %collective-permute-done.28.refs_2_, bf16[256,2048]{1,0:T(8,128)(2,1)} %copy-done.6), custom_call_target="tpu_custom_call" | custom-call | flops 268435456 | bytes 2097152 | tf_op jit(solution)/shard_map/pallas_call | solution.py:192
  171.6 1.7 convert.37
  174.0 3.2 %collective-permute-start.33 = (bf16[128,512]{1,0:T(8,128)(2,1)S(1)}, bf16[128,512]{1,0:T(8,128)(2,1)S(1)}, u32[]{:S(2)}, u32[]{:S(2)}) collective-permute-start(bf16[128,512]{1,0:T(8,128)(2,1)S(1)} %get-tuple-element.70), channel_id=1, source_target_pairs={{0,192},{64,0},{128,64},{192,128},{1,193},{65,1},{129,65},{193,129... | collective-permute-start | bytes 393224 | tf_op jit(solution)/shard_map/ppermute | solution.py:20
  177.3 4.1 %collective-permute-done.20.refs_2_ = bf16[256,2048]{1,0:T(8,128)(2,1)S(1)} collective-permute-done((bf16[256,2048]{1,0:T(8,128)(2,1)}, bf16[256,2048]{1,0:T(8,128)(2,1)S(1)}, u32[]{:S(2)}, u32[]{:S(2)}) %collective-permute-start.20) | collective-permute-done | bytes 1048608 | tf_op jit(solution)/shard_map/ppermute | solution.py:20
  181.4 1.0 copy-done.7
  182.4 5.2 %shard_map.85 = f32[256,2048]{1,0:T(8,128)} custom-call(s32[4]{0:T(128)} %get-tuple-element.57.table, bf16[256,256]{1,0:T(8,128)(2,1)} %shard_map.81.refs_0_, bf16[256,8192]{1,0:T(8,128)(2,1)} %bitcast.35, bf16[256,2048]{1,0:T(8,128)(2,1)} %copy-done.7, bf16[256,2048]{1,0:T(8,128)(2,1)} %copy-done.5), custom_call_target="tpu_custom_call" | custom-call | flops 268435456 | bytes 2097152 | tf_op jit(solution)/shard_map/pallas_call | solution.py:192
  187.6 1.9 convert.33
  189.6 3.2 %collective-permute-start.25 = (bf16[128,512]{1,0:T(8,128)(2,1)S(1)}, bf16[128,512]{1,0:T(8,128)(2,1)S(1)}, u32[]{:S(2)}, u32[]{:S(2)}) collective-permute-start(bf16[128,512]{1,0:T(8,128)(2,1)S(1)} %get-tuple-element.66), channel_id=1, source_target_pairs={{0,48},{16,0},{32,16},{48,32},{1,49},{17,1},{33,17},{49,33},{2,50}... | collective-permute-start | bytes 393224 | tf_op jit(solution)/shard_map/ppermute | solution.py:20
  193.1 2.1 collective-permute-start.32
  195.2 1.9 collective-permute-done.23
  197.2 2.0 collective-permute-start.26
  199.4 1.3 collective-permute-done.32
  200.8 2.9 %collective-permute-done.26 = bf16[256,512]{1,0:T(8,128)(2,1)S(1)} collective-permute-done((bf16[256,512]{1,0:T(8,128)(2,1)S(1)}, bf16[256,512]{1,0:T(8,128)(2,1)S(1)}, u32[]{:S(2)}, u32[]{:S(2)}) %collective-permute-start.26) | collective-permute-done | bytes 262176 | tf_op jit(solution)/shard_map/ppermute | solution.py:20
  203.6 3.3 %collective-permute-done.24 = bf16[256,512]{1,0:T(8,128)(2,1)S(1)} collective-permute-done((bf16[256,512]{1,0:T(8,128)(2,1)S(1)}, bf16[256,512]{1,0:T(8,128)(2,1)S(1)}, u32[]{:S(2)}, u32[]{:S(2)}) %collective-permute-start.24) | collective-permute-done | bytes 262176 | tf_op jit(solution)/shard_map/ppermute | solution.py:20
  207.3 9.8 %collective-permute-done.35 = bf16[512,512]{1,0:T(8,128)(2,1)S(1)} collective-permute-done((bf16[512,512]{1,0:T(8,128)(2,1)S(1)}, bf16[512,512]{1,0:T(8,128)(2,1)S(1)}, u32[]{:S(2)}, u32[]{:S(2)}) %collective-permute-start.35) | collective-permute-done | bytes 524320 | tf_op jit(solution)/shard_map/ppermute | solution.py:20
  217.1 1.1 bitcast_convert_fusion
  (99 shorter events, 8.6 us)
Async XLA Ops:
  1.1 8.4 %collective-permute-start.1 = (bf16[256,512]{1,0:T(8,128)(2,1)S(1)}, bf16[256,512]{1,0:T(8,128)(2,1)S(1)}, u32[]{:S(2)}, u32[]{:S(2)}) collective-permute-start(bf16[256,512]{1,0:T(8,128)(2,1)S(1)} %get-tuple-element.77), channel_id=1, source_target_pairs={{0,48},{16,0},{32,16},{48,32},{1,49},{17,1},{33,17},{49,33},{2,50}... | collective-permute-start | bytes 786440 | tf_op jit(solution)/shard_map/ppermute | solution.py:20
  3.9 9.4 %collective-permute-start = (bf16[256,512]{1,0:T(8,128)(2,1)S(1)}, bf16[256,512]{1,0:T(8,128)(2,1)S(1)}, u32[]{:S(2)}, u32[]{:S(2)}) collective-permute-start(bf16[256,512]{1,0:T(8,128)(2,1)S(1)} %get-tuple-element.77), channel_id=1, source_target_pairs={{0,16},{16,32},{32,48},{48,0},{1,17},{17,33},{33,49},{49,1},{2,18}... | collective-permute-start | bytes 786440 | tf_op jit(solution)/shard_map/ppermute | solution.py:20
  3.9 9.5 %collective-permute-start.9 = (bf16[256,512]{1,0:T(8,128)(2,1)S(1)}, bf16[256,512]{1,0:T(8,128)(2,1)S(1)}, u32[]{:S(2)}, u32[]{:S(2)}) collective-permute-start(bf16[256,512]{1,0:T(8,128)(2,1)S(1)} %get-tuple-element.78), channel_id=1, source_target_pairs={{0,192},{64,0},{128,64},{192,128},{1,193},{65,1},{129,65},{193,129... | collective-permute-start | bytes 786440 | tf_op jit(solution)/shard_map/ppermute | solution.py:20
  6.9 9.6 %collective-permute-start.8 = (bf16[256,512]{1,0:T(8,128)(2,1)S(1)}, bf16[256,512]{1,0:T(8,128)(2,1)S(1)}, u32[]{:S(2)}, u32[]{:S(2)}) collective-permute-start(bf16[256,512]{1,0:T(8,128)(2,1)S(1)} %get-tuple-element.78), channel_id=1, source_target_pairs={{0,64},{64,128},{128,192},{192,0},{1,65},{65,129},{129,193},{193,1... | collective-permute-start | bytes 786440 | tf_op jit(solution)/shard_map/ppermute | solution.py:20
  9.5 7.1 %collective-permute-start.3 = (bf16[128,512]{1,0:T(8,128)(2,1)S(1)}, bf16[128,512]{1,0:T(8,128)(2,1)S(1)}, u32[]{:S(2)}, u32[]{:S(2)}) collective-permute-start(bf16[128,512]{1,0:T(8,128)(2,1)S(1)} %slice.145), channel_id=1, source_target_pairs={{0,48},{16,0},{32,16},{48,32},{1,49},{17,1},{33,17},{49,33},{2,50}... | collective-permute-start | bytes 393224 | tf_op jit(solution)/shard_map/ppermute | solution.py:20
  13.3 6.3 %collective-permute-start.2 = (bf16[128,512]{1,0:T(8,128)(2,1)S(1)}, bf16[128,512]{1,0:T(8,128)(2,1)S(1)}, u32[]{:S(2)}, u32[]{:S(2)}) collective-permute-start(bf16[128,512]{1,0:T(8,128)(2,1)S(1)} %slice.144), channel_id=1, source_target_pairs={{0,16},{16,32},{32,48},{48,0},{1,17},{17,33},{33,49},{49,1},{2,18}... | collective-permute-start | bytes 393224 | tf_op jit(solution)/shard_map/ppermute | solution.py:20
  13.4 9.4 %collective-permute-start.11 = (bf16[128,512]{1,0:T(8,128)(2,1)S(1)}, bf16[128,512]{1,0:T(8,128)(2,1)S(1)}, u32[]{:S(2)}, u32[]{:S(2)}) collective-permute-start(bf16[128,512]{1,0:T(8,128)(2,1)S(1)} %slice.153), channel_id=1, source_target_pairs={{0,192},{64,0},{128,64},{192,128},{1,193},{65,1},{129,65},{193,129... | collective-permute-start | bytes 393224 | tf_op jit(solution)/shard_map/ppermute | solution.py:20
  16.5 11.1 %copy-start.19 = (s32[4]{0:T(128)S(1)}, s32[4]{0:T(128)}, u32[]{:S(2)}) copy-start(s32[4]{0:T(128)} %constant.138.clone) | copy-start | bytes 52
  16.5 6.3 %collective-permute-start.10 = (bf16[128,512]{1,0:T(8,128)(2,1)S(1)}, bf16[128,512]{1,0:T(8,128)(2,1)S(1)}, u32[]{:S(2)}, u32[]{:S(2)}) collective-permute-start(bf16[128,512]{1,0:T(8,128)(2,1)S(1)} %slice.152), channel_id=1, source_target_pairs={{0,64},{64,128},{128,192},{192,0},{1,65},{65,129},{129,193},{193,1... | collective-permute-start | bytes 393224 | tf_op jit(solution)/shard_map/ppermute | solution.py:20
  19.7 30.8 %copy-start.2 = (bf16[256,2048]{1,0:T(8,128)(2,1)}, bf16[256,2048]{1,0:T(8,128)(2,1)S(1)}, u32[]{:S(2)}) copy-start(bf16[256,2048]{1,0:T(8,128)(2,1)S(1)} %maximum_maximum_fusion.refs_0_) | copy-start | bytes 3145732
  19.7 23.2 %collective-permute-start.6 = (bf16[256,2048]{1,0:T(8,128)(2,1)S(1)}, bf16[256,2048]{1,0:T(8,128)(2,1)}, u32[]{:S(2)}, u32[]{:S(2)}) collective-permute-start(bf16[256,2048]{1,0:T(8,128)(2,1)S(1)} %maximum_maximum_fusion.refs_0_), channel_id=1, source_target_pairs={{0,192},{64,0},{128,64},{192,128},{1,193},{65,1},{129,65},{193,129... | collective-permute-start | bytes 3145736 | tf_op jit(solution)/shard_map/ppermute | solution.py:20
  22.8 25.8 %collective-permute-start.4 = (bf16[256,2048]{1,0:T(8,128)(2,1)S(1)}, bf16[256,2048]{1,0:T(8,128)(2,1)}, u32[]{:S(2)}, u32[]{:S(2)}) collective-permute-start(bf16[256,2048]{1,0:T(8,128)(2,1)S(1)} %maximum_maximum_fusion.refs_0_), channel_id=1, source_target_pairs={{0,64},{64,128},{128,192},{192,0},{1,65},{65,129},{129,193},{193,1... | collective-permute-start | bytes 3145736 | tf_op jit(solution)/shard_map/ppermute | solution.py:20
  22.9 28.6 %copy-start.3 = (bf16[256,2048]{1,0:T(8,128)(2,1)}, bf16[256,2048]{1,0:T(8,128)(2,1)S(1)}, u32[]{:S(2)}) copy-start(bf16[256,2048]{1,0:T(8,128)(2,1)S(1)} %maximum_maximum_fusion.1.refs_0_) | copy-start | bytes 3145732
  22.9 28.6 %collective-permute-start.14 = (bf16[256,2048]{1,0:T(8,128)(2,1)S(1)}, bf16[256,2048]{1,0:T(8,128)(2,1)}, u32[]{:S(2)}, u32[]{:S(2)}) collective-permute-start(bf16[256,2048]{1,0:T(8,128)(2,1)S(1)} %maximum_maximum_fusion.1.refs_0_), channel_id=1, source_target_pairs={{0,48},{16,0},{32,16},{48,32},{1,49},{17,1},{33,17},{49,33},{2,50}... | collective-permute-start | bytes 3145736 | tf_op jit(solution)/shard_map/ppermute | solution.py:20
  27.5 27.7 %collective-permute-start.12 = (bf16[256,2048]{1,0:T(8,128)(2,1)S(1)}, bf16[256,2048]{1,0:T(8,128)(2,1)}, u32[]{:S(2)}, u32[]{:S(2)}) collective-permute-start(bf16[256,2048]{1,0:T(8,128)(2,1)S(1)} %maximum_maximum_fusion.1.refs_0_), channel_id=1, source_target_pairs={{0,16},{16,32},{32,48},{48,0},{1,17},{17,33},{33,49},{49,1},{2,18}... | collective-permute-start | bytes 3145736 | tf_op jit(solution)/shard_map/ppermute | solution.py:20
  44.8 41.4 %collective-permute-start.7 = (bf16[128,2048]{1,0:T(8,128)(2,1)}, bf16[128,2048]{1,0:T(8,128)(2,1)S(1)}, u32[]{:S(2)}, u32[]{:S(2)}) collective-permute-start(bf16[128,2048]{1,0:T(8,128)(2,1)} %slice.147), channel_id=1, source_target_pairs={{0,192},{64,0},{128,64},{192,128},{1,193},{65,1},{129,65},{193,129... | collective-permute-start | bytes 1572872 | tf_op jit(solution)/shard_map/ppermute | solution.py:20
  50.5 35.7 %collective-permute-start.5 = (bf16[128,2048]{1,0:T(8,128)(2,1)}, bf16[128,2048]{1,0:T(8,128)(2,1)}, u32[]{:S(2)}, u32[]{:S(2)}) collective-permute-start(bf16[128,2048]{1,0:T(8,128)(2,1)} %slice.146), channel_id=1, source_target_pairs={{0,64},{64,128},{128,192},{192,0},{1,65},{65,129},{129,193},{193,1... | collective-permute-start | bytes 1572872 | tf_op jit(solution)/shard_map/ppermute | solution.py:20
  53.4 39.7 %collective-permute-start.15 = (bf16[128,2048]{1,0:T(8,128)(2,1)}, bf16[128,2048]{1,0:T(8,128)(2,1)S(1)}, u32[]{:S(2)}, u32[]{:S(2)}) collective-permute-start(bf16[128,2048]{1,0:T(8,128)(2,1)} %slice.155), channel_id=1, source_target_pairs={{0,48},{16,0},{32,16},{48,32},{1,49},{17,1},{33,17},{49,33},{2,50}... | collective-permute-start | bytes 1572872 | tf_op jit(solution)/shard_map/ppermute | solution.py:20
  56.3 36.8 %collective-permute-start.13 = (bf16[128,2048]{1,0:T(8,128)(2,1)S(1)}, bf16[128,2048]{1,0:T(8,128)(2,1)S(1)}, u32[]{:S(2)}, u32[]{:S(2)}) collective-permute-start(bf16[128,2048]{1,0:T(8,128)(2,1)S(1)} %slice.154), channel_id=1, source_target_pairs={{0,16},{16,32},{32,48},{48,0},{1,17},{17,33},{33,49},{49,1},{2,18}... | collective-permute-start | bytes 1572872 | tf_op jit(solution)/shard_map/ppermute | solution.py:20
  86.2 0.8 copy-start.10
  93.1 0.8 copy-start.9
  93.1 0.9 copy-start.11
  100.1 9.5 %copy-start.8 = (bf16[512,64]{1,0:T(8,128)(2,1)}, bf16[512,64]{1,0:T(8,128)(2,1)S(1)}, u32[]{:S(2)}) copy-start(bf16[512,64]{1,0:T(8,128)(2,1)S(1)} %constant_dynamic-update-slice_fusion.own) | copy-start | bytes 196612
  100.1 6.3 %collective-permute-start.18 = (bf16[512,64]{1,0:T(8,128)(2,1)S(1)}, bf16[512,64]{1,0:T(8,128)(2,1)S(1)}, u32[]{:S(2)}, u32[]{:S(2)}) collective-permute-start(bf16[512,64]{1,0:T(8,128)(2,1)S(1)} %constant_dynamic-update-slice_fusion.own), channel_id=1, source_target_pairs={{0,16},{16,32},{32,48},{48,0},{1,17},{17,33},{33,49},{49,1},{2,18}... | collective-permute-start | bytes 196616 | tf_op jit(solution)/shard_map/ppermute | solution.py:20
  100.2 8.8 %collective-permute-start.17 = (bf16[512,64]{1,0:T(8,128)(2,1)S(1)}, bf16[512,64]{1,0:T(8,128)(2,1)S(1)}, u32[]{:S(2)}, u32[]{:S(2)}) collective-permute-start(bf16[512,64]{1,0:T(8,128)(2,1)S(1)} %constant_dynamic-update-slice_fusion.own), channel_id=1, source_target_pairs={{0,32},{16,48},{32,0},{48,16},{1,33},{17,49},{33,1},{49,17},{2,34}... | collective-permute-start | bytes 196616 | tf_op jit(solution)/shard_map/ppermute | solution.py:20
  104.7 5.0 %collective-permute-start.16 = (bf16[512,64]{1,0:T(8,128)(2,1)S(1)}, bf16[512,64]{1,0:T(8,128)(2,1)S(1)}, u32[]{:S(2)}, u32[]{:S(2)}) collective-permute-start(bf16[512,64]{1,0:T(8,128)(2,1)S(1)} %constant_dynamic-update-slice_fusion.own), channel_id=1, source_target_pairs={{0,48},{16,0},{32,16},{48,32},{1,49},{17,1},{33,17},{49,33},{2,50}... | collective-permute-start | bytes 196616 | tf_op jit(solution)/shard_map/ppermute | solution.py:20
  106.5 3.2 %copy-start.16 = (bf16[512,64]{1,0:T(8,128)(2,1)}, bf16[512,64]{1,0:T(8,128)(2,1)S(1)}, u32[]{:S(2)}) copy-start(bf16[512,64]{1,0:T(8,128)(2,1)S(1)} %collective-permute-done.18.left) | copy-start | bytes 196612
  109.0 0.7 copy-start.17
  109.6 0.6 copy-start.18
  118.6 12.9 %collective-permute-start.29 = (bf16[128,2048]{1,0:T(8,128)(2,1)}, bf16[128,2048]{1,0:T(8,128)(2,1)S(1)}, u32[]{:S(2)}, u32[]{:S(2)}) collective-permute-start(bf16[128,2048]{1,0:T(8,128)(2,1)} %get-tuple-element.56), channel_id=1, source_target_pairs={{0,48},{16,0},{32,16},{48,32},{1,49},{17,1},{33,17},{49,33},{2,50}... | collective-permute-start | bytes 1572872 | tf_op jit(solution)/shard_map/ppermute | solution.py:20
  120.3 19.6 %collective-permute-start.27 = (bf16[128,2048]{1,0:T(8,128)(2,1)}, bf16[128,2048]{1,0:T(8,128)(2,1)S(1)}, u32[]{:S(2)}, u32[]{:S(2)}) collective-permute-start(bf16[128,2048]{1,0:T(8,128)(2,1)} %get-tuple-element.55), channel_id=1, source_target_pairs={{0,16},{16,32},{32,48},{48,0},{1,17},{17,33},{33,49},{49,1},{2,18}... | collective-permute-start | bytes 1572872 | tf_op jit(solution)/shard_map/ppermute | solution.py:20
  128.3 17.2 %collective-permute-start.21 = (bf16[128,2048]{1,0:T(8,128)(2,1)}, bf16[128,2048]{1,0:T(8,128)(2,1)S(1)}, u32[]{:S(2)}, u32[]{:S(2)}) collective-permute-start(bf16[128,2048]{1,0:T(8,128)(2,1)} %get-tuple-element.53), channel_id=1, source_target_pairs={{0,192},{64,0},{128,64},{192,128},{1,193},{65,1},{129,65},{193,129... | collective-permute-start | bytes 1572872 | tf_op jit(solution)/shard_map/ppermute | solution.py:20
  131.5 22.7 %collective-permute-start.19 = (bf16[128,2048]{1,0:T(8,128)(2,1)}, bf16[128,2048]{1,0:T(8,128)(2,1)S(1)}, u32[]{:S(2)}, u32[]{:S(2)}) collective-permute-start(bf16[128,2048]{1,0:T(8,128)(2,1)} %get-tuple-element.52), channel_id=1, source_target_pairs={{0,64},{64,128},{128,192},{192,0},{1,65},{65,129},{129,193},{193,1... | collective-permute-start | bytes 1572872 | tf_op jit(solution)/shard_map/ppermute | solution.py:20
  131.5 0.8 copy-start.14
  137.0 22.7 %collective-permute-start.30 = (bf16[256,2048]{1,0:T(8,128)(2,1)}, bf16[256,2048]{1,0:T(8,128)(2,1)S(1)}, u32[]{:S(2)}, u32[]{:S(2)}) collective-permute-start(bf16[256,2048]{1,0:T(8,128)(2,1)} %shard_map.89), channel_id=1, source_target_pairs={{0,48},{16,0},{32,16},{48,32},{1,49},{17,1},{33,17},{49,33},{2,50}... | collective-permute-start | bytes 3145736 | tf_op jit(solution)/shard_map/ppermute | solution.py:20
  139.9 0.8 copy-start.12
  145.4 20.9 %collective-permute-start.28 = (bf16[256,2048]{1,0:T(8,128)(2,1)}, bf16[256,2048]{1,0:T(8,128)(2,1)}, u32[]{:S(2)}, u32[]{:S(2)}) collective-permute-start(bf16[256,2048]{1,0:T(8,128)(2,1)} %shard_map.88), channel_id=1, source_target_pairs={{0,16},{16,32},{32,48},{48,0},{1,17},{17,33},{33,49},{49,1},{2,18}... | collective-permute-start | bytes 3145736 | tf_op jit(solution)/shard_map/ppermute | solution.py:20
  145.5 0.8 copy-start.15
  151.0 26.3 %collective-permute-start.22 = (bf16[256,2048]{1,0:T(8,128)(2,1)}, bf16[256,2048]{1,0:T(8,128)(2,1)S(1)}, u32[]{:S(2)}, u32[]{:S(2)}) collective-permute-start(bf16[256,2048]{1,0:T(8,128)(2,1)} %shard_map.84), channel_id=1, source_target_pairs={{0,192},{64,0},{128,64},{192,128},{1,193},{65,1},{129,65},{193,129... | collective-permute-start | bytes 3145736 | tf_op jit(solution)/shard_map/ppermute | solution.py:20
  154.2 0.8 copy-start.13
  159.7 21.7 %collective-permute-start.20 = (bf16[256,2048]{1,0:T(8,128)(2,1)}, bf16[256,2048]{1,0:T(8,128)(2,1)S(1)}, u32[]{:S(2)}, u32[]{:S(2)}) collective-permute-start(bf16[256,2048]{1,0:T(8,128)(2,1)} %shard_map.83), channel_id=1, source_target_pairs={{0,64},{64,128},{128,192},{192,0},{1,65},{65,129},{129,193},{193,1... | collective-permute-start | bytes 3145736 | tf_op jit(solution)/shard_map/ppermute | solution.py:20
  159.7 6.7 %copy-start.6 = (bf16[256,2048]{1,0:T(8,128)(2,1)}, bf16[256,2048]{1,0:T(8,128)(2,1)S(1)}, u32[]{:S(2)}) copy-start(bf16[256,2048]{1,0:T(8,128)(2,1)S(1)} %collective-permute-done.30.refs_3_) | copy-start | bytes 3145732
  174.0 18.8 %collective-permute-start.31 = (bf16[128,512]{1,0:T(8,128)(2,1)}, bf16[128,512]{1,0:T(8,128)(2,1)S(1)}, u32[]{:S(2)}, u32[]{:S(2)}) collective-permute-start(bf16[128,512]{1,0:T(8,128)(2,1)} %get-tuple-element.69), channel_id=1, source_target_pairs={{0,64},{64,128},{128,192},{192,0},{1,65},{65,129},{129,193},{193,1... | collective-permute-start | bytes 393224 | tf_op jit(solution)/shard_map/ppermute | solution.py:20
  174.0 18.8 %collective-permute-start.33 = (bf16[128,512]{1,0:T(8,128)(2,1)S(1)}, bf16[128,512]{1,0:T(8,128)(2,1)S(1)}, u32[]{:S(2)}, u32[]{:S(2)}) collective-permute-start(bf16[128,512]{1,0:T(8,128)(2,1)S(1)} %get-tuple-element.70), channel_id=1, source_target_pairs={{0,192},{64,0},{128,64},{192,128},{1,193},{65,1},{129,65},{193,129... | collective-permute-start | bytes 393224 | tf_op jit(solution)/shard_map/ppermute | solution.py:20
  177.3 4.1 %copy-start.5 = (bf16[256,2048]{1,0:T(8,128)(2,1)}, bf16[256,2048]{1,0:T(8,128)(2,1)S(1)}, u32[]{:S(2)}) copy-start(bf16[256,2048]{1,0:T(8,128)(2,1)S(1)} %collective-permute-done.22.refs_3_) | copy-start | bytes 3145732
  181.4 1.0 copy-start.7
  187.6 5.3 %copy-start = (f32[256,2048]{1,0:T(8,128)S(1)}, f32[256,2048]{1,0:T(8,128)}, u32[]{:S(2)}) copy-start(f32[256,2048]{1,0:T(8,128)} %shard_map.90) | copy-start | bytes 6291460
  189.5 7.6 %copy-start.1 = (f32[256,2048]{1,0:T(8,128)S(1)}, f32[256,2048]{1,0:T(8,128)}, u32[]{:S(2)}) copy-start(f32[256,2048]{1,0:T(8,128)} %shard_map.85) | copy-start | bytes 6291460
  189.5 7.5 %collective-permute-start.23 = (bf16[128,512]{1,0:T(8,128)(2,1)S(1)}, bf16[128,512]{1,0:T(8,128)(2,1)S(1)}, u32[]{:S(2)}, u32[]{:S(2)}) collective-permute-start(bf16[128,512]{1,0:T(8,128)(2,1)S(1)} %get-tuple-element.65), channel_id=1, source_target_pairs={{0,16},{16,32},{32,48},{48,0},{1,17},{17,33},{33,49},{49,1},{2,18}... | collective-permute-start | bytes 393224 | tf_op jit(solution)/shard_map/ppermute | solution.py:20
  189.6 17.3 %copy-start.4 = (bf16[1,512,512]{2,1,0:T(8,128)(2,1)S(1)}, bf16[1,512,512]{2,1,0:T(8,128)(2,1)}, u32[]{:S(2)}) copy-start(bf16[1,512,512]{2,1,0:T(8,128)(2,1)} %param.7) | copy-start | bytes 1572868
  189.6 7.4 %collective-permute-start.25 = (bf16[128,512]{1,0:T(8,128)(2,1)S(1)}, bf16[128,512]{1,0:T(8,128)(2,1)S(1)}, u32[]{:S(2)}, u32[]{:S(2)}) collective-permute-start(bf16[128,512]{1,0:T(8,128)(2,1)S(1)} %get-tuple-element.66), channel_id=1, source_target_pairs={{0,48},{16,0},{32,16},{48,32},{1,49},{17,1},{33,17},{49,33},{2,50}... | collective-permute-start | bytes 393224 | tf_op jit(solution)/shard_map/ppermute | solution.py:20
  193.0 6.5 %collective-permute-start.34 = (bf16[256,512]{1,0:T(8,128)(2,1)S(1)}, bf16[256,512]{1,0:T(8,128)(2,1)S(1)}, u32[]{:S(2)}, u32[]{:S(2)}) collective-permute-start(bf16[256,512]{1,0:T(8,128)(2,1)S(1)} %pad_maximum_fusion.4), channel_id=1, source_target_pairs={{0,192},{64,0},{128,64},{192,128},{1,193},{65,1},{129,65},{193,129... | collective-permute-start | bytes 786440 | tf_op jit(solution)/shard_map/ppermute | solution.py:20
  193.1 7.7 %collective-permute-start.32 = (bf16[256,512]{1,0:T(8,128)(2,1)S(1)}, bf16[256,512]{1,0:T(8,128)(2,1)S(1)}, u32[]{:S(2)}, u32[]{:S(2)}) collective-permute-start(bf16[256,512]{1,0:T(8,128)(2,1)S(1)} %pad_maximum_fusion.3), channel_id=1, source_target_pairs={{0,64},{64,128},{128,192},{192,0},{1,65},{65,129},{129,193},{193,1... | collective-permute-start | bytes 786440 | tf_op jit(solution)/shard_map/ppermute | solution.py:20
  197.2 6.5 %collective-permute-start.26 = (bf16[256,512]{1,0:T(8,128)(2,1)S(1)}, bf16[256,512]{1,0:T(8,128)(2,1)S(1)}, u32[]{:S(2)}, u32[]{:S(2)}) collective-permute-start(bf16[256,512]{1,0:T(8,128)(2,1)S(1)} %pad_maximum_fusion.2), channel_id=1, source_target_pairs={{0,48},{16,0},{32,16},{48,32},{1,49},{17,1},{33,17},{49,33},{2,50}... | collective-permute-start | bytes 786440 | tf_op jit(solution)/shard_map/ppermute | solution.py:20
  199.3 7.7 %collective-permute-start.24 = (bf16[256,512]{1,0:T(8,128)(2,1)S(1)}, bf16[256,512]{1,0:T(8,128)(2,1)S(1)}, u32[]{:S(2)}, u32[]{:S(2)}) collective-permute-start(bf16[256,512]{1,0:T(8,128)(2,1)S(1)} %pad_maximum_fusion.1), channel_id=1, source_target_pairs={{0,16},{16,32},{32,48},{48,0},{1,17},{17,33},{33,49},{49,1},{2,18}... | collective-permute-start | bytes 786440 | tf_op jit(solution)/shard_map/ppermute | solution.py:20
  207.3 9.8 %collective-permute-start.35 = (bf16[512,512]{1,0:T(8,128)(2,1)S(1)}, bf16[512,512]{1,0:T(8,128)(2,1)S(1)}, u32[]{:S(2)}, u32[]{:S(2)}) collective-permute-start(bf16[512,512]{1,0:T(8,128)(2,1)S(1)} %pad_maximum_fusion), channel_id=1, source_target_pairs={{0,1},{1,2},{2,3},{3,4},{4,5},{5,6},{6,7},{7,8},{8,9},{9,10},{10,1... | collective-permute-start | bytes 1572872 | tf_op jit(solution)/shard_map/ppermute | solution.py:20

commit v2 on v0

v2 whole, which is shorter than its diff:
```python
import functools
import math

import jax
import jax.numpy as jnp
import numpy as np
from jax import lax
from jax.experimental import pallas as pl
from jax.experimental.pallas import tpu as pltpu
from jax.sharding import Mesh
from jax.sharding import PartitionSpec as P

KVH = 4
HD = 128
SIDE = 4
EPS = 1e-05
COST = 16
VMEM_BYTES = 20 * 2**20

ROUNDS = (
    (
        ((-1, 0), (0, 0), "tx", 1),
        ((1, 0), (0, 0), "tx", -1),
        ((0, -1), (0, 0), "ty", 1),
        ((0, 1), (0, 0), "ty", -1),
    ),
    (
        ((-1, -1), (0, -1), "tx", 1),
        ((1, 1), (0, 1), "tx", -1),
        ((1, -1), (1, 0), "ty", 1),
        ((-1, 1), (-1, 0), "ty", -1),
    ),
    (
        ((2, 1), (1, 1), "tx", -1),
        ((2, -1), (-1, -1), "tx", 1),
        ((0, 2), (0, -1), "ty", 1),
        ((-1, 2), (-1, 1), "ty", -1),
    ),
    (
        ((2, 2), (2, 1), "ty", -1),
        ((1, 2), (1, -1), "ty", 1),
        ((2, 0), (1, 0), "tx", -1),
    ),
)
HOPS = {hop[0]: hop for hops in ROUNDS for hop in hops}
PLACES = [(0, 0)] + list(HOPS)
SUMS = (
    ((2, 2), (2, -1), (1, 2), (2, 0)),
    ((0, 2), (-1, 2)),
    ((2, 1),),
    ((-1, -1), (1, -1)),
    ((1, 1), (-1, 1)),
    ((1, 0), (0, -1)),
    ((-1, 0), (0, 1)),
)
AFTER = {(0, 2): (1, 2), (-1, 2): (2, 2), (1, -1): (0, 2)}


def shift(block, axis, step):
    count = lax.axis_size(axis)
    return lax.ppermute(block, axis, [(i, (i + step) % count) for i in range(count)])


def dot(a, b, dims=((1,), (0,))):
    return lax.dot_general(a, b, (dims, ((), ())), preferred_element_type=jnp.float32)


def call(kernel, table, args, specs, outs, flops, scratch=()):
    held = sum(math.prod(s.block_shape) for s in specs)
    return pl.pallas_call(
        kernel,
        out_shape=[jax.ShapeDtypeStruct(s, d) for s, d in outs],
        grid_spec=pltpu.PrefetchScalarGridSpec(
            num_scalar_prefetch=1,
            grid=(1,),
            in_specs=specs,
            out_specs=[whole(s) for s, _ in outs],
            scratch_shapes=scratch,
        ),
        compiler_params=pltpu.CompilerParams(vmem_limit_bytes=VMEM_BYTES),
        cost_estimate=pl.CostEstimate(flops=flops, bytes_accessed=4 * held, transcendentals=0),
    )(table, *args)


def whole(shape):
    return pl.BlockSpec(shape, lambda i, t: (0,) * len(shape))


def accumulate_kernel(count, first, last, width, table, *refs):
    refs = list(refs)
    take = lambda n: [refs.pop(0) for _ in range(n)]
    blocks = take(count)
    weights = [take(4) for _ in range(count)]
    prior = [] if first else take(3)
    tables = take(2) if last else []
    sums = [ref[...] for ref in prior] or [None] * 3
    for block, (gain, wq, wk, wv) in zip(blocks, weights):
        x = block[...].astype(jnp.float32)
        squares = x * x
        total = squares[:, :128]
        for j in range(1, x.shape[1] // 128):
            total = total + squares[:, j * 128 : (j + 1) * 128]
        scaled = (x * gain[...]).astype(jnp.bfloat16)
        kv_weights = jnp.concatenate([wk[...], wv[...]], axis=0)
        terms = (dot(scaled, wq[...]), dot(scaled, kv_weights, ((1,), (1,))), total)
        sums = [t if s is None else s + t for s, t in zip(sums, terms)]
    if not last:
        for ref, value in zip(refs, sums):
            ref[...] = value
        return
    cosine, sine = tables
    q, kv = refs
    row = lax.rsqrt(jnp.sum(sums[2], axis=1, keepdims=True) / width + EPS)
    kv[...] = (sums[1] * row).astype(jnp.bfloat16)
    for h in range(sums[0].shape[1] // HD):
        one = sums[0][:, h * HD : (h + 1) * HD] * row
        turned = one * cosine[...] + pltpu.roll(one, HD // 2, 1) * sine[...]
        q[:, h * HD : (h + 1) * HD] = turned.astype(jnp.bfloat16)


def accumulate(blocks, table, gain, wq, wk, wv, prior=None, tables=None):
    places, blocks = [PLACES.index(p) for p in blocks], list(blocks.values())
    count = len(blocks)
    rows, depth = blocks[0].shape
    heads, narrow = wq.shape[1], 2 * wk.shape[0]
    args = list(blocks)
    specs = [whole(b.shape) for b in blocks]
    for k in places:
        args += [gain, wq, wk, wv]
        specs += [
            pl.BlockSpec((1, depth), lambda i, t, k=k: (0, t[k])),
            pl.BlockSpec((depth, heads), lambda i, t, k=k: (t[k], 0)),
            pl.BlockSpec((narrow // 2, depth), lambda i, t, k=k: (0, t[k])),
            pl.BlockSpec((narrow // 2, depth), lambda i, t, k=k: (0, t[k])),
        ]
    for group in (prior, tables):
        if group is not None:
            args += list(group)
            specs += [whole(a.shape) for a in group]
    sums = [(rows, heads), (rows, narrow), (rows, 128)]
    if tables is None:
        outs = [(s, jnp.float32) for s in sums]
    else:
        outs = [(s, jnp.bfloat16) for s in sums[:2]]
    kernel = functools.partial(
        accumulate_kernel, count, prior is None, tables is not None, gain.shape[1]
    )
    return call(kernel, table, args, specs, outs, COST * rows * depth * count * (heads + narrow))


def attend_kernel(place, q, own, right, two, left, cosine, sine, out):
    rows = q.shape[0]
    half = rows // 2
    part = own.shape[1] // 2
    line = lax.broadcasted_iota(jnp.int32, (2 * part, 2 * HD), 0)
    column = lax.broadcasted_iota(jnp.int32, (2 * part, 2 * HD), 1)
    home = jnp.where(line < part, line, line - part + HD)
    both = jnp.zeros((rows, 2 * HD), jnp.float32)
    for d, piece in enumerate((own, right, two, left)):
        at = lax.rem(place[len(PLACES)] + d, SIDE) * part
        both += dot(piece[...], (column == home + at).astype(jnp.bfloat16))
    raw = both[:, :HD]
    keys = (raw * cosine[...] + pltpu.roll(raw, HD // 2, 1) * sine[...]).astype(jnp.bfloat16)
    values = both[:, HD:].astype(jnp.bfloat16)
    seen = lax.broadcasted_iota(jnp.int32, (half, half), 0) >= lax.broadcasted_iota(
        jnp.int32, (half, half), 1
    )
    for i in range(2):
        for h in range(q.shape[1] // HD):
            head = slice(h * HD, (h + 1) * HD)
            mine = q[i * half : (i + 1) * half, head]
            scores = []
            for j in range(i + 1):
                some = dot(mine, keys[j * half : (j + 1) * half], ((1,), (1,)))
                some = some * (1.0 / math.sqrt(HD))
                scores.append(jnp.where(seen, some, jnp.float32(-1e30)) if j == i else some)
            scores = jnp.concatenate(scores, axis=1)
            weights = jnp.exp(scores - jnp.max(scores, axis=1, keepdims=True))
            probs = weights * (1.0 / jnp.sum(weights, axis=1, keepdims=True))
            context = dot(probs.astype(jnp.bfloat16), values[: (i + 1) * half])
            out[i * half : (i + 1) * half, head] = context.astype(jnp.bfloat16)


def attend(place, q, parts, cosine, sine):
    args = [q, *parts, cosine, sine]
    specs = [whole(a.shape) for a in args]
    outs = [(q.shape, jnp.bfloat16)]
    return call(attend_kernel, place, args, specs, outs, 8 * q.shape[0] ** 2 * HD)[0]


def project_kernel(counts, base, table, context, *refs):
    refs = list(refs)
    take = lambda n: [refs.pop(0) for _ in range(n)]
    weights = take(len(counts))
    arrived = [take(n) for n in counts]
    residual = take(1) if base else []
    for weight, terms, out in zip(weights, arrived, refs):
        value = dot(context[...], weight[...])
        for term in terms + residual:
            value = value + term[...].astype(jnp.float32)
        out[...] = value.astype(out.dtype)


def project(context, wo, table, places, arrived, base=None):
    rows, depth = context.shape
    width = wo.shape[1] // SIDE**2
    args, specs = [context], [whole(context.shape)]
    for k in (PLACES.index(p) for p in places):
        args.append(wo)
        specs.append(pl.BlockSpec((depth, width), lambda i, t, k=k: (0, t[k])))
    more = [a for terms in arrived for a in terms] + ([] if base is None else [base])
    args += more
    specs += [whole(a.shape) for a in more]
    outs = [((rows, width), jnp.bfloat16)] * len(arrived)
    kernel = functools.partial(project_kernel, [len(t) for t in arrived], base is not None)
    return call(kernel, table, args, specs, outs, 2 * rows * depth * width * len(arrived))


def on_device(tokens, norm_gain, w_query, w_key, w_value, w_output):
    own = tokens[0]
    rows = own.shape[0]
    y, x = lax.axis_index("ty"), lax.axis_index("tx")
    wq, wk, wv, wo = w_query[0], w_key[0].T, w_value[0].T, w_output[0]

    freq = np.exp(np.arange(HD // 2) * (-2.0 * math.log(500000.0) / HD)).astype(np.float32)
    angle = np.arange(rows, dtype=np.float32)[:, None] * freq[None, :]
    cosine = np.concatenate([np.cos(angle)] * 2, axis=1)
    sine = np.concatenate([-np.sin(angle), np.sin(angle)], axis=1)

    dx = jnp.array([p[0] + SIDE for p in PLACES], jnp.int32)
    dy = jnp.array([p[1] + SIDE for p in PLACES], jnp.int32)
    owners = (y + dy) % SIDE * SIDE + (x + dx) % SIDE
    owners = jnp.concatenate([owners.astype(jnp.int32), x.astype(jnp.int32)[None]])

    common = (norm_gain, wq, wk, wv)
    held = {(0, 0): own}
    sums, group = None, [(0, 0)]
    for i, hops in enumerate(ROUNDS):
        for place, source, axis, step in hops:
            held[place] = shift(held[source], axis, step)
        group = group + [hop[0] for hop in hops]
        last = i == len(ROUNDS) - 1
        sums = accumulate(
            {p: held[p] for p in group},
            owners,
            *common,
            prior=sums,
            tables=(cosine, sine) if last else None,
        )
        group = []
    queries, kv = sums
    parts = [kv, shift(kv, "tx", -1), shift(kv, "tx", 2), shift(kv, "tx", 1)]
    context = attend(owners, queries, parts, cosine, sine)

    run = functools.partial(project, context, wo, owners)
    landed = {}
    terms = lambda place: [landed[p] for p in HOPS if HOPS[p][1] == place]
    for places in SUMS:
        for place, block in zip(places, run(places, [terms(p) for p in places])):
            _, _, axis, step = HOPS[place]
            if place in AFTER:
                earlier = AFTER[place]
                block, landed[earlier] = lax.optimization_barrier((block, landed[earlier]))
            landed[place] = shift(block, axis, -step)
    merged = run([(0, 0)], [terms((0, 0))], own)[0]
    return shift(merged, "pp", 1).astype(jnp.float32)[None]


def solution(mesh):
    shape = mesh.devices.shape
    grid = Mesh(mesh.devices.reshape(SIDE, shape[0] // SIDE, shape[1]), ("ty", "tx", "pp"))
    tp = ("ty", "tx")
    return jax.shard_map(
        on_device,
        mesh=grid,
        in_specs=(
            P("pp", None, tp),
            P("pp", None),
            P("pp", None, tp),
            P("pp", None, tp),
            P("pp", None, tp),
            P("pp", tp, None),
        ),
        out_specs=P("pp", None, tp),
        check_vma=False,
    )
```

time: 258 us -> 150 us (0.58)
  waiting for transfers between devices: 177 us -> 76.3 us
  starting transfers between devices: 6.85 us -> 45.6 us
  local copies, waits for them, and re-layouts: 26.9 us -> 6.11 us
  Pallas kernels: 0 us -> 19.8 us
  matrix products: 15.3 us -> 0 us
  other arithmetic: 15.7 us -> 1.86 us
  between operations: 13.6 us -> 0.24 us
    reduce_scatter x1 -> x0, waiting for transfers between devices: 88.7 us -> none  [on_device(): lax.psum_scatter(dequantize(quant, scale, BLOCK).astype(jnp.bfloat16), 't...]
    all_gather x1 -> x0, waiting for transfers between devices: 73.8 us -> none  [on_device(): whole = lax.all_gather(tokens[0], 'tp', axis=1, tiled=True)]
    ppermute x6 -> x34, waiting for transfers between devices: 14.2 us -> 76.3 us  [shift(): lax.ppermute(block, axis, [(i, (i + step) % count) for i in range(count)])]
    ppermute x6 -> x34, starting transfers between devices: 6.81 us -> 45.6 us  [shift(): lax.ppermute(block, axis, [(i, (i + step) % count) for i in range(count)])]
    pallas_call x0 -> x13, Pallas kernels: none -> 19.8 us  [call(): pl.pallas_call(kernel, out_shape=[jax.ShapeDtypeStruct(s, d) for s, d in...]
    dot_general x5 -> x0, matrix products: 14.3 us -> none  [the longest x1 5.04 us: on_device(): jnp.dot(context, w_output[0], preferred_element_type=jnp.float32)]
    dot_general x2 -> x0, local copies, waits for them, and re-layouts: 12.9 us -> none  [the longest x1 6.45 us: on_device(): jnp.dot(normed, w_query[0], preferred_element_type=jnp.float32)]
    convert_element_type x1 -> x0, local copies, waits for them, and re-layouts: 12 us -> none  [on_device(): dequantize(quant, scale, BLOCK).astype(jnp.bfloat16)]
  transfers between devices with their start and end apart: 8 -> 34, of which waited for: 6 -> 18; matrix products, arithmetic and copies ran while one was open for 8% -> 1% of each run, Pallas kernels for 0% -> 8%
where the time goes in v2:
time: 150 us
  waiting for transfers between devices  76.3 us (51%)
  starting transfers between devices  45.6 us (30%)
  Pallas kernels  19.8 us (13%)
  local copies, waits for them, and re-layouts  6.11 us (4%)
  other arithmetic  1.86 us (1%)
    ppermute x34, waiting for transfers between devices, shift(): lax.ppermute(block, axis, [(i, (i + step) % count) for i in range(count)])  76.3 us
    ppermute x34, starting transfers between devices, shift(): lax.ppermute(block, axis, [(i, (i + step) % count) for i in range(count)])  45.6 us
    pallas_call x13, Pallas kernels, call(): pl.pallas_call(kernel, out_shape=[jax.ShapeDtypeStruct(s, d) for s, d in...  19.8 us
    unnamed x24, local copies, waits for them, and re-layouts  6.11 us
  transfers between devices with their start and end apart: 34, of which 18 were waited for; matrix products, arithmetic and copies ran while one was open for 1% of the time, Pallas kernels for 8%

profile of v2, /device:TPU:128, one launch (start us, length us, event | category | flops | bytes accessed | tf_op | source)
XLA Modules:
  0.0 149.9 jit_solution(3212508336848233651)
XLA Ops:
  0.0 1.6 %collective-permute-start.8 = (bf16[512,512]{1,0:T(8,128)(2,1)}, bf16[512,512]{1,0:T(8,128)(2,1)S(1)}, u32[]{:S(2)}, u32[]{:S(2)}) collective-permute-start(bf16[512,512]{1,0:T(8,128)(2,1)} %bitcast.77), channel_id=1, source_target_pairs={{0,64},{64,128},{128,192},{192,0},{1,65},{65,129},{129,193},{193,1... | collective-permute-start | bytes 1572872 | tf_op jit(solution)/shard_map/ppermute | solution.py:61
  1.6 1.7 %collective-permute-start = (bf16[512,512]{1,0:T(8,128)(2,1)}, bf16[512,512]{1,0:T(8,128)(2,1)S(1)}, u32[]{:S(2)}, u32[]{:S(2)}) collective-permute-start(bf16[512,512]{1,0:T(8,128)(2,1)} %bitcast.78), channel_id=1, source_target_pairs={{0,192},{64,0},{128,64},{192,128},{1,193},{65,1},{129,65},{193,129... | collective-permute-start | bytes 1572872 | tf_op jit(solution)/shard_map/ppermute | solution.py:61
  3.2 1.5 collective-permute-start.12
  4.7 1.7 %collective-permute-start.4 = (bf16[512,512]{1,0:T(8,128)(2,1)}, bf16[512,512]{1,0:T(8,128)(2,1)S(1)}, u32[]{:S(2)}, u32[]{:S(2)}) collective-permute-start(bf16[512,512]{1,0:T(8,128)(2,1)} %bitcast.80), channel_id=1, source_target_pairs={{0,48},{16,0},{32,16},{48,32},{1,49},{17,1},{33,17},{49,33},{2,50}... | collective-permute-start | bytes 1572872 | tf_op jit(solution)/shard_map/ppermute | solution.py:61
  6.5 8.7 %collective-permute-done.8.refs_3_ = bf16[512,512]{1,0:T(8,128)(2,1)S(1)} collective-permute-done((bf16[512,512]{1,0:T(8,128)(2,1)}, bf16[512,512]{1,0:T(8,128)(2,1)S(1)}, u32[]{:S(2)}, u32[]{:S(2)}) %collective-permute-start.8) | collective-permute-done | bytes 524320 | tf_op jit(solution)/shard_map/ppermute | solution.py:61
  15.1 1.5 collective-permute-start.9
  16.6 1.7 %collective-permute-start.1 = (bf16[512,512]{1,0:T(8,128)(2,1)S(1)}, bf16[512,512]{1,0:T(8,128)(2,1)}, u32[]{:S(2)}, u32[]{:S(2)}) collective-permute-start(bf16[512,512]{1,0:T(8,128)(2,1)S(1)} %collective-permute-done.refs_4_), channel_id=1, source_target_pairs={{0,48},{16,0},{32,16},{48,32},{1,49},{17,1},{33,17},{49,33},{2,50}... | collective-permute-start | bytes 1572872 | tf_op jit(solution)/shard_map/ppermute | solution.py:61
  18.4 2.5 %collective-permute-start.13 = (bf16[512,512]{1,0:T(8,128)(2,1)S(1)}, bf16[512,512]{1,0:T(8,128)(2,1)S(1)}, u32[]{:S(2)}, u32[]{:S(2)}) collective-permute-start(bf16[512,512]{1,0:T(8,128)(2,1)S(1)} %collective-permute-done.12.refs_1_), channel_id=1, source_target_pairs={{0,192},{64,0},{128,64},{192,128},{1,193},{65,1},{129,65},{193,129... | collective-permute-start | bytes 1572872 | tf_op jit(solution)/shard_map/ppermute | solution.py:61
  20.9 0.7 fusion
  21.7 0.7 collective-permute-start.5
  22.3 6.9 %collective-permute-done.9.refs_0_ = bf16[512,512]{1,0:T(8,128)(2,1)S(1)} collective-permute-done((bf16[512,512]{1,0:T(8,128)(2,1)S(1)}, bf16[512,512]{1,0:T(8,128)(2,1)S(1)}, u32[]{:S(2)}, u32[]{:S(2)}) %collective-permute-start.9) | collective-permute-done | bytes 524320 | tf_op jit(solution)/shard_map/ppermute | solution.py:61
  29.2 0.3 collective-permute-start.10
  29.5 3.0 %collective-permute-start.2 = (bf16[512,512]{1,0:T(8,128)(2,1)}, bf16[512,512]{1,0:T(8,128)(2,1)S(1)}, u32[]{:S(2)}, u32[]{:S(2)}) collective-permute-start(bf16[512,512]{1,0:T(8,128)(2,1)} %collective-permute-done.1.refs_1_), channel_id=1, source_target_pairs={{0,48},{16,0},{32,16},{48,32},{1,49},{17,1},{33,17},{49,33},{2,50}... | collective-permute-start | bytes 1572872 | tf_op jit(solution)/shard_map/ppermute | solution.py:61
  32.5 2.3 %collective-permute-start.14 = (bf16[512,512]{1,0:T(8,128)(2,1)S(1)}, bf16[512,512]{1,0:T(8,128)(2,1)S(1)}, u32[]{:S(2)}, u32[]{:S(2)}) collective-permute-start(bf16[512,512]{1,0:T(8,128)(2,1)S(1)} %collective-permute-done.13.refs_3_), channel_id=1, source_target_pairs={{0,192},{64,0},{128,64},{192,128},{1,193},{65,1},{129,65},{193,129... | collective-permute-start | bytes 1572872 | tf_op jit(solution)/shard_map/ppermute | solution.py:61
  34.7 2.2 %copy-done.1 = bf16[1,8192,256]{2,1,0:T(8,128)(2,1)S(1)} copy-done((bf16[1,8192,256]{2,1,0:T(8,128)(2,1)S(1)}, bf16[1,8192,256]{2,1,0:T(8,128)(2,1)}, u32[]{:S(2)}) %copy-start.1) | copy-done | bytes 4194328
  36.9 1.0 copy-done.3
  38.0 1.0 copy-done.5
  39.0 0.8 copy-done.7
  39.8 1.0 copy-done.8
  40.8 2.1 %shard_map.100 = (f32[512,256]{1,0:T(8,128)S(1)}, f32[512,64]{1,0:T(8,128)S(1)}, f32[512,128]{1,0:T(8,128)S(1)}) custom-call(s32[17]{0:T(128)S(1)} %pad_add_fusion.table.place, bf16[512,512]{1,0:T(8,128)(2,1)S(1)} %bitcast.81, bf16[512,512]{1,0:T(8,128)(2,1)S(1)} %collective-permute-done.12.refs_1_, bf16[512,512]{1,0:T(8,128)(2,1)S(1)} %collective-permute-done.4.refs_2_, ...), custom_call_target="tpu_custom_call" | custom-call | flops 6710886400 | bytes 8529920 | tf_op jit(solution)/shard_map/pallas_call | solution.py:70
  42.9 3.2 %collective-permute-done.5.refs_2_ = bf16[512,512]{1,0:T(8,128)(2,1)S(1)} collective-permute-done((bf16[512,512]{1,0:T(8,128)(2,1)S(1)}, bf16[512,512]{1,0:T(8,128)(2,1)S(1)}, u32[]{:S(2)}, u32[]{:S(2)}) %collective-permute-start.5) | collective-permute-done | bytes 524320 | tf_op jit(solution)/shard_map/ppermute | solution.py:61
  46.1 0.8 collective-permute-start.7
  46.9 3.2 %collective-permute-start.3 = (bf16[512,512]{1,0:T(8,128)(2,1)S(1)}, bf16[512,512]{1,0:T(8,128)(2,1)S(1)}, u32[]{:S(2)}, u32[]{:S(2)}) collective-permute-start(bf16[512,512]{1,0:T(8,128)(2,1)S(1)} %collective-permute-done.2.refs_0_), channel_id=1, source_target_pairs={{0,192},{64,0},{128,64},{192,128},{1,193},{65,1},{129,65},{193,129... | collective-permute-start | bytes 1572872 | tf_op jit(solution)/shard_map/ppermute | solution.py:61
  50.1 2.9 %shard_map.101 = (f32[512,256]{1,0:T(8,128)S(1)}, f32[512,64]{1,0:T(8,128)S(1)}, f32[512,128]{1,0:T(8,128)S(1)}) custom-call(s32[17]{0:T(128)S(1)} %pad_add_fusion.table.place, bf16[512,512]{1,0:T(8,128)(2,1)S(1)} %collective-permute-done.9.refs_0_, bf16[512,512]{1,0:T(8,128)(2,1)} %collective-permute-done.1.refs_1_, ...), custom_call_target="tpu_custom_call" | custom-call | flops 5368709120 | bytes 7741440 | tf_op jit(solution)/shard_map/pallas_call | solution.py:70
  53.1 1.8 %shard_map.102 = (f32[512,256]{1,0:T(8,128)S(1)}, f32[512,64]{1,0:T(8,128)S(1)}, f32[512,128]{1,0:T(8,128)S(1)}) custom-call(s32[17]{0:T(128)S(1)} %pad_add_fusion.table.place, bf16[512,512]{1,0:T(8,128)(2,1)S(1)} %collective-permute-done.2.refs_0_, bf16[512,512]{1,0:T(8,128)(2,1)S(1)} %collective-permute-done.10.refs_1_, ...), custom_call_target="tpu_custom_call" | custom-call | flops 5368709120 | bytes 7741440 | tf_op jit(solution)/shard_map/pallas_call | solution.py:70
  54.9 2.2 %collective-permute-done.7.refs_2_ = bf16[512,512]{1,0:T(8,128)(2,1)S(1)} collective-permute-done((bf16[512,512]{1,0:T(8,128)(2,1)S(1)}, bf16[512,512]{1,0:T(8,128)(2,1)S(1)}, u32[]{:S(2)}, u32[]{:S(2)}) %collective-permute-start.7) | collective-permute-done | bytes 524320 | tf_op jit(solution)/shard_map/ppermute | solution.py:61
  57.1 1.8 %collective-permute-done.6.refs_1_ = bf16[512,512]{1,0:T(8,128)(2,1)S(1)} collective-permute-done((bf16[512,512]{1,0:T(8,128)(2,1)S(1)}, bf16[512,512]{1,0:T(8,128)(2,1)S(1)}, u32[]{:S(2)}, u32[]{:S(2)}) %collective-permute-start.6) | collective-permute-done | bytes 524320 | tf_op jit(solution)/shard_map/ppermute | solution.py:61
  58.9 1.7 %shard_map.103 = (bf16[512,256]{1,0:T(8,128)(2,1)S(1)}, bf16[512,64]{1,0:T(8,128)(2,1)S(1)}) custom-call(s32[17]{0:T(128)S(1)} %pad_add_fusion.table.place, bf16[512,512]{1,0:T(8,128)(2,1)S(1)} %collective-permute-done.3.refs_0_, bf16[512,512]{1,0:T(8,128)(2,1)S(1)} %collective-permute-done.6.refs_1_, bf16[512,512]{1,0:T(8,128)(2,1)S(1)} %collective-permute-done.7.refs_2_, ...), custom_call_target="tpu_custom_call" | custom-call | flops 4026531840 | bytes 6559744 | tf_op jit(solution)/shard_map/pallas_call | solution.py:70
  60.6 0.8 collective-permute-start.15
  61.5 2.5 %collective-permute-start.16 = (bf16[512,64]{1,0:T(8,128)(2,1)S(1)}, bf16[512,64]{1,0:T(8,128)(2,1)S(1)}, u32[]{:S(2)}, u32[]{:S(2)}) collective-permute-start(bf16[512,64]{1,0:T(8,128)(2,1)S(1)} %get-tuple-element.46.own), channel_id=1, source_target_pairs={{0,32},{16,48},{32,0},{48,16},{1,33},{17,49},{33,1},{49,17},{2,34}... | collective-permute-start | bytes 196616 | tf_op jit(solution)/shard_map/ppermute | solution.py:61
  64.0 1.7 %collective-permute-done.15.right = bf16[512,64]{1,0:T(8,128)(2,1)S(1)} collective-permute-done((bf16[512,64]{1,0:T(8,128)(2,1)S(1)}, bf16[512,64]{1,0:T(8,128)(2,1)S(1)}, u32[]{:S(2)}, u32[]{:S(2)}) %collective-permute-start.15) | collective-permute-done | bytes 65568 | tf_op jit(solution)/shard_map/ppermute | solution.py:61
  65.7 2.3 %collective-permute-done.16.two = bf16[512,64]{1,0:T(8,128)(2,1)S(1)} collective-permute-done((bf16[512,64]{1,0:T(8,128)(2,1)S(1)}, bf16[512,64]{1,0:T(8,128)(2,1)S(1)}, u32[]{:S(2)}, u32[]{:S(2)}) %collective-permute-start.16) | collective-permute-done | bytes 65568 | tf_op jit(solution)/shard_map/ppermute | solution.py:61
  68.0 2.2 %collective-permute-done.17.left = bf16[512,64]{1,0:T(8,128)(2,1)S(1)} collective-permute-done((bf16[512,64]{1,0:T(8,128)(2,1)S(1)}, bf16[512,64]{1,0:T(8,128)(2,1)S(1)}, u32[]{:S(2)}, u32[]{:S(2)}) %collective-permute-start.17) | collective-permute-done | bytes 65568 | tf_op jit(solution)/shard_map/ppermute | solution.py:61
  70.2 3.1 %shard_map.104.context = bf16[512,256]{1,0:T(8,128)(2,1)S(1)} custom-call(s32[17]{0:T(128)S(1)} %pad_add_fusion.table.place, bf16[512,256]{1,0:T(8,128)(2,1)S(1)} %get-tuple-element.45.q, bf16[512,64]{1,0:T(8,128)(2,1)S(1)} %get-tuple-element.46.own, bf16[512,64]{1,0:T(8,128)(2,1)S(1)} %collective-permute-done.15.right, ...), custom_call_target="tpu_custom_call" | custom-call | flops 268435456 | bytes 1572864 | tf_op jit(solution)/shard_map/pallas_call | solution.py:70
  73.3 1.3 shard_map.106
  74.5 3.0 %collective-permute-start.25 = (bf16[512,512]{1,0:T(8,128)(2,1)S(1)}, bf16[512,512]{1,0:T(8,128)(2,1)S(1)}, u32[]{:S(2)}, u32[]{:S(2)}) collective-permute-start(bf16[512,512]{1,0:T(8,128)(2,1)S(1)} %get-tuple-element.56), channel_id=1, source_target_pairs={{0,192},{64,0},{128,64},{192,128},{1,193},{65,1},{129,65},{193,129... | collective-permute-start | bytes 1572872 | tf_op jit(solution)/shard_map/ppermute | solution.py:61
  77.6 0.2 collective-permute-start.24
  77.8 1.0 shard_map.105
  78.8 8.7 %collective-permute-done.25.refs_3_ = bf16[512,512]{1,0:T(8,128)(2,1)S(1)} collective-permute-done((bf16[512,512]{1,0:T(8,128)(2,1)S(1)}, bf16[512,512]{1,0:T(8,128)(2,1)S(1)}, u32[]{:S(2)}, u32[]{:S(2)}) %collective-permute-start.25) | collective-permute-done | bytes 524320 | tf_op jit(solution)/shard_map/ppermute | solution.py:61
  87.5 3.7 %collective-permute-start.26 = (bf16[512,512]{1,0:T(8,128)(2,1)S(1)}, bf16[512,512]{1,0:T(8,128)(2,1)S(1)}, u32[]{:S(2)}, u32[]{:S(2)}) collective-permute-start(bf16[512,512]{1,0:T(8,128)(2,1)S(1)} %get-tuple-element.59), channel_id=1, source_target_pairs={{0,192},{64,0},{128,64},{192,128},{1,193},{65,1},{129,65},{193,129... | collective-permute-start | bytes 1572872 | tf_op jit(solution)/shard_map/ppermute | solution.py:61
  91.2 0.8 shard_map.107
  92.0 0.1 collective-permute-start.19
  92.1 0.1 collective-permute-start.20
  92.2 0.8 collective-permute-start.28
  93.0 1.0 shard_map.110
  94.0 2.6 %collective-permute-start.29 = (bf16[512,512]{1,0:T(8,128)(2,1)S(1)}, bf16[512,512]{1,0:T(8,128)(2,1)S(1)}, u32[]{:S(2)}, u32[]{:S(2)}) collective-permute-start(bf16[512,512]{1,0:T(8,128)(2,1)S(1)} %get-tuple-element.62), channel_id=1, source_target_pairs={{0,48},{16,0},{32,16},{48,32},{1,49},{17,1},{33,17},{49,33},{2,50}... | collective-permute-start | bytes 1572872 | tf_op jit(solution)/shard_map/ppermute | solution.py:61
  96.6 5.6 %collective-permute-done.26.refs_5_ = bf16[512,512]{1,0:T(8,128)(2,1)S(1)} collective-permute-done((bf16[512,512]{1,0:T(8,128)(2,1)S(1)}, bf16[512,512]{1,0:T(8,128)(2,1)S(1)}, u32[]{:S(2)}, u32[]{:S(2)}) %collective-permute-start.26) | collective-permute-done | bytes 524320 | tf_op jit(solution)/shard_map/ppermute | solution.py:61
  102.2 3.7 %collective-permute-start.27 = (bf16[512,512]{1,0:T(8,128)(2,1)S(1)}, bf16[512,512]{1,0:T(8,128)(2,1)S(1)}, u32[]{:S(2)}, u32[]{:S(2)}) collective-permute-start(bf16[512,512]{1,0:T(8,128)(2,1)S(1)} %get-tuple-element.60), channel_id=1, source_target_pairs={{0,192},{64,0},{128,64},{192,128},{1,193},{65,1},{129,65},{193,129... | collective-permute-start | bytes 1572872 | tf_op jit(solution)/shard_map/ppermute | solution.py:61
  105.9 0.7 collective-permute-done.19.refs_2_
  106.6 0.3 collective-permute-done.20.refs_3_
  106.9 1.0 shard_map.108
  108.0 1.6 %collective-permute-start.22 = (bf16[512,512]{1,0:T(8,128)(2,1)S(1)}, bf16[512,512]{1,0:T(8,128)(2,1)S(1)}, u32[]{:S(2)}, u32[]{:S(2)}) collective-permute-start(bf16[512,512]{1,0:T(8,128)(2,1)S(1)} %get-tuple-element.52), channel_id=1, source_target_pairs={{0,16},{16,32},{32,48},{48,0},{1,17},{17,33},{33,49},{49,1},{2,18}... | collective-permute-start | bytes 1572872 | tf_op jit(solution)/shard_map/ppermute | solution.py:61
  109.6 8.3 %collective-permute-done.28.refs_3_ = bf16[512,512]{1,0:T(8,128)(2,1)S(1)} collective-permute-done((bf16[512,512]{1,0:T(8,128)(2,1)S(1)}, bf16[512,512]{1,0:T(8,128)(2,1)S(1)}, u32[]{:S(2)}, u32[]{:S(2)}) %collective-permute-start.28) | collective-permute-done | bytes 524320 | tf_op jit(solution)/shard_map/ppermute | solution.py:61
  117.9 1.1 shard_map.111
  119.1 2.4 %collective-permute-start.31 = (bf16[512,512]{1,0:T(8,128)(2,1)S(1)}, bf16[512,512]{1,0:T(8,128)(2,1)S(1)}, u32[]{:S(2)}, u32[]{:S(2)}) collective-permute-start(bf16[512,512]{1,0:T(8,128)(2,1)S(1)} %get-tuple-element.65), channel_id=1, source_target_pairs={{0,192},{64,0},{128,64},{192,128},{1,193},{65,1},{129,65},{193,129... | collective-permute-start | bytes 1572872 | tf_op jit(solution)/shard_map/ppermute | solution.py:61
  121.5 3.5 %collective-permute-done.22.refs_3_ = bf16[512,512]{1,0:T(8,128)(2,1)S(1)} collective-permute-done((bf16[512,512]{1,0:T(8,128)(2,1)S(1)}, bf16[512,512]{1,0:T(8,128)(2,1)S(1)}, u32[]{:S(2)}, u32[]{:S(2)}) %collective-permute-start.22) | collective-permute-done | bytes 524320 | tf_op jit(solution)/shard_map/ppermute | solution.py:61
  125.0 1.0 shard_map.109
  126.0 1.5 collective-permute-start.23
  127.4 3.1 %collective-permute-done.30.refs_2_ = bf16[512,512]{1,0:T(8,128)(2,1)S(1)} collective-permute-done((bf16[512,512]{1,0:T(8,128)(2,1)S(1)}, bf16[512,512]{1,0:T(8,128)(2,1)S(1)}, u32[]{:S(2)}, u32[]{:S(2)}) %collective-permute-start.30) | collective-permute-done | bytes 524320 | tf_op jit(solution)/shard_map/ppermute | solution.py:61
  130.6 4.6 %collective-permute-done.23.refs_1_ = bf16[512,512]{1,0:T(8,128)(2,1)S(1)} collective-permute-done((bf16[512,512]{1,0:T(8,128)(2,1)S(1)}, bf16[512,512]{1,0:T(8,128)(2,1)S(1)}, u32[]{:S(2)}, u32[]{:S(2)}) %collective-permute-start.23) | collective-permute-done | bytes 524320 | tf_op jit(solution)/shard_map/ppermute | solution.py:61
  135.2 2.6 %collective-permute-done.32.refs_4_ = bf16[512,512]{1,0:T(8,128)(2,1)S(1)} collective-permute-done((bf16[512,512]{1,0:T(8,128)(2,1)S(1)}, bf16[512,512]{1,0:T(8,128)(2,1)S(1)}, u32[]{:S(2)}, u32[]{:S(2)}) %collective-permute-start.32) | collective-permute-done | bytes 524320 | tf_op jit(solution)/shard_map/ppermute | solution.py:61
  137.8 1.1 shard_map.112
  138.9 9.8 %collective-permute-done.33 = bf16[512,512]{1,0:T(8,128)(2,1)S(1)} collective-permute-done((bf16[512,512]{1,0:T(8,128)(2,1)S(1)}, bf16[512,512]{1,0:T(8,128)(2,1)S(1)}, u32[]{:S(2)}, u32[]{:S(2)}) %collective-permute-start.33) | collective-permute-done | bytes 524320 | tf_op jit(solution)/shard_map/ppermute | solution.py:61
  148.8 1.1 bitcast_convert_fusion
  (44 shorter events, 0.4 us)
Async XLA Ops:
  0.0 15.1 %collective-permute-start.8 = (bf16[512,512]{1,0:T(8,128)(2,1)}, bf16[512,512]{1,0:T(8,128)(2,1)S(1)}, u32[]{:S(2)}, u32[]{:S(2)}) collective-permute-start(bf16[512,512]{1,0:T(8,128)(2,1)} %bitcast.77), channel_id=1, source_target_pairs={{0,64},{64,128},{128,192},{192,0},{1,65},{65,129},{129,193},{193,1... | collective-permute-start | bytes 1572872 | tf_op jit(solution)/shard_map/ppermute | solution.py:61
  1.6 15.1 %collective-permute-start = (bf16[512,512]{1,0:T(8,128)(2,1)}, bf16[512,512]{1,0:T(8,128)(2,1)S(1)}, u32[]{:S(2)}, u32[]{:S(2)}) collective-permute-start(bf16[512,512]{1,0:T(8,128)(2,1)} %bitcast.78), channel_id=1, source_target_pairs={{0,192},{64,0},{128,64},{192,128},{1,193},{65,1},{129,65},{193,129... | collective-permute-start | bytes 1572872 | tf_op jit(solution)/shard_map/ppermute | solution.py:61
  3.2 15.2 %collective-permute-start.12 = (bf16[512,512]{1,0:T(8,128)(2,1)}, bf16[512,512]{1,0:T(8,128)(2,1)S(1)}, u32[]{:S(2)}, u32[]{:S(2)}) collective-permute-start(bf16[512,512]{1,0:T(8,128)(2,1)} %bitcast.79), channel_id=1, source_target_pairs={{0,16},{16,32},{32,48},{48,0},{1,17},{17,33},{33,49},{49,1},{2,18}... | collective-permute-start | bytes 1572872 | tf_op jit(solution)/shard_map/ppermute | solution.py:61
  4.7 16.9 %collective-permute-start.4 = (bf16[512,512]{1,0:T(8,128)(2,1)}, bf16[512,512]{1,0:T(8,128)(2,1)S(1)}, u32[]{:S(2)}, u32[]{:S(2)}) collective-permute-start(bf16[512,512]{1,0:T(8,128)(2,1)} %bitcast.80), channel_id=1, source_target_pairs={{0,48},{16,0},{32,16},{48,32},{1,49},{17,1},{33,17},{49,33},{2,50}... | collective-permute-start | bytes 1572872 | tf_op jit(solution)/shard_map/ppermute | solution.py:61
  15.1 14.1 %collective-permute-start.9 = (bf16[512,512]{1,0:T(8,128)(2,1)S(1)}, bf16[512,512]{1,0:T(8,128)(2,1)S(1)}, u32[]{:S(2)}, u32[]{:S(2)}) collective-permute-start(bf16[512,512]{1,0:T(8,128)(2,1)S(1)} %collective-permute-done.8.refs_3_), channel_id=1, source_target_pairs={{0,16},{16,32},{32,48},{48,0},{1,17},{17,33},{33,49},{49,1},{2,18}... | collective-permute-start | bytes 1572872 | tf_op jit(solution)/shard_map/ppermute | solution.py:61
  16.6 12.9 %collective-permute-start.1 = (bf16[512,512]{1,0:T(8,128)(2,1)S(1)}, bf16[512,512]{1,0:T(8,128)(2,1)}, u32[]{:S(2)}, u32[]{:S(2)}) collective-permute-start(bf16[512,512]{1,0:T(8,128)(2,1)S(1)} %collective-permute-done.refs_4_), channel_id=1, source_target_pairs={{0,48},{16,0},{32,16},{48,32},{1,49},{17,1},{33,17},{49,33},{2,50}... | collective-permute-start | bytes 1572872 | tf_op jit(solution)/shard_map/ppermute | solution.py:61
  18.4 14.1 %collective-permute-start.13 = (bf16[512,512]{1,0:T(8,128)(2,1)S(1)}, bf16[512,512]{1,0:T(8,128)(2,1)S(1)}, u32[]{:S(2)}, u32[]{:S(2)}) collective-permute-start(bf16[512,512]{1,0:T(8,128)(2,1)S(1)} %collective-permute-done.12.refs_1_), channel_id=1, source_target_pairs={{0,192},{64,0},{128,64},{192,128},{1,193},{65,1},{129,65},{193,129... | collective-permute-start | bytes 1572872 | tf_op jit(solution)/shard_map/ppermute | solution.py:61
  21.6 25.3 %collective-permute-start.11 = (bf16[512,512]{1,0:T(8,128)(2,1)S(1)}, bf16[512,512]{1,0:T(8,128)(2,1)S(1)}, u32[]{:S(2)}, u32[]{:S(2)}) collective-permute-start(bf16[512,512]{1,0:T(8,128)(2,1)S(1)} %collective-permute-done.8.refs_3_), channel_id=1, source_target_pairs={{0,64},{64,128},{128,192},{192,0},{1,65},{65,129},{129,193},{193,1... | collective-permute-start | bytes 1572872 | tf_op jit(solution)/shard_map/ppermute | solution.py:61
  21.7 24.4 %collective-permute-start.5 = (bf16[512,512]{1,0:T(8,128)(2,1)S(1)}, bf16[512,512]{1,0:T(8,128)(2,1)S(1)}, u32[]{:S(2)}, u32[]{:S(2)}) collective-permute-start(bf16[512,512]{1,0:T(8,128)(2,1)S(1)} %collective-permute-done.4.refs_2_), channel_id=1, source_target_pairs={{0,64},{64,128},{128,192},{192,0},{1,65},{65,129},{129,193},{193,1... | collective-permute-start | bytes 1572872 | tf_op jit(solution)/shard_map/ppermute | solution.py:61
  29.2 23.8 %collective-permute-start.10 = (bf16[512,512]{1,0:T(8,128)(2,1)S(1)}, bf16[512,512]{1,0:T(8,128)(2,1)S(1)}, u32[]{:S(2)}, u32[]{:S(2)}) collective-permute-start(bf16[512,512]{1,0:T(8,128)(2,1)S(1)} %collective-permute-done.9.refs_0_), channel_id=1, source_target_pairs={{0,16},{16,32},{32,48},{48,0},{1,17},{17,33},{33,49},{49,1},{2,18}... | collective-permute-start | bytes 1572872 | tf_op jit(solution)/shard_map/ppermute | solution.py:61
  29.5 17.4 %collective-permute-start.2 = (bf16[512,512]{1,0:T(8,128)(2,1)}, bf16[512,512]{1,0:T(8,128)(2,1)S(1)}, u32[]{:S(2)}, u32[]{:S(2)}) collective-permute-start(bf16[512,512]{1,0:T(8,128)(2,1)} %collective-permute-done.1.refs_1_), channel_id=1, source_target_pairs={{0,48},{16,0},{32,16},{48,32},{1,49},{17,1},{33,17},{49,33},{2,50}... | collective-permute-start | bytes 1572872 | tf_op jit(solution)/shard_map/ppermute | solution.py:61
  32.5 20.6 %collective-permute-start.14 = (bf16[512,512]{1,0:T(8,128)(2,1)S(1)}, bf16[512,512]{1,0:T(8,128)(2,1)S(1)}, u32[]{:S(2)}, u32[]{:S(2)}) collective-permute-start(bf16[512,512]{1,0:T(8,128)(2,1)S(1)} %collective-permute-done.13.refs_3_), channel_id=1, source_target_pairs={{0,192},{64,0},{128,64},{192,128},{1,193},{65,1},{129,65},{193,129... | collective-permute-start | bytes 1572872 | tf_op jit(solution)/shard_map/ppermute | solution.py:61
  34.7 2.2 %copy-start.1 = (bf16[1,8192,256]{2,1,0:T(8,128)(2,1)S(1)}, bf16[1,8192,256]{2,1,0:T(8,128)(2,1)}, u32[]{:S(2)}) copy-start(bf16[1,8192,256]{2,1,0:T(8,128)(2,1)} %param.12) | copy-start | bytes 12582916
  36.9 1.0 copy-start.3
  38.0 1.0 copy-start.5
  39.0 0.8 copy-start.7
  39.8 1.0 copy-start.8
  40.8 9.3 %copy-start.2 = (bf16[1,8192,256]{2,1,0:T(8,128)(2,1)S(1)}, bf16[1,8192,256]{2,1,0:T(8,128)(2,1)}, u32[]{:S(2)}) copy-start(bf16[1,8192,256]{2,1,0:T(8,128)(2,1)} %param.12) | copy-start | bytes 12582916
  40.8 9.3 %copy-start.4 = (bf16[1,8192,32]{1,2,0:T(8,128)(2,1)S(1)}, bf16[1,8192,32]{1,2,0:T(8,128)(2,1)}, u32[]{:S(2)}) copy-start(bf16[1,8192,32]{1,2,0:T(8,128)(2,1)} %param.13) | copy-start | bytes 1572868
  40.8 9.3 %copy-start.6 = (bf16[1,8192,32]{1,2,0:T(8,128)(2,1)S(1)}, bf16[1,8192,32]{1,2,0:T(8,128)(2,1)}, u32[]{:S(2)}) copy-start(bf16[1,8192,32]{1,2,0:T(8,128)(2,1)} %param.14) | copy-start | bytes 1572868
  46.1 11.1 %collective-permute-start.7 = (bf16[512,512]{1,0:T(8,128)(2,1)S(1)}, bf16[512,512]{1,0:T(8,128)(2,1)S(1)}, u32[]{:S(2)}, u32[]{:S(2)}) collective-permute-start(bf16[512,512]{1,0:T(8,128)(2,1)S(1)} %collective-permute-done.4.refs_2_), channel_id=1, source_target_pairs={{0,48},{16,0},{32,16},{48,32},{1,49},{17,1},{33,17},{49,33},{2,50}... | collective-permute-start | bytes 1572872 | tf_op jit(solution)/shard_map/ppermute | solution.py:61
  46.9 12.0 %collective-permute-start.6 = (bf16[512,512]{1,0:T(8,128)(2,1)S(1)}, bf16[512,512]{1,0:T(8,128)(2,1)S(1)}, u32[]{:S(2)}, u32[]{:S(2)}) collective-permute-start(bf16[512,512]{1,0:T(8,128)(2,1)S(1)} %collective-permute-done.5.refs_2_), channel_id=1, source_target_pairs={{0,64},{64,128},{128,192},{192,0},{1,65},{65,129},{129,193},{193,1... | collective-permute-start | bytes 1572872 | tf_op jit(solution)/shard_map/ppermute | solution.py:61
  46.9 12.0 %collective-permute-start.3 = (bf16[512,512]{1,0:T(8,128)(2,1)S(1)}, bf16[512,512]{1,0:T(8,128)(2,1)S(1)}, u32[]{:S(2)}, u32[]{:S(2)}) collective-permute-start(bf16[512,512]{1,0:T(8,128)(2,1)S(1)} %collective-permute-done.2.refs_0_), channel_id=1, source_target_pairs={{0,192},{64,0},{128,64},{192,128},{1,193},{65,1},{129,65},{193,129... | collective-permute-start | bytes 1572872 | tf_op jit(solution)/shard_map/ppermute | solution.py:61
  53.0 5.9 %copy-start.10 = (f32[512,128]{1,0:T(8,128)S(1)}, f32[512,128]{1,0:T(8,128)}, u32[]{:S(2)}) copy-start(f32[512,128]{1,0:T(8,128)} %constant.41.clone.refs_18_.cosine) | copy-start | bytes 786436
  53.0 5.8 %copy-start.11 = (f32[512,128]{1,0:T(8,128)S(1)}, f32[512,128]{1,0:T(8,128)}, u32[]{:S(2)}) copy-start(f32[512,128]{1,0:T(8,128)} %constant.42.clone.refs_19_.sine) | copy-start | bytes 786436
  58.9 14.4 %copy-start = (bf16[1,256,8192]{2,1,0:T(8,128)(2,1)S(1)}, bf16[1,256,8192]{2,1,0:T(8,128)(2,1)}, u32[]{:S(2)}) copy-start(bf16[1,256,8192]{2,1,0:T(8,128)(2,1)} %param.15) | copy-start | bytes 12582916
  60.6 5.0 %collective-permute-start.15 = (bf16[512,64]{1,0:T(8,128)(2,1)S(1)}, bf16[512,64]{1,0:T(8,128)(2,1)S(1)}, u32[]{:S(2)}, u32[]{:S(2)}) collective-permute-start(bf16[512,64]{1,0:T(8,128)(2,1)S(1)} %get-tuple-element.46.own), channel_id=1, source_target_pairs={{0,48},{16,0},{32,16},{48,32},{1,49},{17,1},{33,17},{49,33},{2,50}... | collective-permute-start | bytes 196616 | tf_op jit(solution)/shard_map/ppermute | solution.py:61
  61.5 6.5 %collective-permute-start.16 = (bf16[512,64]{1,0:T(8,128)(2,1)S(1)}, bf16[512,64]{1,0:T(8,128)(2,1)S(1)}, u32[]{:S(2)}, u32[]{:S(2)}) collective-permute-start(bf16[512,64]{1,0:T(8,128)(2,1)S(1)} %get-tuple-element.46.own), channel_id=1, source_target_pairs={{0,32},{16,48},{32,0},{48,16},{1,33},{17,49},{33,1},{49,17},{2,34}... | collective-permute-start | bytes 196616 | tf_op jit(solution)/shard_map/ppermute | solution.py:61
  64.0 6.2 %collective-permute-start.17 = (bf16[512,64]{1,0:T(8,128)(2,1)S(1)}, bf16[512,64]{1,0:T(8,128)(2,1)S(1)}, u32[]{:S(2)}, u32[]{:S(2)}) collective-permute-start(bf16[512,64]{1,0:T(8,128)(2,1)S(1)} %get-tuple-element.46.own), channel_id=1, source_target_pairs={{0,16},{16,32},{32,48},{48,0},{1,17},{17,33},{33,49},{49,1},{2,18}... | collective-permute-start | bytes 196616 | tf_op jit(solution)/shard_map/ppermute | solution.py:61
  74.5 13.0 %collective-permute-start.25 = (bf16[512,512]{1,0:T(8,128)(2,1)S(1)}, bf16[512,512]{1,0:T(8,128)(2,1)S(1)}, u32[]{:S(2)}, u32[]{:S(2)}) collective-permute-start(bf16[512,512]{1,0:T(8,128)(2,1)S(1)} %get-tuple-element.56), channel_id=1, source_target_pairs={{0,192},{64,0},{128,64},{192,128},{1,193},{65,1},{129,65},{193,129... | collective-permute-start | bytes 1572872 | tf_op jit(solution)/shard_map/ppermute | solution.py:61
  77.6 13.6 %collective-permute-start.18 = (bf16[512,512]{1,0:T(8,128)(2,1)S(1)}, bf16[512,512]{1,0:T(8,128)(2,1)S(1)}, u32[]{:S(2)}, u32[]{:S(2)}) collective-permute-start(bf16[512,512]{1,0:T(8,128)(2,1)S(1)} %get-tuple-element.48), channel_id=1, source_target_pairs={{0,64},{64,128},{128,192},{192,0},{1,65},{65,129},{129,193},{193,1... | collective-permute-start | bytes 1572872 | tf_op jit(solution)/shard_map/ppermute | solution.py:61
  77.6 15.5 %collective-permute-start.24 = (bf16[512,512]{1,0:T(8,128)(2,1)S(1)}, bf16[512,512]{1,0:T(8,128)(2,1)S(1)}, u32[]{:S(2)}, u32[]{:S(2)}) collective-permute-start(bf16[512,512]{1,0:T(8,128)(2,1)S(1)} %get-tuple-element.54), channel_id=1, source_target_pairs={{0,48},{16,0},{32,16},{48,32},{1,49},{17,1},{33,17},{49,33},{2,50}... | collective-permute-start | bytes 1572872 | tf_op jit(solution)/shard_map/ppermute | solution.py:61
  87.5 14.7 %collective-permute-start.26 = (bf16[512,512]{1,0:T(8,128)(2,1)S(1)}, bf16[512,512]{1,0:T(8,128)(2,1)S(1)}, u32[]{:S(2)}, u32[]{:S(2)}) collective-permute-start(bf16[512,512]{1,0:T(8,128)(2,1)S(1)} %get-tuple-element.59), channel_id=1, source_target_pairs={{0,192},{64,0},{128,64},{192,128},{1,193},{65,1},{129,65},{193,129... | collective-permute-start | bytes 1572872 | tf_op jit(solution)/shard_map/ppermute | solution.py:61
  92.0 14.6 %collective-permute-start.19 = (bf16[512,512]{1,0:T(8,128)(2,1)S(1)}, bf16[512,512]{1,0:T(8,128)(2,1)S(1)}, u32[]{:S(2)}, u32[]{:S(2)}) collective-permute-start(bf16[512,512]{1,0:T(8,128)(2,1)S(1)} %shard_map.107), channel_id=1, source_target_pairs={{0,16},{16,32},{32,48},{48,0},{1,17},{17,33},{33,49},{49,1},{2,18}... | collective-permute-start | bytes 1572872 | tf_op jit(solution)/shard_map/ppermute | solution.py:61
  92.1 14.8 %collective-permute-start.20 = (bf16[512,512]{1,0:T(8,128)(2,1)S(1)}, bf16[512,512]{1,0:T(8,128)(2,1)S(1)}, u32[]{:S(2)}, u32[]{:S(2)}) collective-permute-start(bf16[512,512]{1,0:T(8,128)(2,1)S(1)} %get-tuple-element.50), channel_id=1, source_target_pairs={{0,64},{64,128},{128,192},{192,0},{1,65},{65,129},{129,193},{193,1... | collective-permute-start | bytes 1572872 | tf_op jit(solution)/shard_map/ppermute | solution.py:61
  92.2 25.6 %collective-permute-start.28 = (bf16[512,512]{1,0:T(8,128)(2,1)S(1)}, bf16[512,512]{1,0:T(8,128)(2,1)S(1)}, u32[]{:S(2)}, u32[]{:S(2)}) collective-permute-start(bf16[512,512]{1,0:T(8,128)(2,1)S(1)} %get-tuple-element.61), channel_id=1, source_target_pairs={{0,16},{16,32},{32,48},{48,0},{1,17},{17,33},{33,49},{49,1},{2,18}... | collective-permute-start | bytes 1572872 | tf_op jit(solution)/shard_map/ppermute | solution.py:61
  94.0 23.8 %collective-permute-start.29 = (bf16[512,512]{1,0:T(8,128)(2,1)S(1)}, bf16[512,512]{1,0:T(8,128)(2,1)S(1)}, u32[]{:S(2)}, u32[]{:S(2)}) collective-permute-start(bf16[512,512]{1,0:T(8,128)(2,1)S(1)} %get-tuple-element.62), channel_id=1, source_target_pairs={{0,48},{16,0},{32,16},{48,32},{1,49},{17,1},{33,17},{49,33},{2,50}... | collective-permute-start | bytes 1572872 | tf_op jit(solution)/shard_map/ppermute | solution.py:61
  102.2 15.6 %collective-permute-start.27 = (bf16[512,512]{1,0:T(8,128)(2,1)S(1)}, bf16[512,512]{1,0:T(8,128)(2,1)S(1)}, u32[]{:S(2)}, u32[]{:S(2)}) collective-permute-start(bf16[512,512]{1,0:T(8,128)(2,1)S(1)} %get-tuple-element.60), channel_id=1, source_target_pairs={{0,192},{64,0},{128,64},{192,128},{1,193},{65,1},{129,65},{193,129... | collective-permute-start | bytes 1572872 | tf_op jit(solution)/shard_map/ppermute | solution.py:61
  107.9 13.6 %collective-permute-start.21 = (bf16[512,512]{1,0:T(8,128)(2,1)S(1)}, bf16[512,512]{1,0:T(8,128)(2,1)S(1)}, u32[]{:S(2)}, u32[]{:S(2)}) collective-permute-start(bf16[512,512]{1,0:T(8,128)(2,1)S(1)} %get-tuple-element.51), channel_id=1, source_target_pairs={{0,64},{64,128},{128,192},{192,0},{1,65},{65,129},{129,193},{193,1... | collective-permute-start | bytes 1572872 | tf_op jit(solution)/shard_map/ppermute | solution.py:61
  108.0 17.0 %collective-permute-start.22 = (bf16[512,512]{1,0:T(8,128)(2,1)S(1)}, bf16[512,512]{1,0:T(8,128)(2,1)S(1)}, u32[]{:S(2)}, u32[]{:S(2)}) collective-permute-start(bf16[512,512]{1,0:T(8,128)(2,1)S(1)} %get-tuple-element.52), channel_id=1, source_target_pairs={{0,16},{16,32},{32,48},{48,0},{1,17},{17,33},{33,49},{49,1},{2,18}... | collective-permute-start | bytes 1572872 | tf_op jit(solution)/shard_map/ppermute | solution.py:61
  119.0 11.6 %collective-permute-start.30 = (bf16[512,512]{1,0:T(8,128)(2,1)S(1)}, bf16[512,512]{1,0:T(8,128)(2,1)S(1)}, u32[]{:S(2)}, u32[]{:S(2)}) collective-permute-start(bf16[512,512]{1,0:T(8,128)(2,1)S(1)} %get-tuple-element.64), channel_id=1, source_target_pairs={{0,16},{16,32},{32,48},{48,0},{1,17},{17,33},{33,49},{49,1},{2,18}... | collective-permute-start | bytes 1572872 | tf_op jit(solution)/shard_map/ppermute | solution.py:61
  119.1 18.8 %copy-start.9 = (bf16[1,512,512]{2,1,0:T(8,128)(2,1)S(1)}, bf16[1,512,512]{2,1,0:T(8,128)(2,1)}, u32[]{:S(2)}) copy-start(bf16[1,512,512]{2,1,0:T(8,128)(2,1)} %param.10) | copy-start | bytes 1572868
  119.1 11.5 %collective-permute-start.31 = (bf16[512,512]{1,0:T(8,128)(2,1)S(1)}, bf16[512,512]{1,0:T(8,128)(2,1)S(1)}, u32[]{:S(2)}, u32[]{:S(2)}) collective-permute-start(bf16[512,512]{1,0:T(8,128)(2,1)S(1)} %get-tuple-element.65), channel_id=1, source_target_pairs={{0,192},{64,0},{128,64},{192,128},{1,193},{65,1},{129,65},{193,129... | collective-permute-start | bytes 1572872 | tf_op jit(solution)/shard_map/ppermute | solution.py:61
  126.0 9.3 %collective-permute-start.23 = (bf16[512,512]{1,0:T(8,128)(2,1)S(1)}, bf16[512,512]{1,0:T(8,128)(2,1)S(1)}, u32[]{:S(2)}, u32[]{:S(2)}) collective-permute-start(bf16[512,512]{1,0:T(8,128)(2,1)S(1)} %get-tuple-element.53), channel_id=1, source_target_pairs={{0,48},{16,0},{32,16},{48,32},{1,49},{17,1},{33,17},{49,33},{2,50}... | collective-permute-start | bytes 1572872 | tf_op jit(solution)/shard_map/ppermute | solution.py:61
  127.4 10.4 %collective-permute-start.32 = (bf16[512,512]{1,0:T(8,128)(2,1)S(1)}, bf16[512,512]{1,0:T(8,128)(2,1)S(1)}, u32[]{:S(2)}, u32[]{:S(2)}) collective-permute-start(bf16[512,512]{1,0:T(8,128)(2,1)S(1)} %get-tuple-element.66), channel_id=1, source_target_pairs={{0,64},{64,128},{128,192},{192,0},{1,65},{65,129},{129,193},{193,1... | collective-permute-start | bytes 1572872 | tf_op jit(solution)/shard_map/ppermute | solution.py:61
  138.9 9.8 %collective-permute-start.33 = (bf16[512,512]{1,0:T(8,128)(2,1)S(1)}, bf16[512,512]{1,0:T(8,128)(2,1)S(1)}, u32[]{:S(2)}, u32[]{:S(2)}) collective-permute-start(bf16[512,512]{1,0:T(8,128)(2,1)S(1)} %shard_map.112), channel_id=1, source_target_pairs={{0,1},{1,2},{2,3},{3,4},{4,5},{5,6},{6,7},{7,8},{8,9},{9,10},{10,1... | collective-permute-start | bytes 1572872 | tf_op jit(solution)/shard_map/ppermute | solution.py:61

commit v3 on v2

v3 whole, which is shorter than its diff:
```python
import functools
import math

import jax
import jax.numpy as jnp
import numpy as np
from jax import lax
from jax.experimental import pallas as pl
from jax.experimental.pallas import tpu as pltpu
from jax.sharding import Mesh
from jax.sharding import PartitionSpec as P

KVH = 4
HD = 128
SIDE = 4
SECTIONS = 16
EPS = 1e-05
COST = 16
VMEM_BYTES = 20 * 2**20

OFFSETS = (0, -1, 1, 2)


def route(axis_of_core, step):
    pairs = []
    for y in range(SIDE):
        for x in range(SIDE):
            for p in range(SECTIONS):
                along_x = axis_of_core[p % 2] == "tx"
                to_y = y if along_x else (y + step) % SIDE
                to_x = (x + step) % SIDE if along_x else x
                pairs.append(((y * SIDE + x) * SECTIONS + p, (to_y * SIDE + to_x) * SECTIONS + p))
    return pairs


def shift(block, axis_of_core, step):
    return lax.ppermute(block, ("ty", "tx", "pp"), route(axis_of_core, step))


SHORT = ("tx", "ty")
LONG = ("ty", "tx")
ROW = ("tx", "tx")


def dot(a, b, dims=((1,), (0,))):
    return lax.dot_general(a, b, (dims, ((), ())), preferred_element_type=jnp.float32)


def call(kernel, table, args, specs, outs, flops, scratch=()):
    held = sum(math.prod(s.block_shape) for s in specs)
    return pl.pallas_call(
        kernel,
        out_shape=[jax.ShapeDtypeStruct(s, d) for s, d in outs],
        grid_spec=pltpu.PrefetchScalarGridSpec(
            num_scalar_prefetch=1,
            grid=(1,),
            in_specs=specs,
            out_specs=[whole(s) for s, _ in outs],
            scratch_shapes=scratch,
        ),
        compiler_params=pltpu.CompilerParams(vmem_limit_bytes=VMEM_BYTES),
        cost_estimate=pl.CostEstimate(flops=flops, bytes_accessed=4 * held, transcendentals=0),
    )(table, *args)


def whole(shape):
    return pl.BlockSpec(shape, lambda i, t: (0,) * len(shape))


def accumulate_kernel(stacks, part, n_prior, n_extra, width, table, *refs):
    refs = list(refs)
    take = lambda n: [refs.pop(0) for _ in range(n)]
    blocks = []
    for ref, parts in zip(take(len(stacks)), stacks):
        rows = ref.shape[0] // parts
        blocks += [ref.at[pl.ds(n * rows, rows)] for n in range(parts)]
    weights = [take(2 if part == "q" else 4 if part == "all" else 3) for _ in blocks]
    prior, extra = take(n_prior), take(n_extra)
    sums = [ref[...] for ref in prior] or [None] * 3
    for block, (gain, *columns) in zip(blocks, weights):
        x = block[...].astype(jnp.float32)
        scaled = (x * gain[...]).astype(jnp.bfloat16)
        terms = []
        if part != "kv":
            terms.append(dot(scaled, columns[0][...]))
        if part != "q":
            kv_weights = jnp.concatenate([w[...] for w in columns[-2:]], axis=0)
            terms.append(dot(scaled, kv_weights, ((1,), (1,))))
            squares = x * x
            total = squares[:, :128]
            for j in range(1, x.shape[1] // 128):
                total = total + squares[:, j * 128 : (j + 1) * 128]
            terms.append(total)
        sums = [t if s is None else s + t for s, t in zip(sums, terms)]
    if part == "all":
        for ref, value in zip(refs, sums):
            ref[...] = value
    elif part == "kv":
        kv, factor = refs
        row = lax.rsqrt(jnp.sum(sums[1], axis=1, keepdims=True) / width + EPS)
        narrow = kv.shape[0]
        wide = jnp.concatenate([sums[0] * row, jnp.zeros((row.shape[0], HD - narrow), jnp.float32)], axis=1)
        kv[...] = wide.T[:narrow].astype(jnp.bfloat16)
        factor[...] = jnp.broadcast_to(row, factor.shape)
    else:
        factor, cosine, sine = extra
        (q,) = refs
        for h in range(q.shape[1] // HD):
            one = sums[0][:, h * HD : (h + 1) * HD] * factor[...]
            turned = one * cosine[...] + pltpu.roll(one, HD // 2, 1) * sine[...]
            q[:, h * HD : (h + 1) * HD] = turned.astype(jnp.bfloat16)


def accumulate(stacks, places, table, gain, wq, wk, wv, prior=(), extra=(), part="all"):
    count = len(places)
    depth = wq.shape[0] // SIDE**2
    rows = sum(s.shape[0] for s in stacks) // count
    parts = [s.shape[0] // rows for s in stacks]
    heads, narrow = wq.shape[1], 2 * wk.shape[0]
    args = list(stacks)
    specs = [whole(s.shape) for s in stacks]
    for k in places:
        args.append(gain)
        specs.append(pl.BlockSpec((1, depth), lambda i, t, k=k: (0, t[k])))
        if part != "kv":
            args.append(wq)
            specs.append(pl.BlockSpec((depth, heads), lambda i, t, k=k: (t[k], 0)))
        if part != "q":
            args += [wk, wv]
            specs += [pl.BlockSpec((narrow // 2, depth), lambda i, t, k=k: (0, t[k]))] * 2
    args += [*prior, *extra]
    specs += [whole(a.shape) for a in (*prior, *extra)]
    sums = [(rows, heads), (rows, narrow), (rows, HD)]
    outs = {
        "all": [(s, jnp.float32) for s in sums],
        "kv": [((narrow, rows), jnp.bfloat16), (sums[2], jnp.float32)],
        "q": [(sums[0], jnp.bfloat16)],
    }[part]
    kernel = functools.partial(
        accumulate_kernel, parts, part, len(prior), len(extra), gain.shape[1]
    )
    return call(kernel, table, args, specs, outs, COST * rows * depth * count * (heads + narrow))


def attend_kernel(place, q, own, right, two, left, cosine, sine, out, keys_raw, values):
    rows = q.shape[0]
    half = rows // 2
    part = own.shape[0] // 2
    for d, piece in enumerate((own, right, two, left)):
        at = pl.multiple_of(lax.rem(place[SIDE**2] + d, SIDE) * part, part)
        keys_raw[pl.ds(at, part), :] = piece[:part]
        values[pl.ds(at, part), :] = piece[part:]
    first = keys_raw[: HD // 2].astype(jnp.float32)
    second = keys_raw[HD // 2 :].astype(jnp.float32)
    keys = jnp.concatenate(
        [
            first * cosine[...] - second * sine[...],
            second * cosine[...] + first * sine[...],
        ],
        axis=0,
    ).astype(jnp.bfloat16)
    seen = lax.broadcasted_iota(jnp.int32, (half, half), 0) >= lax.broadcasted_iota(
        jnp.int32, (half, half), 1
    )
    for i in range(2):
        for h in range(q.shape[1] // HD):
            head = slice(h * HD, (h + 1) * HD)
            mine = q[i * half : (i + 1) * half, head]
            scores = []
            for j in range(i + 1):
                some = dot(mine, keys[:, j * half : (j + 1) * half]) * (1.0 / math.sqrt(HD))
                scores.append(jnp.where(seen, some, jnp.float32(-1e30)) if j == i else some)
            scores = jnp.concatenate(scores, axis=1)
            weights = jnp.exp(scores - jnp.max(scores, axis=1, keepdims=True))
            probs = weights * (1.0 / jnp.sum(weights, axis=1, keepdims=True))
            context = dot(probs.astype(jnp.bfloat16), values[:, : (i + 1) * half], ((1,), (1,)))
            out[i * half : (i + 1) * half, head] = context.astype(jnp.bfloat16)


def attend(place, q, parts, cosine, sine):
    args = [q, *parts, cosine, sine]
    specs = [whole(a.shape) for a in args]
    outs = [(q.shape, jnp.bfloat16)]
    scratch = [pltpu.VMEM((HD, q.shape[0]), jnp.bfloat16)] * 2
    return call(attend_kernel, place, args, specs, outs, 8 * q.shape[0] ** 2 * HD, scratch)[0]


def project_kernel(jobs, base, table, context, *refs):
    refs = list(refs)
    take = lambda n: [refs.pop(0) for _ in range(n)]
    weights = [take(len(job["places"])) for job in jobs]
    arrived = [take(len(job["adds"])) for job in jobs]
    residual = take(1) if base else []
    rows = context.shape[0]
    for job, group, terms in zip(jobs, weights, arrived):
        out = None if job["apart"] else refs.pop(0)
        for n, weight in enumerate(group):
            cut = pl.ds(n * rows, rows)
            value = dot(context[...], weight[...])
            for term in terms:
                value = value + term[cut].astype(jnp.float32)
            if not job["apart"]:
                out[cut] = value.astype(out.dtype)
                continue
            if residual:
                value = value + residual.pop()[...].astype(jnp.float32)
            alone = refs.pop(0)
            alone[...] = value.astype(alone.dtype)


def project(context, wo, table, jobs, base=None):
    rows, depth = context.shape
    width = wo.shape[1] // SIDE**2
    args, specs, outs = [context], [whole(context.shape)], []
    for job in jobs:
        for k in job["places"]:
            args.append(wo)
            specs.append(pl.BlockSpec((depth, width), lambda i, t, k=k: (0, t[k])))
        count = len(job["places"])
        if job["apart"]:
            outs += [((rows, width), jnp.bfloat16)] * count
        else:
            outs.append(((rows * count, width), jnp.bfloat16))
    if base is not None:
        outs[0] = (outs[0][0], jnp.float32)
    more = [a for job in jobs for a in job["adds"]] + ([] if base is None else [base])
    args += more
    specs += [whole(a.shape) for a in more]
    kernel = functools.partial(project_kernel, jobs, base is not None)
    count = sum(len(job["places"]) for job in jobs)
    return call(kernel, table, args, specs, outs, 2 * rows * depth * width * count)


def on_device(tokens, norm_gain, w_query, w_key, w_value, w_output):
    own = tokens[0]
    rows = own.shape[0]
    y, x = lax.axis_index("ty"), lax.axis_index("tx")
    wq, wk, wv, wo = w_query[0], w_key[0].T, w_value[0].T, w_output[0]

    freq = np.exp(np.arange(HD // 2) * (-2.0 * math.log(500000.0) / HD)).astype(np.float32)
    angle = np.arange(rows, dtype=np.float32)[:, None] * freq[None, :]
    cosine = np.concatenate([np.cos(angle)] * 2, axis=1)
    sine = np.concatenate([-np.sin(angle), np.sin(angle)], axis=1)

    far = jnp.array([f + SIDE for f in OFFSETS for _ in OFFSETS], jnp.int32)
    near = jnp.array([n + SIDE for _ in OFFSETS for n in OFFSETS], jnp.int32)
    x_first = lax.rem(lax.axis_index("pp"), 2) == 0
    owners = (y + jnp.where(x_first, far, near)) % SIDE * SIDE
    owners += (x + jnp.where(x_first, near, far)) % SIDE
    owners = jnp.concatenate([owners.astype(jnp.int32), x.astype(jnp.int32)[None]])
    spots = lambda far, *nears: [SIDE * OFFSETS.index(far) + OFFSETS.index(n) for n in nears]
    one, two = (0, -1), (1, 2)

    common = (owners, norm_gain, wq, wk, wv)
    behind, ahead, opposite = (shift(own, SHORT, -d) for d in OFFSETS[1:])
    first = jnp.concatenate([own, behind])
    first_up, first_down = shift(first, LONG, 1), shift(first, LONG, -1)
    second = jnp.concatenate([ahead, opposite])
    second_up, second_down = shift(second, LONG, 1), shift(second, LONG, -1)
    first_far, second_far = shift(first_up, LONG, 1), shift(second_down, LONG, -1)
    sums = accumulate([own, behind, ahead, opposite], spots(0, *one, *two), *common)
    sums = accumulate(
        [first_up, first_down], spots(-1, *one) + spots(1, *one), *common, prior=sums
    )
    sums = accumulate(
        [second_up, second_down], spots(-1, *two) + spots(1, *two), *common, prior=sums
    )
    stacks, places = [first_far, second_far], spots(2, *one, *two)
    kv, row = accumulate(stacks, places, *common, prior=sums[1:], part="kv")
    queries = accumulate(
        stacks, places, *common, prior=sums[:1], extra=(row, cosine, sine), part="q"
    )[0]
    parts = [kv, shift(kv, ROW, -1), shift(kv, ROW, 2), shift(kv, ROW, 1)]
    context = attend(owners, queries, parts, np.cos(angle).T.copy(), np.sin(angle).T.copy())

    job = lambda far, nears, adds=(), apart=False: dict(
        places=spots(far, *nears), adds=list(adds), apart=apart
    )
    sent = project(context, wo, owners, [job(2, one), job(2, two)])
    up, down = shift(sent[0], LONG, 1), shift(sent[1], LONG, -1)
    context, _ = lax.optimization_barrier((context, sent[0]))
    run = functools.partial(project, context, wo, owners)
    sent = run([job(1, two), job(-1, one)])
    two_up, one_down = shift(sent[0], LONG, 1), shift(sent[1], LONG, -1)
    one_up = shift(run([job(1, one, [up])])[0], LONG, 1)
    two_down = shift(run([job(-1, two, [down])])[0], LONG, -1)
    jobs = [job(0, one, [one_up, one_down], True), job(0, two, [two_up, two_down], True)]
    mine, *others = run(jobs, own)
    for d, block in zip(OFFSETS[1:], others):
        mine = mine + shift(block, SHORT, d).astype(jnp.float32)
    step = [(p, (p + 1) % SECTIONS) for p in range(SECTIONS)]
    return lax.ppermute(mine.astype(jnp.bfloat16), "pp", step).astype(jnp.float32)[None]


def solution(mesh):
    shape = mesh.devices.shape
    grid = Mesh(mesh.devices.reshape(SIDE, shape[0] // SIDE, shape[1]), ("ty", "tx", "pp"))
    tp = ("ty", "tx")
    return jax.shard_map(
        on_device,
        mesh=grid,
        in_specs=(
            P("pp", None, tp),
            P("pp", None),
            P("pp", None, tp),
            P("pp", None, tp),
            P("pp", None, tp),
            P("pp", tp, None),
        ),
        out_specs=P("pp", None, tp),
        check_vma=False,
    )
```

time: 150 us -> 143 us (0.953)
  starting transfers between devices: 45.6 us -> 29.3 us
  waiting for transfers between devices: 76.3 us -> 88 us
  local copies, waits for them, and re-layouts: 6.11 us -> 3.9 us
    ppermute x34 -> x22, starting transfers between devices: 45.6 us -> 29.3 us  [the longest x21 29.2 us: shift(): return lax.ppermute(block, ('ty', 'tx', 'pp'), route(axis_of_core, step))]
    ppermute x34 -> x22, waiting for transfers between devices: 76.3 us -> 88 us  [the longest x21 78.2 us: shift(): return lax.ppermute(block, ('ty', 'tx', 'pp'), route(axis_of_core, step))]
    unnamed x24 -> x27, local copies, waits for them, and re-layouts: 6.11 us -> 3.06 us
    pallas_call x13 -> x11, Pallas kernels: 19.8 us -> 18.9 us  [call(): pl.pallas_call(kernel, out_shape=[jax.ShapeDtypeStruct(s, d) for s, d in...]
  transfers between devices with their start and end apart: 34 -> 22, of which waited for: 18 -> 17; matrix products, arithmetic and copies ran while one was open for 1% -> 2% of each run, Pallas kernels for 8% -> 9%
where the time goes in v3:
time: 143 us
  waiting for transfers between devices  88 us (62%)
  starting transfers between devices  29.3 us (20%)
  Pallas kernels  18.9 us (13%)
  local copies, waits for them, and re-layouts  3.9 us (3%)
  other arithmetic  2.52 us (2%)
    ppermute x21, waiting for transfers between devices, shift(): return lax.ppermute(block, ('ty', 'tx', 'pp'), route(axis_of_core, step))  78.2 us
    ppermute x21, starting transfers between devices, shift(): return lax.ppermute(block, ('ty', 'tx', 'pp'), route(axis_of_core, step))  29.2 us
    pallas_call x11, Pallas kernels, call(): pl.pallas_call(kernel, out_shape=[jax.ShapeDtypeStruct(s, d) for s, d in...  18.9 us
    ppermute x1, waiting for transfers between devices, on_device(): lax.ppermute(mine.astype(jnp.bfloat16), 'pp', step).astype(jnp.float32)  9.8 us
    unnamed x27, local copies, waits for them, and re-layouts  3.06 us
  transfers between devices with their start and end apart: 22, of which 17 were waited for; matrix products, arithmetic and copies ran while one was open for 2% of the time, Pallas kernels for 9%

profile of v3, /device:TPU:128, one launch (start us, length us, event | category | flops | bytes accessed | tf_op | source)
XLA Modules:
  0.0 142.8 jit_solution(9118604708445031594)
XLA Ops:
  0.0 2.8 %collective-permute-start.3 = (bf16[512,512]{1,0:T(8,128)(2,1)}, bf16[512,512]{1,0:T(8,128)(2,1)S(1)}, u32[]{:S(2)}, u32[]{:S(2)}) collective-permute-start(bf16[512,512]{1,0:T(8,128)(2,1)} %bitcast.77), channel_id=1, source_target_pairs={{0,48},{1,193},{2,50},{3,195},{4,52},{5,197},{6,54},{7,199},{8,56}... | collective-permute-start | bytes 1572872 | tf_op jit(solution)/shard_map/ppermute | solution.py:37
  2.9 0.8 collective-permute-start.4
  3.7 0.9 collective-permute-start
  4.6 11.0 %collective-permute-done.3.refs_2_ = bf16[512,512]{1,0:T(8,128)(2,1)S(1)} collective-permute-done((bf16[512,512]{1,0:T(8,128)(2,1)}, bf16[512,512]{1,0:T(8,128)(2,1)S(1)}, u32[]{:S(2)}, u32[]{:S(2)}) %collective-permute-start.3) | collective-permute-done | bytes 524320 | tf_op jit(solution)/shard_map/ppermute | solution.py:37
  15.5 0.8 constant_dynamic-update-slice_fusion.1
  16.4 0.0 collective-permute-done.4.refs_3_
  16.4 0.8 constant_dynamic-update-slice_fusion
  17.2 3.0 %collective-permute-start.5 = (bf16[1024,512]{1,0:T(8,128)(2,1)}, bf16[1024,512]{1,0:T(8,128)(2,1)}, u32[]{:S(2)}, u32[]{:S(2)}) collective-permute-start(bf16[1024,512]{1,0:T(8,128)(2,1)} %constant_dynamic-update-slice_fusion), channel_id=1, source_target_pairs={{0,192},{1,49},{2,194},{3,51},{4,196},{5,53},{6,198},{7,55},{8,200... | collective-permute-start | bytes 3145736 | tf_op jit(solution)/shard_map/ppermute | solution.py:37
  20.2 0.0 collective-permute-done.refs_1_
  20.2 1.0 pad_maximum_fusion
  21.3 0.7 collective-permute-start.1
  22.0 2.5 %collective-permute-start.8 = (bf16[1024,512]{1,0:T(8,128)(2,1)}, bf16[1024,512]{1,0:T(8,128)(2,1)}, u32[]{:S(2)}, u32[]{:S(2)}) collective-permute-start(bf16[1024,512]{1,0:T(8,128)(2,1)} %pad_maximum_fusion), channel_id=1, source_target_pairs={{0,192},{1,49},{2,194},{3,51},{4,196},{5,53},{6,198},{7,55},{8,200... | collective-permute-start | bytes 3145736 | tf_op jit(solution)/shard_map/ppermute | solution.py:37
  24.5 0.1 collective-permute-start.7
  24.6 0.1 pad_add_fusion.table.place
  24.7 8.2 %collective-permute-done.5.refs_1_ = bf16[1024,512]{1,0:T(8,128)(2,1)} collective-permute-done((bf16[1024,512]{1,0:T(8,128)(2,1)}, bf16[1024,512]{1,0:T(8,128)(2,1)}, u32[]{:S(2)}, u32[]{:S(2)}) %collective-permute-start.5) | collective-permute-done | bytes 1048608 | tf_op jit(solution)/shard_map/ppermute | solution.py:37
  32.9 3.7 %collective-permute-start.6 = (bf16[1024,512]{1,0:T(8,128)(2,1)}, bf16[1024,512]{1,0:T(8,128)(2,1)S(1)}, u32[]{:S(2)}, u32[]{:S(2)}) collective-permute-start(bf16[1024,512]{1,0:T(8,128)(2,1)} %collective-permute-done.5.refs_1_), channel_id=1, source_target_pairs={{0,192},{1,49},{2,194},{3,51},{4,196},{5,53},{6,198},{7,55},{8,200... | collective-permute-start | bytes 3145736 | tf_op jit(solution)/shard_map/ppermute | solution.py:37
  36.6 1.0 collective-permute-done.1.refs_0_
  37.6 0.0 collective-permute-start.2
  37.6 0.0 copy-start.1
  37.6 2.2 %copy-done.1 = bf16[1,8192,256]{2,1,0:T(8,128)(2,1)S(1)} copy-done((bf16[1,8192,256]{2,1,0:T(8,128)(2,1)S(1)}, bf16[1,8192,256]{2,1,0:T(8,128)(2,1)}, u32[]{:S(2)}) %copy-start.1) | copy-done | bytes 4194328
  39.8 1.8 %shard_map.118 = (f32[512,256]{1,0:T(8,128)S(1)}, f32[512,64]{1,0:T(8,128)S(1)}, f32[512,128]{1,0:T(8,128)S(1)}) custom-call(s32[17]{0:T(128)S(1)} %pad_add_fusion.table.place, bf16[512,512]{1,0:T(8,128)(2,1)S(1)} %bitcast.81, bf16[512,512]{1,0:T(8,128)(2,1)S(1)} %collective-permute-done.refs_1_, bf16[512,512]{1,0:T(8,128)(2,1)S(1)} %collective-permute-done.3.refs_2_, ...), custom_call_target="tpu_custom_call" | custom-call | flops 5368709120 | bytes 6823936 | tf_op jit(solution)/shard_map/pallas_call | solution.py:51
  41.6 2.5 %collective-permute-done.8.refs_1_ = bf16[1024,512]{1,0:T(8,128)(2,1)} collective-permute-done((bf16[1024,512]{1,0:T(8,128)(2,1)}, bf16[1024,512]{1,0:T(8,128)(2,1)}, u32[]{:S(2)}, u32[]{:S(2)}) %collective-permute-start.8) | collective-permute-done | bytes 1048608 | tf_op jit(solution)/shard_map/ppermute | solution.py:37
  44.1 3.3 %shard_map.119 = (f32[512,256]{1,0:T(8,128)S(1)}, f32[512,64]{1,0:T(8,128)S(1)}, f32[512,128]{1,0:T(8,128)S(1)}) custom-call(s32[17]{0:T(128)S(1)} %pad_add_fusion.table.place, bf16[1024,512]{1,0:T(8,128)(2,1)} %collective-permute-done.1.refs_0_, bf16[1024,512]{1,0:T(8,128)(2,1)} %collective-permute-done.8.refs_1_, f32[1,8192]{1,0:T(1,128)S(1)} %copy-done.5, ...), custom_call_target="tpu_custom_call" | custom-call | flops 5368709120 | bytes 7741440 | tf_op jit(solution)/shard_map/pallas_call | solution.py:51
  47.5 1.3 collective-permute-done.7.refs_0_
  48.7 3.0 %shard_map.120 = (f32[512,256]{1,0:T(8,128)S(1)}, f32[512,64]{1,0:T(8,128)S(1)}, f32[512,128]{1,0:T(8,128)S(1)}) custom-call(s32[17]{0:T(128)S(1)} %pad_add_fusion.table.place, bf16[1024,512]{1,0:T(8,128)(2,1)S(1)} %collective-permute-done.7.refs_0_, bf16[1024,512]{1,0:T(8,128)(2,1)} %collective-permute-done.5.refs_1_, f32[1,8192]{1,0:T(1,128)S(1)} %copy-done.5, ...), custom_call_target="tpu_custom_call" | custom-call | flops 5368709120 | bytes 7741440 | tf_op jit(solution)/shard_map/pallas_call | solution.py:51
  51.8 3.5 %collective-permute-done.6.refs_1_ = bf16[1024,512]{1,0:T(8,128)(2,1)S(1)} collective-permute-done((bf16[1024,512]{1,0:T(8,128)(2,1)}, bf16[1024,512]{1,0:T(8,128)(2,1)S(1)}, u32[]{:S(2)}, u32[]{:S(2)}) %collective-permute-start.6) | collective-permute-done | bytes 1048608 | tf_op jit(solution)/shard_map/ppermute | solution.py:37
  55.3 4.6 %collective-permute-done.2.refs_0_ = bf16[1024,512]{1,0:T(8,128)(2,1)S(1)} collective-permute-done((bf16[1024,512]{1,0:T(8,128)(2,1)}, bf16[1024,512]{1,0:T(8,128)(2,1)S(1)}, u32[]{:S(2)}, u32[]{:S(2)}) %collective-permute-start.2) | collective-permute-done | bytes 1048608 | tf_op jit(solution)/shard_map/ppermute | solution.py:37
  60.0 1.5 %shard_map.121 = (bf16[64,512]{1,0:T(8,128)(2,1)S(1)}, f32[512,128]{1,0:T(8,128)S(1)}) custom-call(s32[17]{0:T(128)S(1)} %pad_add_fusion.table.place, bf16[1024,512]{1,0:T(8,128)(2,1)S(1)} %collective-permute-done.2.refs_0_, bf16[1024,512]{1,0:T(8,128)(2,1)S(1)} %collective-permute-done.6.refs_1_, f32[1,8192]{1,0:T(1,128)S(1)} %copy-done.5, ...), custom_call_target="tpu_custom_call" | custom-call | flops 5368709120 | bytes 5120000 | tf_op jit(solution)/shard_map/pallas_call | solution.py:51
  61.5 0.3 collective-permute-start.10
  61.7 4.4 %collective-permute-start.11 = (bf16[64,512]{1,0:T(8,128)(2,1)S(1)}, bf16[64,512]{1,0:T(8,128)(2,1)S(1)}, u32[]{:S(2)}, u32[]{:S(2)}) collective-permute-start(bf16[64,512]{1,0:T(8,128)(2,1)S(1)} %get-tuple-element.35.own), channel_id=1, source_target_pairs={{0,16},{1,17},{2,18},{3,19},{4,20},{5,21},{6,22},{7,23},{8,24},{9,... | collective-permute-start | bytes 196616 | tf_op jit(solution)/shard_map/ppermute | solution.py:37
  66.1 0.0 collective-permute-start.9
  66.1 0.0 copy-start.9
  66.2 0.0 copy-start.10
  66.2 0.0 copy-start
  66.2 1.3 shard_map.122.q
  67.5 0.0 collective-permute-done.10.two
  67.5 0.7 collective-permute-done.11.left
  68.2 2.2 %collective-permute-done.9.right = bf16[64,512]{1,0:T(8,128)(2,1)S(1)} collective-permute-done((bf16[64,512]{1,0:T(8,128)(2,1)S(1)}, bf16[64,512]{1,0:T(8,128)(2,1)S(1)}, u32[]{:S(2)}, u32[]{:S(2)}) %collective-permute-start.9) | collective-permute-done | bytes 65568 | tf_op jit(solution)/shard_map/ppermute | solution.py:37
  70.4 1.9 %shard_map.123.context = bf16[512,256]{1,0:T(8,128)(2,1)S(1)} custom-call(s32[17]{0:T(128)S(1)} %pad_add_fusion.table.place, bf16[512,256]{1,0:T(8,128)(2,1)S(1)} %shard_map.122.q, bf16[64,512]{1,0:T(8,128)(2,1)S(1)} %get-tuple-element.35.own, bf16[64,512]{1,0:T(8,128)(2,1)S(1)} %collective-permute-done.9.right, ...), custom_call_target="tpu_custom_call" | custom-call | flops 268435456 | bytes 1310720 | tf_op jit(solution)/shard_map/pallas_call | solution.py:51
  72.3 1.3 shard_map.124
  73.6 0.2 collective-permute-start.16
  73.8 1.9 %collective-permute-start.12 = (bf16[1024,512]{1,0:T(8,128)(2,1)S(1)}, bf16[1024,512]{1,0:T(8,128)(2,1)S(1)}, u32[]{:S(2)}, u32[]{:S(2)}) collective-permute-start(bf16[1024,512]{1,0:T(8,128)(2,1)S(1)} %get-tuple-element.36), channel_id=1, source_target_pairs={{0,64},{1,17},{2,66},{3,19},{4,68},{5,21},{6,70},{7,23},{8,72},{9,... | collective-permute-start | bytes 3145736 | tf_op jit(solution)/shard_map/ppermute | solution.py:37
  75.7 1.3 shard_map.126
  76.9 1.4 collective-permute-start.14
  78.3 0.7 collective-permute-start.15
  79.1 9.4 %collective-permute-done.16.refs_2_ = bf16[1024,512]{1,0:T(8,128)(2,1)S(1)} collective-permute-done((bf16[1024,512]{1,0:T(8,128)(2,1)S(1)}, bf16[1024,512]{1,0:T(8,128)(2,1)S(1)}, u32[]{:S(2)}, u32[]{:S(2)}) %collective-permute-start.16) | collective-permute-done | bytes 1048608 | tf_op jit(solution)/shard_map/ppermute | solution.py:37
  88.5 1.0 shard_map.127
  89.4 1.4 collective-permute-start.17
  90.8 1.0 shard_map.125
  91.8 0.8 collective-permute-start.13
  92.6 7.1 %collective-permute-done.14.refs_5_ = bf16[1024,512]{1,0:T(8,128)(2,1)S(1)} collective-permute-done((bf16[1024,512]{1,0:T(8,128)(2,1)S(1)}, bf16[1024,512]{1,0:T(8,128)(2,1)S(1)}, u32[]{:S(2)}, u32[]{:S(2)}) %collective-permute-start.14) | collective-permute-done | bytes 1048608 | tf_op jit(solution)/shard_map/ppermute | solution.py:37
  99.7 1.3 collective-permute-done.15.refs_6_
  101.0 9.9 %collective-permute-done.17.refs_7_ = bf16[1024,512]{1,0:T(8,128)(2,1)S(1)} collective-permute-done((bf16[1024,512]{1,0:T(8,128)(2,1)S(1)}, bf16[1024,512]{1,0:T(8,128)(2,1)S(1)}, u32[]{:S(2)}, u32[]{:S(2)}) %collective-permute-start.17) | collective-permute-done | bytes 1048608 | tf_op jit(solution)/shard_map/ppermute | solution.py:37
  110.9 1.3 collective-permute-done.13.refs_4_
  112.3 1.5 %shard_map.128 = (f32[512,512]{1,0:T(8,128)S(1)}, bf16[512,512]{1,0:T(8,128)(2,1)S(1)}, bf16[512,512]{1,0:T(8,128)(2,1)S(1)}, bf16[512,512]{1,0:T(8,128)(2,1)S(1)}) custom-call(s32[17]{0:T(128)S(1)} %pad_add_fusion.table.place, bf16[512,256]{1,0:T(8,128)(2,1)S(1)} %shard_map.123.context, bf16[256,8192]{1,0:T(8,128)(2,1)S(1)} %bitcast.25, ...), custom_call_target="tpu_custom_call" | custom-call | flops 536870912 | bytes 12058624 | tf_op jit(solution)/shard_map/pallas_call | solution.py:51
  113.8 1.8 %collective-permute-start.18 = (bf16[512,512]{1,0:T(8,128)(2,1)S(1)}, bf16[512,512]{1,0:T(8,128)(2,1)S(1)}, u32[]{:S(2)}, u32[]{:S(2)}) collective-permute-start(bf16[512,512]{1,0:T(8,128)(2,1)S(1)} %get-tuple-element.42), channel_id=1, source_target_pairs={{0,48},{1,193},{2,50},{3,195},{4,52},{5,197},{6,54},{7,199},{8,56}... | collective-permute-start | bytes 1572872 | tf_op jit(solution)/shard_map/ppermute | solution.py:37
  115.6 0.3 collective-permute-start.19
  115.9 1.5 %collective-permute-start.20 = (bf16[512,512]{1,0:T(8,128)(2,1)S(1)}, bf16[512,512]{1,0:T(8,128)(2,1)S(1)}, u32[]{:S(2)}, u32[]{:S(2)}) collective-permute-start(bf16[512,512]{1,0:T(8,128)(2,1)S(1)} %get-tuple-element.44), channel_id=1, source_target_pairs={{0,32},{1,129},{2,34},{3,131},{4,36},{5,133},{6,38},{7,135},{8,40}... | collective-permute-start | bytes 1572872 | tf_op jit(solution)/shard_map/ppermute | solution.py:37
  117.4 5.6 %collective-permute-done.18 = bf16[512,512]{1,0:T(8,128)(2,1)S(1)} collective-permute-done((bf16[512,512]{1,0:T(8,128)(2,1)S(1)}, bf16[512,512]{1,0:T(8,128)(2,1)S(1)}, u32[]{:S(2)}, u32[]{:S(2)}) %collective-permute-start.18) | collective-permute-done | bytes 524320 | tf_op jit(solution)/shard_map/ppermute | solution.py:37
  123.0 8.5 %collective-permute-done.19 = bf16[512,512]{1,0:T(8,128)(2,1)S(1)} collective-permute-done((bf16[512,512]{1,0:T(8,128)(2,1)S(1)}, bf16[512,512]{1,0:T(8,128)(2,1)S(1)}, u32[]{:S(2)}, u32[]{:S(2)}) %collective-permute-start.19) | collective-permute-done | bytes 524320 | tf_op jit(solution)/shard_map/ppermute | solution.py:37
  131.6 0.3 add_convert_fusion
  131.9 0.0 collective-permute-start.21
  131.9 9.8 %collective-permute-done.21 = bf16[512,512]{1,0:T(8,128)(2,1)S(1)} collective-permute-done((bf16[512,512]{1,0:T(8,128)(2,1)S(1)}, bf16[512,512]{1,0:T(8,128)(2,1)S(1)}, u32[]{:S(2)}, u32[]{:S(2)}) %collective-permute-start.21) | collective-permute-done | bytes 524320 | tf_op jit(solution)/shard_map/ppermute | solution.py:292
  141.7 1.1 bitcast_convert_fusion
  (24 shorter events, 0.1 us)
Async XLA Ops:
  0.0 20.2 %copy-start.6 = (bf16[1,512,512]{2,1,0:T(8,128)(2,1)S(1)}, bf16[1,512,512]{2,1,0:T(8,128)(2,1)}, u32[]{:S(2)}) copy-start(bf16[1,512,512]{2,1,0:T(8,128)(2,1)} %param.12) | copy-start | bytes 1572868
  0.0 24.5 %copy-start.11 = (s32[16]{0:T(128)S(1)}, s32[16]{0:T(128)}, u32[]{:S(2)}) copy-start(s32[16]{0:T(128)} %constant.51.clone) | copy-start | bytes 196
  0.0 24.5 %copy-start.12 = (s32[16]{0:T(128)S(1)}, s32[16]{0:T(128)}, u32[]{:S(2)}) copy-start(s32[16]{0:T(128)} %constant.52.clone) | copy-start | bytes 196
  0.0 37.6 %copy-start.3 = (bf16[1,8192,32]{1,2,0:T(8,128)(2,1)S(1)}, bf16[1,8192,32]{1,2,0:T(8,128)(2,1)}, u32[]{:S(2)}) copy-start(bf16[1,8192,32]{1,2,0:T(8,128)(2,1)} %param.15) | copy-start | bytes 1572868
  0.0 37.6 %copy-start.4 = (bf16[1,8192,32]{1,2,0:T(8,128)(2,1)S(1)}, bf16[1,8192,32]{1,2,0:T(8,128)(2,1)}, u32[]{:S(2)}) copy-start(bf16[1,8192,32]{1,2,0:T(8,128)(2,1)} %param.16) | copy-start | bytes 1572868
  0.0 37.6 %copy-start.5 = (f32[1,8192]{1,0:T(1,128)S(1)}, f32[1,8192]{1,0:T(1,128)}, u32[]{:S(2)}) copy-start(f32[1,8192]{1,0:T(1,128)} %refs_8_.5) | copy-start | bytes 98308
  0.0 15.5 %collective-permute-start.3 = (bf16[512,512]{1,0:T(8,128)(2,1)}, bf16[512,512]{1,0:T(8,128)(2,1)S(1)}, u32[]{:S(2)}, u32[]{:S(2)}) collective-permute-start(bf16[512,512]{1,0:T(8,128)(2,1)} %bitcast.77), channel_id=1, source_target_pairs={{0,48},{1,193},{2,50},{3,195},{4,52},{5,197},{6,54},{7,199},{8,56}... | collective-permute-start | bytes 1572872 | tf_op jit(solution)/shard_map/ppermute | solution.py:37
  2.9 13.5 %collective-permute-start.4 = (bf16[512,512]{1,0:T(8,128)(2,1)}, bf16[512,512]{1,0:T(8,128)(2,1)S(1)}, u32[]{:S(2)}, u32[]{:S(2)}) collective-permute-start(bf16[512,512]{1,0:T(8,128)(2,1)} %bitcast.78), channel_id=1, source_target_pairs={{0,32},{1,129},{2,34},{3,131},{4,36},{5,133},{6,38},{7,135},{8,40}... | collective-permute-start | bytes 1572872 | tf_op jit(solution)/shard_map/ppermute | solution.py:37
  3.7 16.6 %collective-permute-start = (bf16[512,512]{1,0:T(8,128)(2,1)}, bf16[512,512]{1,0:T(8,128)(2,1)S(1)}, u32[]{:S(2)}, u32[]{:S(2)}) collective-permute-start(bf16[512,512]{1,0:T(8,128)(2,1)} %bitcast.79), channel_id=1, source_target_pairs={{0,16},{1,65},{2,18},{3,67},{4,20},{5,69},{6,22},{7,71},{8,24},{9,... | collective-permute-start | bytes 1572872 | tf_op jit(solution)/shard_map/ppermute | solution.py:37
  17.2 15.6 %collective-permute-start.5 = (bf16[1024,512]{1,0:T(8,128)(2,1)}, bf16[1024,512]{1,0:T(8,128)(2,1)}, u32[]{:S(2)}, u32[]{:S(2)}) collective-permute-start(bf16[1024,512]{1,0:T(8,128)(2,1)} %constant_dynamic-update-slice_fusion), channel_id=1, source_target_pairs={{0,192},{1,49},{2,194},{3,51},{4,196},{5,53},{6,198},{7,55},{8,200... | collective-permute-start | bytes 3145736 | tf_op jit(solution)/shard_map/ppermute | solution.py:37
  21.3 16.3 %collective-permute-start.1 = (bf16[1024,512]{1,0:T(8,128)(2,1)}, bf16[1024,512]{1,0:T(8,128)(2,1)}, u32[]{:S(2)}, u32[]{:S(2)}) collective-permute-start(bf16[1024,512]{1,0:T(8,128)(2,1)} %pad_maximum_fusion), channel_id=1, source_target_pairs={{0,64},{1,17},{2,66},{3,19},{4,68},{5,21},{6,70},{7,23},{8,72},{9,... | collective-permute-start | bytes 3145736 | tf_op jit(solution)/shard_map/ppermute | solution.py:37
  22.0 22.1 %collective-permute-start.8 = (bf16[1024,512]{1,0:T(8,128)(2,1)}, bf16[1024,512]{1,0:T(8,128)(2,1)}, u32[]{:S(2)}, u32[]{:S(2)}) collective-permute-start(bf16[1024,512]{1,0:T(8,128)(2,1)} %pad_maximum_fusion), channel_id=1, source_target_pairs={{0,192},{1,49},{2,194},{3,51},{4,196},{5,53},{6,198},{7,55},{8,200... | collective-permute-start | bytes 3145736 | tf_op jit(solution)/shard_map/ppermute | solution.py:37
  24.5 24.2 %collective-permute-start.7 = (bf16[1024,512]{1,0:T(8,128)(2,1)}, bf16[1024,512]{1,0:T(8,128)(2,1)S(1)}, u32[]{:S(2)}, u32[]{:S(2)}) collective-permute-start(bf16[1024,512]{1,0:T(8,128)(2,1)} %constant_dynamic-update-slice_fusion), channel_id=1, source_target_pairs={{0,64},{1,17},{2,66},{3,19},{4,68},{5,21},{6,70},{7,23},{8,72},{9,... | collective-permute-start | bytes 3145736 | tf_op jit(solution)/shard_map/ppermute | solution.py:37
  32.9 22.5 %collective-permute-start.6 = (bf16[1024,512]{1,0:T(8,128)(2,1)}, bf16[1024,512]{1,0:T(8,128)(2,1)S(1)}, u32[]{:S(2)}, u32[]{:S(2)}) collective-permute-start(bf16[1024,512]{1,0:T(8,128)(2,1)} %collective-permute-done.5.refs_1_), channel_id=1, source_target_pairs={{0,192},{1,49},{2,194},{3,51},{4,196},{5,53},{6,198},{7,55},{8,200... | collective-permute-start | bytes 3145736 | tf_op jit(solution)/shard_map/ppermute | solution.py:37
  37.6 22.4 %collective-permute-start.2 = (bf16[1024,512]{1,0:T(8,128)(2,1)}, bf16[1024,512]{1,0:T(8,128)(2,1)S(1)}, u32[]{:S(2)}, u32[]{:S(2)}) collective-permute-start(bf16[1024,512]{1,0:T(8,128)(2,1)} %collective-permute-done.1.refs_0_), channel_id=1, source_target_pairs={{0,64},{1,17},{2,66},{3,19},{4,68},{5,21},{6,70},{7,23},{8,72},{9,... | collective-permute-start | bytes 3145736 | tf_op jit(solution)/shard_map/ppermute | solution.py:37
  37.6 2.2 %copy-start.1 = (bf16[1,8192,256]{2,1,0:T(8,128)(2,1)S(1)}, bf16[1,8192,256]{2,1,0:T(8,128)(2,1)}, u32[]{:S(2)}) copy-start(bf16[1,8192,256]{2,1,0:T(8,128)(2,1)} %param.14) | copy-start | bytes 12582916
  39.8 4.3 %copy-start.2 = (bf16[1,8192,256]{2,1,0:T(8,128)(2,1)S(1)}, bf16[1,8192,256]{2,1,0:T(8,128)(2,1)}, u32[]{:S(2)}) copy-start(bf16[1,8192,256]{2,1,0:T(8,128)(2,1)} %param.14) | copy-start | bytes 12582916
  60.0 6.2 %copy-start.7 = (f32[512,128]{1,0:T(8,128)S(1)}, f32[512,128]{1,0:T(8,128)}, u32[]{:S(2)}) copy-start(f32[512,128]{1,0:T(8,128)} %constant.53.clone.refs_12_) | copy-start | bytes 786436
  60.0 6.2 %copy-start.8 = (f32[512,128]{1,0:T(8,128)S(1)}, f32[512,128]{1,0:T(8,128)}, u32[]{:S(2)}) copy-start(f32[512,128]{1,0:T(8,128)} %constant.54.clone.refs_13_) | copy-start | bytes 786436
  61.5 6.1 %collective-permute-start.10 = (bf16[64,512]{1,0:T(8,128)(2,1)S(1)}, bf16[64,512]{1,0:T(8,128)(2,1)S(1)}, u32[]{:S(2)}, u32[]{:S(2)}) collective-permute-start(bf16[64,512]{1,0:T(8,128)(2,1)S(1)} %get-tuple-element.35.own), channel_id=1, source_target_pairs={{0,32},{1,33},{2,34},{3,35},{4,36},{5,37},{6,38},{7,39},{8,40},{9,... | collective-permute-start | bytes 196616 | tf_op jit(solution)/shard_map/ppermute | solution.py:37
  61.7 6.5 %collective-permute-start.11 = (bf16[64,512]{1,0:T(8,128)(2,1)S(1)}, bf16[64,512]{1,0:T(8,128)(2,1)S(1)}, u32[]{:S(2)}, u32[]{:S(2)}) collective-permute-start(bf16[64,512]{1,0:T(8,128)(2,1)S(1)} %get-tuple-element.35.own), channel_id=1, source_target_pairs={{0,16},{1,17},{2,18},{3,19},{4,20},{5,21},{6,22},{7,23},{8,24},{9,... | collective-permute-start | bytes 196616 | tf_op jit(solution)/shard_map/ppermute | solution.py:37
  66.1 4.3 %collective-permute-start.9 = (bf16[64,512]{1,0:T(8,128)(2,1)S(1)}, bf16[64,512]{1,0:T(8,128)(2,1)S(1)}, u32[]{:S(2)}, u32[]{:S(2)}) collective-permute-start(bf16[64,512]{1,0:T(8,128)(2,1)S(1)} %get-tuple-element.35.own), channel_id=1, source_target_pairs={{0,48},{1,49},{2,50},{3,51},{4,52},{5,53},{6,54},{7,55},{8,56},{9,... | collective-permute-start | bytes 196616 | tf_op jit(solution)/shard_map/ppermute | solution.py:37
  66.1 4.3 %copy-start.9 = (f32[64,512]{1,0:T(8,128)S(1)}, f32[64,512]{1,0:T(8,128)}, u32[]{:S(2)}) copy-start(f32[64,512]{1,0:T(8,128)} %constant.55.clone.cosine) | copy-start | bytes 393220
  66.2 4.2 %copy-start.10 = (f32[64,512]{1,0:T(8,128)S(1)}, f32[64,512]{1,0:T(8,128)}, u32[]{:S(2)}) copy-start(f32[64,512]{1,0:T(8,128)} %constant.56.clone.sine) | copy-start | bytes 393220
  66.2 6.1 %copy-start = (bf16[1,256,8192]{2,1,0:T(8,128)(2,1)S(1)}, bf16[1,256,8192]{2,1,0:T(8,128)(2,1)}, u32[]{:S(2)}) copy-start(bf16[1,256,8192]{2,1,0:T(8,128)(2,1)} %param.17) | copy-start | bytes 12582916
  73.6 14.9 %collective-permute-start.16 = (bf16[1024,512]{1,0:T(8,128)(2,1)S(1)}, bf16[1024,512]{1,0:T(8,128)(2,1)S(1)}, u32[]{:S(2)}, u32[]{:S(2)}) collective-permute-start(bf16[1024,512]{1,0:T(8,128)(2,1)S(1)} %get-tuple-element.40), channel_id=1, source_target_pairs={{0,192},{1,49},{2,194},{3,51},{4,196},{5,53},{6,198},{7,55},{8,200... | collective-permute-start | bytes 3145736 | tf_op jit(solution)/shard_map/ppermute | solution.py:37
  73.8 17.1 %collective-permute-start.12 = (bf16[1024,512]{1,0:T(8,128)(2,1)S(1)}, bf16[1024,512]{1,0:T(8,128)(2,1)S(1)}, u32[]{:S(2)}, u32[]{:S(2)}) collective-permute-start(bf16[1024,512]{1,0:T(8,128)(2,1)S(1)} %get-tuple-element.36), channel_id=1, source_target_pairs={{0,64},{1,17},{2,66},{3,19},{4,68},{5,21},{6,70},{7,23},{8,72},{9,... | collective-permute-start | bytes 3145736 | tf_op jit(solution)/shard_map/ppermute | solution.py:37
  76.9 22.7 %collective-permute-start.14 = (bf16[1024,512]{1,0:T(8,128)(2,1)S(1)}, bf16[1024,512]{1,0:T(8,128)(2,1)S(1)}, u32[]{:S(2)}, u32[]{:S(2)}) collective-permute-start(bf16[1024,512]{1,0:T(8,128)(2,1)S(1)} %get-tuple-element.38), channel_id=1, source_target_pairs={{0,192},{1,49},{2,194},{3,51},{4,196},{5,53},{6,198},{7,55},{8,200... | collective-permute-start | bytes 3145736 | tf_op jit(solution)/shard_map/ppermute | solution.py:37
  78.3 22.7 %collective-permute-start.15 = (bf16[1024,512]{1,0:T(8,128)(2,1)S(1)}, bf16[1024,512]{1,0:T(8,128)(2,1)S(1)}, u32[]{:S(2)}, u32[]{:S(2)}) collective-permute-start(bf16[1024,512]{1,0:T(8,128)(2,1)S(1)} %get-tuple-element.39), channel_id=1, source_target_pairs={{0,64},{1,17},{2,66},{3,19},{4,68},{5,21},{6,70},{7,23},{8,72},{9,... | collective-permute-start | bytes 3145736 | tf_op jit(solution)/shard_map/ppermute | solution.py:37
  89.4 21.5 %collective-permute-start.17 = (bf16[1024,512]{1,0:T(8,128)(2,1)S(1)}, bf16[1024,512]{1,0:T(8,128)(2,1)S(1)}, u32[]{:S(2)}, u32[]{:S(2)}) collective-permute-start(bf16[1024,512]{1,0:T(8,128)(2,1)S(1)} %shard_map.127), channel_id=1, source_target_pairs={{0,192},{1,49},{2,194},{3,51},{4,196},{5,53},{6,198},{7,55},{8,200... | collective-permute-start | bytes 3145736 | tf_op jit(solution)/shard_map/ppermute | solution.py:37
  91.8 20.4 %collective-permute-start.13 = (bf16[1024,512]{1,0:T(8,128)(2,1)S(1)}, bf16[1024,512]{1,0:T(8,128)(2,1)S(1)}, u32[]{:S(2)}, u32[]{:S(2)}) collective-permute-start(bf16[1024,512]{1,0:T(8,128)(2,1)S(1)} %shard_map.125), channel_id=1, source_target_pairs={{0,64},{1,17},{2,66},{3,19},{4,68},{5,21},{6,70},{7,23},{8,72},{9,... | collective-permute-start | bytes 3145736 | tf_op jit(solution)/shard_map/ppermute | solution.py:37
  113.8 9.3 %collective-permute-start.18 = (bf16[512,512]{1,0:T(8,128)(2,1)S(1)}, bf16[512,512]{1,0:T(8,128)(2,1)S(1)}, u32[]{:S(2)}, u32[]{:S(2)}) collective-permute-start(bf16[512,512]{1,0:T(8,128)(2,1)S(1)} %get-tuple-element.42), channel_id=1, source_target_pairs={{0,48},{1,193},{2,50},{3,195},{4,52},{5,197},{6,54},{7,199},{8,56}... | collective-permute-start | bytes 1572872 | tf_op jit(solution)/shard_map/ppermute | solution.py:37
  115.6 16.0 %collective-permute-start.19 = (bf16[512,512]{1,0:T(8,128)(2,1)S(1)}, bf16[512,512]{1,0:T(8,128)(2,1)S(1)}, u32[]{:S(2)}, u32[]{:S(2)}) collective-permute-start(bf16[512,512]{1,0:T(8,128)(2,1)S(1)} %get-tuple-element.43), channel_id=1, source_target_pairs={{0,16},{1,65},{2,18},{3,67},{4,20},{5,69},{6,22},{7,71},{8,24},{9,... | collective-permute-start | bytes 1572872 | tf_op jit(solution)/shard_map/ppermute | solution.py:37
  115.9 15.7 %collective-permute-start.20 = (bf16[512,512]{1,0:T(8,128)(2,1)S(1)}, bf16[512,512]{1,0:T(8,128)(2,1)S(1)}, u32[]{:S(2)}, u32[]{:S(2)}) collective-permute-start(bf16[512,512]{1,0:T(8,128)(2,1)S(1)} %get-tuple-element.44), channel_id=1, source_target_pairs={{0,32},{1,129},{2,34},{3,131},{4,36},{5,133},{6,38},{7,135},{8,40}... | collective-permute-start | bytes 1572872 | tf_op jit(solution)/shard_map/ppermute | solution.py:37
  131.9 9.8 %collective-permute-start.21 = (bf16[512,512]{1,0:T(8,128)(2,1)S(1)}, bf16[512,512]{1,0:T(8,128)(2,1)S(1)}, u32[]{:S(2)}, u32[]{:S(2)}) collective-permute-start(bf16[512,512]{1,0:T(8,128)(2,1)S(1)} %add_convert_fusion), channel_id=1, source_target_pairs={{0,1},{1,2},{2,3},{3,4},{4,5},{5,6},{6,7},{7,8},{8,9},{9,10},{10,1... | collective-permute-start | bytes 1572872 | tf_op jit(solution)/shard_map/ppermute | solution.py:292

commit v4 on v3

--- a/solution.py
+++ b/solution.py
@@ -142,7 +142,8 @@
     return call(kernel, table, args, specs, outs, COST * rows * depth * count * (heads + narrow))
 
 
-def attend_kernel(place, q, own, right, two, left, cosine, sine, out, keys_raw, values):
+def attend_kernel(place, q, own, right, two, left, cosine, sine, *refs):
+    columns, (out, up, down, keys_raw, values) = refs[:SIDE], refs[SIDE:]
     rows = q.shape[0]
     half = rows // 2
     part = own.shape[0] // 2
@@ -175,14 +176,22 @@
             probs = weights * (1.0 / jnp.sum(weights, axis=1, keepdims=True))
             context = dot(probs.astype(jnp.bfloat16), values[:, : (i + 1) * half], ((1,), (1,)))
             out[i * half : (i + 1) * half, head] = context.astype(jnp.bfloat16)
-
-
-def attend(place, q, parts, cosine, sine):
+    for n, weight in enumerate(columns):
+        sums = (up, down)[n // 2]
+        sums[pl.ds(n % 2 * rows, rows)] = dot(out[...], weight[...]).astype(jnp.bfloat16)
+
+
+def attend(place, q, parts, cosine, sine, wo, places):
+    rows, depth = q.shape
+    width = wo.shape[1] // SIDE**2
     args = [q, *parts, cosine, sine]
     specs = [whole(a.shape) for a in args]
-    outs = [(q.shape, jnp.bfloat16)]
-    scratch = [pltpu.VMEM((HD, q.shape[0]), jnp.bfloat16)] * 2
-    return call(attend_kernel, place, args, specs, outs, 8 * q.shape[0] ** 2 * HD, scratch)[0]
+    for k in places:
+        args.append(wo)
+        specs.append(pl.BlockSpec((depth, width), lambda i, t, k=k: (0, t[k])))
+    outs = [(q.shape, jnp.bfloat16)] + [((2 * rows, width), jnp.bfloat16)] * 2
+    scratch = [pltpu.VMEM((HD, rows), jnp.bfloat16)] * 2
+    return call(attend_kernel, place, args, specs, outs, 12 * rows**2 * HD, scratch)
 
 
 def project_kernel(jobs, base, table, context, *refs):
@@ -265,20 +274,20 @@
     sums = accumulate(
         [second_up, second_down], spots(-1, *two) + spots(1, *two), *common, prior=sums
     )
-    stacks, places = [first_far, second_far], spots(2, *one, *two)
+    sums = accumulate([second_far], spots(2, *two), *common, prior=sums)
+    stacks, places = [first_far], spots(2, *one)
     kv, row = accumulate(stacks, places, *common, prior=sums[1:], part="kv")
     queries = accumulate(
         stacks, places, *common, prior=sums[:1], extra=(row, cosine, sine), part="q"
     )[0]
     parts = [kv, shift(kv, ROW, -1), shift(kv, ROW, 2), shift(kv, ROW, 1)]
-    context = attend(owners, queries, parts, np.cos(angle).T.copy(), np.sin(angle).T.copy())
+    turns = (np.cos(angle).T.copy(), np.sin(angle).T.copy())
+    context, *sent = attend(owners, queries, parts, *turns, wo, spots(2, *one, *two))
 
     job = lambda far, nears, adds=(), apart=False: dict(
         places=spots(far, *nears), adds=list(adds), apart=apart
     )
-    sent = project(context, wo, owners, [job(2, one), job(2, two)])
     up, down = shift(sent[0], LONG, 1), shift(sent[1], LONG, -1)
-    context, _ = lax.optimization_barrier((context, sent[0]))
     run = functools.partial(project, context, wo, owners)
     sent = run([job(1, two), job(-1, one)])
     two_up, one_down = shift(sent[0], LONG, 1), shift(sent[1], LONG, -1)

time: 143 us -> 142 us (level)
  transfers between devices with their start and end apart: 22 -> 22, of which waited for: 17 -> 17; matrix products, arithmetic and copies ran while one was open for 2% -> 2% of each run, Pallas kernels for 9% -> 10%
where the time goes in v4:
time: 142 us
  waiting for transfers between devices  87.1 us (61%)
  starting transfers between devices  29.2 us (21%)
  Pallas kernels  18.9 us (13%)
  local copies, waits for them, and re-layouts  3.9 us (3%)
  other arithmetic  2.52 us (2%)
    ppermute x21, waiting for transfers between devices, shift(): return lax.ppermute(block, ('ty', 'tx', 'pp'), route(axis_of_core, step))  77.3 us
    ppermute x21, starting transfers between devices, shift(): return lax.ppermute(block, ('ty', 'tx', 'pp'), route(axis_of_core, step))  29.2 us
    pallas_call x11, Pallas kernels, call(): pl.pallas_call(kernel, out_shape=[jax.ShapeDtypeStruct(s, d) for s, d in...  18.9 us
    ppermute x1, waiting for transfers between devices, on_device(): lax.ppermute(mine.astype(jnp.bfloat16), 'pp', step).astype(jnp.float32)  9.8 us
    unnamed x27, local copies, waits for them, and re-layouts  3.06 us
  transfers between devices with their start and end apart: 22, of which 17 were waited for; matrix products, arithmetic and copies ran while one was open for 2% of the time, Pallas kernels for 10%

profile of v4, /device:TPU:128, one launch (start us, length us, event | category | flops | bytes accessed | tf_op | source)
XLA Modules:
  0.0 141.7 jit_solution(14210354014345143301)
XLA Ops:
  0.0 2.8 %collective-permute-start.3 = (bf16[512,512]{1,0:T(8,128)(2,1)}, bf16[512,512]{1,0:T(8,128)(2,1)S(1)}, u32[]{:S(2)}, u32[]{:S(2)}) collective-permute-start(bf16[512,512]{1,0:T(8,128)(2,1)} %bitcast.77), channel_id=1, source_target_pairs={{0,48},{1,193},{2,50},{3,195},{4,52},{5,197},{6,54},{7,199},{8,56}... | collective-permute-start | bytes 1572872 | tf_op jit(solution)/shard_map/ppermute | solution.py:37
  2.9 0.8 collective-permute-start.4
  3.7 0.9 collective-permute-start
  4.6 11.0 %collective-permute-done.3.refs_2_ = bf16[512,512]{1,0:T(8,128)(2,1)S(1)} collective-permute-done((bf16[512,512]{1,0:T(8,128)(2,1)}, bf16[512,512]{1,0:T(8,128)(2,1)S(1)}, u32[]{:S(2)}, u32[]{:S(2)}) %collective-permute-start.3) | collective-permute-done | bytes 524320 | tf_op jit(solution)/shard_map/ppermute | solution.py:37
  15.5 0.8 constant_dynamic-update-slice_fusion.1
  16.4 0.0 collective-permute-done.4.refs_3_
  16.4 0.8 constant_dynamic-update-slice_fusion
  17.2 3.0 %collective-permute-start.5 = (bf16[1024,512]{1,0:T(8,128)(2,1)}, bf16[1024,512]{1,0:T(8,128)(2,1)}, u32[]{:S(2)}, u32[]{:S(2)}) collective-permute-start(bf16[1024,512]{1,0:T(8,128)(2,1)} %constant_dynamic-update-slice_fusion), channel_id=1, source_target_pairs={{0,192},{1,49},{2,194},{3,51},{4,196},{5,53},{6,198},{7,55},{8,200... | collective-permute-start | bytes 3145736 | tf_op jit(solution)/shard_map/ppermute | solution.py:37
  20.2 0.0 collective-permute-done.refs_1_
  20.2 1.0 pad_maximum_fusion
  21.3 0.7 collective-permute-start.1
  22.0 2.5 %collective-permute-start.8 = (bf16[1024,512]{1,0:T(8,128)(2,1)}, bf16[1024,512]{1,0:T(8,128)(2,1)}, u32[]{:S(2)}, u32[]{:S(2)}) collective-permute-start(bf16[1024,512]{1,0:T(8,128)(2,1)} %pad_maximum_fusion), channel_id=1, source_target_pairs={{0,192},{1,49},{2,194},{3,51},{4,196},{5,53},{6,198},{7,55},{8,200... | collective-permute-start | bytes 3145736 | tf_op jit(solution)/shard_map/ppermute | solution.py:37
  24.5 0.1 collective-permute-start.7
  24.6 0.1 pad_add_fusion.table.place
  24.7 8.2 %collective-permute-done.5.refs_1_ = bf16[1024,512]{1,0:T(8,128)(2,1)} collective-permute-done((bf16[1024,512]{1,0:T(8,128)(2,1)}, bf16[1024,512]{1,0:T(8,128)(2,1)}, u32[]{:S(2)}, u32[]{:S(2)}) %collective-permute-start.5) | collective-permute-done | bytes 1048608 | tf_op jit(solution)/shard_map/ppermute | solution.py:37
  32.9 3.7 %collective-permute-start.6 = (bf16[1024,512]{1,0:T(8,128)(2,1)}, bf16[1024,512]{1,0:T(8,128)(2,1)S(1)}, u32[]{:S(2)}, u32[]{:S(2)}) collective-permute-start(bf16[1024,512]{1,0:T(8,128)(2,1)} %collective-permute-done.5.refs_1_), channel_id=1, source_target_pairs={{0,192},{1,49},{2,194},{3,51},{4,196},{5,53},{6,198},{7,55},{8,200... | collective-permute-start | bytes 3145736 | tf_op jit(solution)/shard_map/ppermute | solution.py:37
  36.6 2.2 %copy-done.1 = bf16[1,8192,256]{2,1,0:T(8,128)(2,1)S(1)} copy-done((bf16[1,8192,256]{2,1,0:T(8,128)(2,1)S(1)}, bf16[1,8192,256]{2,1,0:T(8,128)(2,1)}, u32[]{:S(2)}) %copy-start.1) | copy-done | bytes 4194328
  38.7 1.8 %shard_map.118 = (f32[512,256]{1,0:T(8,128)S(1)}, f32[512,64]{1,0:T(8,128)S(1)}, f32[512,128]{1,0:T(8,128)S(1)}) custom-call(s32[17]{0:T(128)S(1)} %pad_add_fusion.table.place, bf16[512,512]{1,0:T(8,128)(2,1)S(1)} %bitcast.81, bf16[512,512]{1,0:T(8,128)(2,1)S(1)} %collective-permute-done.refs_1_, bf16[512,512]{1,0:T(8,128)(2,1)S(1)} %collective-permute-done.3.refs_2_, ...), custom_call_target="tpu_custom_call" | custom-call | flops 5368709120 | bytes 6823936 | tf_op jit(solution)/shard_map/pallas_call | solution.py:51
  40.5 0.0 collective-permute-done.1.refs_0_
  40.5 0.1 collective-permute-start.2
  40.6 3.4 %collective-permute-done.8.refs_1_ = bf16[1024,512]{1,0:T(8,128)(2,1)} collective-permute-done((bf16[1024,512]{1,0:T(8,128)(2,1)}, bf16[1024,512]{1,0:T(8,128)(2,1)}, u32[]{:S(2)}, u32[]{:S(2)}) %collective-permute-start.8) | collective-permute-done | bytes 1048608 | tf_op jit(solution)/shard_map/ppermute | solution.py:37
  44.1 3.3 %shard_map.119 = (f32[512,256]{1,0:T(8,128)S(1)}, f32[512,64]{1,0:T(8,128)S(1)}, f32[512,128]{1,0:T(8,128)S(1)}) custom-call(s32[17]{0:T(128)S(1)} %pad_add_fusion.table.place, bf16[1024,512]{1,0:T(8,128)(2,1)} %collective-permute-done.1.refs_0_, bf16[1024,512]{1,0:T(8,128)(2,1)} %collective-permute-done.8.refs_1_, f32[1,8192]{1,0:T(1,128)S(1)} %copy-done.5, ...), custom_call_target="tpu_custom_call" | custom-call | flops 5368709120 | bytes 7741440 | tf_op jit(solution)/shard_map/pallas_call | solution.py:51
  47.4 1.3 collective-permute-done.7.refs_0_
  48.7 3.0 %shard_map.120 = (f32[512,256]{1,0:T(8,128)S(1)}, f32[512,64]{1,0:T(8,128)S(1)}, f32[512,128]{1,0:T(8,128)S(1)}) custom-call(s32[17]{0:T(128)S(1)} %pad_add_fusion.table.place, bf16[1024,512]{1,0:T(8,128)(2,1)S(1)} %collective-permute-done.7.refs_0_, bf16[1024,512]{1,0:T(8,128)(2,1)} %collective-permute-done.5.refs_1_, f32[1,8192]{1,0:T(1,128)S(1)} %copy-done.5, ...), custom_call_target="tpu_custom_call" | custom-call | flops 5368709120 | bytes 7741440 | tf_op jit(solution)/shard_map/pallas_call | solution.py:51
  51.8 3.6 %collective-permute-done.6.refs_0_ = bf16[1024,512]{1,0:T(8,128)(2,1)S(1)} collective-permute-done((bf16[1024,512]{1,0:T(8,128)(2,1)}, bf16[1024,512]{1,0:T(8,128)(2,1)S(1)}, u32[]{:S(2)}, u32[]{:S(2)}) %collective-permute-start.6) | collective-permute-done | bytes 1048608 | tf_op jit(solution)/shard_map/ppermute | solution.py:37
  55.3 1.3 shard_map.121
  56.6 3.4 %collective-permute-done.2.refs_0_ = bf16[1024,512]{1,0:T(8,128)(2,1)S(1)} collective-permute-done((bf16[1024,512]{1,0:T(8,128)(2,1)}, bf16[1024,512]{1,0:T(8,128)(2,1)S(1)}, u32[]{:S(2)}, u32[]{:S(2)}) %collective-permute-start.2) | collective-permute-done | bytes 1048608 | tf_op jit(solution)/shard_map/ppermute | solution.py:37
  60.0 1.1 shard_map.122
  61.1 0.3 collective-permute-start.10
  61.4 4.4 %collective-permute-start.11 = (bf16[64,512]{1,0:T(8,128)(2,1)S(1)}, bf16[64,512]{1,0:T(8,128)(2,1)S(1)}, u32[]{:S(2)}, u32[]{:S(2)}) collective-permute-start(bf16[64,512]{1,0:T(8,128)(2,1)S(1)} %get-tuple-element.41.own), channel_id=1, source_target_pairs={{0,16},{1,17},{2,18},{3,19},{4,20},{5,21},{6,22},{7,23},{8,24},{9,... | collective-permute-start | bytes 196616 | tf_op jit(solution)/shard_map/ppermute | solution.py:37
  65.8 0.0 collective-permute-start.9
  65.8 0.0 copy-start
  65.8 0.0 copy-start.9
  65.8 0.0 copy-start.10
  65.8 1.1 shard_map.123.q
  66.9 0.3 collective-permute-done.10.two
  67.2 0.7 collective-permute-done.11.left
  67.8 2.4 %collective-permute-done.9.right = bf16[64,512]{1,0:T(8,128)(2,1)S(1)} collective-permute-done((bf16[64,512]{1,0:T(8,128)(2,1)S(1)}, bf16[64,512]{1,0:T(8,128)(2,1)S(1)}, u32[]{:S(2)}, u32[]{:S(2)}) %collective-permute-start.9) | collective-permute-done | bytes 65568 | tf_op jit(solution)/shard_map/ppermute | solution.py:37
  70.2 2.5 %shard_map.124 = (bf16[512,256]{1,0:T(8,128)(2,1)S(1)}, bf16[1024,512]{1,0:T(8,128)(2,1)S(1)}, bf16[1024,512]{1,0:T(8,128)(2,1)S(1)}) custom-call(s32[17]{0:T(128)S(1)} %pad_add_fusion.table.place, bf16[512,256]{1,0:T(8,128)(2,1)S(1)} %shard_map.123.q, bf16[64,512]{1,0:T(8,128)(2,1)S(1)} %get-tuple-element.41.own, ...), custom_call_target="tpu_custom_call" | custom-call | flops 402653184 | bytes 3407872 | tf_op jit(solution)/shard_map/pallas_call | solution.py:51
  72.7 0.2 collective-permute-start.16
  72.9 1.9 %collective-permute-start.12 = (bf16[1024,512]{1,0:T(8,128)(2,1)S(1)}, bf16[1024,512]{1,0:T(8,128)(2,1)S(1)}, u32[]{:S(2)}, u32[]{:S(2)}) collective-permute-start(bf16[1024,512]{1,0:T(8,128)(2,1)S(1)} %get-tuple-element.43), channel_id=1, source_target_pairs={{0,64},{1,17},{2,66},{3,19},{4,68},{5,21},{6,70},{7,23},{8,72},{9,... | collective-permute-start | bytes 3145736 | tf_op jit(solution)/shard_map/ppermute | solution.py:37
  74.8 1.3 shard_map.126
  76.1 1.4 collective-permute-start.14
  77.5 0.7 collective-permute-start.15
  78.2 9.4 %collective-permute-done.16.refs_2_ = bf16[1024,512]{1,0:T(8,128)(2,1)S(1)} collective-permute-done((bf16[1024,512]{1,0:T(8,128)(2,1)S(1)}, bf16[1024,512]{1,0:T(8,128)(2,1)S(1)}, u32[]{:S(2)}, u32[]{:S(2)}) %collective-permute-start.16) | collective-permute-done | bytes 1048608 | tf_op jit(solution)/shard_map/ppermute | solution.py:37
  87.6 1.0 shard_map.127
  88.6 1.4 collective-permute-start.17
  89.9 1.0 shard_map.125
  90.9 0.8 collective-permute-start.13
  91.8 7.1 %collective-permute-done.14.refs_5_ = bf16[1024,512]{1,0:T(8,128)(2,1)S(1)} collective-permute-done((bf16[1024,512]{1,0:T(8,128)(2,1)S(1)}, bf16[1024,512]{1,0:T(8,128)(2,1)S(1)}, u32[]{:S(2)}, u32[]{:S(2)}) %collective-permute-start.14) | collective-permute-done | bytes 1048608 | tf_op jit(solution)/shard_map/ppermute | solution.py:37
  98.8 1.3 collective-permute-done.15.refs_6_
  100.1 9.9 %collective-permute-done.17.refs_7_ = bf16[1024,512]{1,0:T(8,128)(2,1)S(1)} collective-permute-done((bf16[1024,512]{1,0:T(8,128)(2,1)S(1)}, bf16[1024,512]{1,0:T(8,128)(2,1)S(1)}, u32[]{:S(2)}, u32[]{:S(2)}) %collective-permute-start.17) | collective-permute-done | bytes 1048608 | tf_op jit(solution)/shard_map/ppermute | solution.py:37
  110.1 1.3 collective-permute-done.13.refs_4_
  111.4 1.5 %shard_map.128 = (f32[512,512]{1,0:T(8,128)S(1)}, bf16[512,512]{1,0:T(8,128)(2,1)S(1)}, bf16[512,512]{1,0:T(8,128)(2,1)S(1)}, bf16[512,512]{1,0:T(8,128)(2,1)S(1)}) custom-call(s32[17]{0:T(128)S(1)} %pad_add_fusion.table.place, bf16[512,256]{1,0:T(8,128)(2,1)S(1)} %get-tuple-element.42.context, bf16[256,8192]{1,0:T(8,128)(2,1)S(1)} %bitcast.25, ...), custom_call_target="tpu_custom_call" | custom-call | flops 536870912 | bytes 12058624 | tf_op jit(solution)/shard_map/pallas_call | solution.py:51
  112.9 1.6 %collective-permute-start.18 = (bf16[512,512]{1,0:T(8,128)(2,1)S(1)}, bf16[512,512]{1,0:T(8,128)(2,1)S(1)}, u32[]{:S(2)}, u32[]{:S(2)}) collective-permute-start(bf16[512,512]{1,0:T(8,128)(2,1)S(1)} %get-tuple-element.48), channel_id=1, source_target_pairs={{0,48},{1,193},{2,50},{3,195},{4,52},{5,197},{6,54},{7,199},{8,56}... | collective-permute-start | bytes 1572872 | tf_op jit(solution)/shard_map/ppermute | solution.py:37
  114.5 0.5 collective-permute-start.19
  115.0 1.4 collective-permute-start.20
  116.4 5.8 %collective-permute-done.18 = bf16[512,512]{1,0:T(8,128)(2,1)S(1)} collective-permute-done((bf16[512,512]{1,0:T(8,128)(2,1)S(1)}, bf16[512,512]{1,0:T(8,128)(2,1)S(1)}, u32[]{:S(2)}, u32[]{:S(2)}) %collective-permute-start.18) | collective-permute-done | bytes 524320 | tf_op jit(solution)/shard_map/ppermute | solution.py:37
  122.2 8.3 %collective-permute-done.19 = bf16[512,512]{1,0:T(8,128)(2,1)S(1)} collective-permute-done((bf16[512,512]{1,0:T(8,128)(2,1)S(1)}, bf16[512,512]{1,0:T(8,128)(2,1)S(1)}, u32[]{:S(2)}, u32[]{:S(2)}) %collective-permute-start.19) | collective-permute-done | bytes 524320 | tf_op jit(solution)/shard_map/ppermute | solution.py:37
  130.5 0.0 collective-permute-done.20
  130.5 0.3 add_convert_fusion
  130.8 0.0 collective-permute-start.21
  130.8 9.8 %collective-permute-done.21 = bf16[512,512]{1,0:T(8,128)(2,1)S(1)} collective-permute-done((bf16[512,512]{1,0:T(8,128)(2,1)S(1)}, bf16[512,512]{1,0:T(8,128)(2,1)S(1)}, u32[]{:S(2)}, u32[]{:S(2)}) %collective-permute-start.21) | collective-permute-done | bytes 524320 | tf_op jit(solution)/shard_map/ppermute | solution.py:301
  140.6 1.1 bitcast_convert_fusion
  (24 shorter events, 0.1 us)
Async XLA Ops:
  0.0 20.2 %copy-start.6 = (bf16[1,512,512]{2,1,0:T(8,128)(2,1)S(1)}, bf16[1,512,512]{2,1,0:T(8,128)(2,1)}, u32[]{:S(2)}) copy-start(bf16[1,512,512]{2,1,0:T(8,128)(2,1)} %param.12) | copy-start | bytes 1572868
  0.0 24.5 %copy-start.11 = (s32[16]{0:T(128)S(1)}, s32[16]{0:T(128)}, u32[]{:S(2)}) copy-start(s32[16]{0:T(128)} %constant.51.clone) | copy-start | bytes 196
  0.0 24.5 %copy-start.12 = (s32[16]{0:T(128)S(1)}, s32[16]{0:T(128)}, u32[]{:S(2)}) copy-start(s32[16]{0:T(128)} %constant.52.clone) | copy-start | bytes 196
  0.0 36.5 %copy-start.3 = (bf16[1,8192,32]{1,2,0:T(8,128)(2,1)S(1)}, bf16[1,8192,32]{1,2,0:T(8,128)(2,1)}, u32[]{:S(2)}) copy-start(bf16[1,8192,32]{1,2,0:T(8,128)(2,1)} %param.15) | copy-start | bytes 1572868
  0.0 36.5 %copy-start.4 = (bf16[1,8192,32]{1,2,0:T(8,128)(2,1)S(1)}, bf16[1,8192,32]{1,2,0:T(8,128)(2,1)}, u32[]{:S(2)}) copy-start(bf16[1,8192,32]{1,2,0:T(8,128)(2,1)} %param.16) | copy-start | bytes 1572868
  0.0 36.5 %copy-start.5 = (f32[1,8192]{1,0:T(1,128)S(1)}, f32[1,8192]{1,0:T(1,128)}, u32[]{:S(2)}) copy-start(f32[1,8192]{1,0:T(1,128)} %refs_3_.1) | copy-start | bytes 98308
  0.0 15.5 %collective-permute-start.3 = (bf16[512,512]{1,0:T(8,128)(2,1)}, bf16[512,512]{1,0:T(8,128)(2,1)S(1)}, u32[]{:S(2)}, u32[]{:S(2)}) collective-permute-start(bf16[512,512]{1,0:T(8,128)(2,1)} %bitcast.77), channel_id=1, source_target_pairs={{0,48},{1,193},{2,50},{3,195},{4,52},{5,197},{6,54},{7,199},{8,56}... | collective-permute-start | bytes 1572872 | tf_op jit(solution)/shard_map/ppermute | solution.py:37
  2.9 13.5 %collective-permute-start.4 = (bf16[512,512]{1,0:T(8,128)(2,1)}, bf16[512,512]{1,0:T(8,128)(2,1)S(1)}, u32[]{:S(2)}, u32[]{:S(2)}) collective-permute-start(bf16[512,512]{1,0:T(8,128)(2,1)} %bitcast.78), channel_id=1, source_target_pairs={{0,32},{1,129},{2,34},{3,131},{4,36},{5,133},{6,38},{7,135},{8,40}... | collective-permute-start | bytes 1572872 | tf_op jit(solution)/shard_map/ppermute | solution.py:37
  3.7 16.5 %collective-permute-start = (bf16[512,512]{1,0:T(8,128)(2,1)}, bf16[512,512]{1,0:T(8,128)(2,1)S(1)}, u32[]{:S(2)}, u32[]{:S(2)}) collective-permute-start(bf16[512,512]{1,0:T(8,128)(2,1)} %bitcast.79), channel_id=1, source_target_pairs={{0,16},{1,65},{2,18},{3,67},{4,20},{5,69},{6,22},{7,71},{8,24},{9,... | collective-permute-start | bytes 1572872 | tf_op jit(solution)/shard_map/ppermute | solution.py:37
  17.2 15.6 %collective-permute-start.5 = (bf16[1024,512]{1,0:T(8,128)(2,1)}, bf16[1024,512]{1,0:T(8,128)(2,1)}, u32[]{:S(2)}, u32[]{:S(2)}) collective-permute-start(bf16[1024,512]{1,0:T(8,128)(2,1)} %constant_dynamic-update-slice_fusion), channel_id=1, source_target_pairs={{0,192},{1,49},{2,194},{3,51},{4,196},{5,53},{6,198},{7,55},{8,200... | collective-permute-start | bytes 3145736 | tf_op jit(solution)/shard_map/ppermute | solution.py:37
  21.3 19.3 %collective-permute-start.1 = (bf16[1024,512]{1,0:T(8,128)(2,1)}, bf16[1024,512]{1,0:T(8,128)(2,1)}, u32[]{:S(2)}, u32[]{:S(2)}) collective-permute-start(bf16[1024,512]{1,0:T(8,128)(2,1)} %pad_maximum_fusion), channel_id=1, source_target_pairs={{0,64},{1,17},{2,66},{3,19},{4,68},{5,21},{6,70},{7,23},{8,72},{9,... | collective-permute-start | bytes 3145736 | tf_op jit(solution)/shard_map/ppermute | solution.py:37
  22.0 22.1 %collective-permute-start.8 = (bf16[1024,512]{1,0:T(8,128)(2,1)}, bf16[1024,512]{1,0:T(8,128)(2,1)}, u32[]{:S(2)}, u32[]{:S(2)}) collective-permute-start(bf16[1024,512]{1,0:T(8,128)(2,1)} %pad_maximum_fusion), channel_id=1, source_target_pairs={{0,192},{1,49},{2,194},{3,51},{4,196},{5,53},{6,198},{7,55},{8,200... | collective-permute-start | bytes 3145736 | tf_op jit(solution)/shard_map/ppermute | solution.py:37
  24.5 24.2 %collective-permute-start.7 = (bf16[1024,512]{1,0:T(8,128)(2,1)}, bf16[1024,512]{1,0:T(8,128)(2,1)S(1)}, u32[]{:S(2)}, u32[]{:S(2)}) collective-permute-start(bf16[1024,512]{1,0:T(8,128)(2,1)} %constant_dynamic-update-slice_fusion), channel_id=1, source_target_pairs={{0,64},{1,17},{2,66},{3,19},{4,68},{5,21},{6,70},{7,23},{8,72},{9,... | collective-permute-start | bytes 3145736 | tf_op jit(solution)/shard_map/ppermute | solution.py:37
  32.9 22.5 %collective-permute-start.6 = (bf16[1024,512]{1,0:T(8,128)(2,1)}, bf16[1024,512]{1,0:T(8,128)(2,1)S(1)}, u32[]{:S(2)}, u32[]{:S(2)}) collective-permute-start(bf16[1024,512]{1,0:T(8,128)(2,1)} %collective-permute-done.5.refs_1_), channel_id=1, source_target_pairs={{0,192},{1,49},{2,194},{3,51},{4,196},{5,53},{6,198},{7,55},{8,200... | collective-permute-start | bytes 3145736 | tf_op jit(solution)/shard_map/ppermute | solution.py:37
  36.6 2.2 %copy-start.1 = (bf16[1,8192,256]{2,1,0:T(8,128)(2,1)S(1)}, bf16[1,8192,256]{2,1,0:T(8,128)(2,1)}, u32[]{:S(2)}) copy-start(bf16[1,8192,256]{2,1,0:T(8,128)(2,1)} %param.14) | copy-start | bytes 12582916
  38.7 5.3 %copy-start.2 = (bf16[1,8192,256]{2,1,0:T(8,128)(2,1)S(1)}, bf16[1,8192,256]{2,1,0:T(8,128)(2,1)}, u32[]{:S(2)}) copy-start(bf16[1,8192,256]{2,1,0:T(8,128)(2,1)} %param.14) | copy-start | bytes 12582916
  40.5 19.4 %collective-permute-start.2 = (bf16[1024,512]{1,0:T(8,128)(2,1)}, bf16[1024,512]{1,0:T(8,128)(2,1)S(1)}, u32[]{:S(2)}, u32[]{:S(2)}) collective-permute-start(bf16[1024,512]{1,0:T(8,128)(2,1)} %collective-permute-done.1.refs_0_), channel_id=1, source_target_pairs={{0,64},{1,17},{2,66},{3,19},{4,68},{5,21},{6,70},{7,23},{8,72},{9,... | collective-permute-start | bytes 3145736 | tf_op jit(solution)/shard_map/ppermute | solution.py:37
  60.0 5.8 %copy-start.7 = (f32[512,128]{1,0:T(8,128)S(1)}, f32[512,128]{1,0:T(8,128)}, u32[]{:S(2)}) copy-start(f32[512,128]{1,0:T(8,128)} %constant.53.clone.refs_7_) | copy-start | bytes 786436
  60.0 5.8 %copy-start.8 = (f32[512,128]{1,0:T(8,128)S(1)}, f32[512,128]{1,0:T(8,128)}, u32[]{:S(2)}) copy-start(f32[512,128]{1,0:T(8,128)} %constant.54.clone.refs_8_) | copy-start | bytes 786436
  61.1 6.1 %collective-permute-start.10 = (bf16[64,512]{1,0:T(8,128)(2,1)S(1)}, bf16[64,512]{1,0:T(8,128)(2,1)S(1)}, u32[]{:S(2)}, u32[]{:S(2)}) collective-permute-start(bf16[64,512]{1,0:T(8,128)(2,1)S(1)} %get-tuple-element.41.own), channel_id=1, source_target_pairs={{0,32},{1,33},{2,34},{3,35},{4,36},{5,37},{6,38},{7,39},{8,40},{9,... | collective-permute-start | bytes 196616 | tf_op jit(solution)/shard_map/ppermute | solution.py:37
  61.4 6.5 %collective-permute-start.11 = (bf16[64,512]{1,0:T(8,128)(2,1)S(1)}, bf16[64,512]{1,0:T(8,128)(2,1)S(1)}, u32[]{:S(2)}, u32[]{:S(2)}) collective-permute-start(bf16[64,512]{1,0:T(8,128)(2,1)S(1)} %get-tuple-element.41.own), channel_id=1, source_target_pairs={{0,16},{1,17},{2,18},{3,19},{4,20},{5,21},{6,22},{7,23},{8,24},{9,... | collective-permute-start | bytes 196616 | tf_op jit(solution)/shard_map/ppermute | solution.py:37
  65.8 4.4 %collective-permute-start.9 = (bf16[64,512]{1,0:T(8,128)(2,1)S(1)}, bf16[64,512]{1,0:T(8,128)(2,1)S(1)}, u32[]{:S(2)}, u32[]{:S(2)}) collective-permute-start(bf16[64,512]{1,0:T(8,128)(2,1)S(1)} %get-tuple-element.41.own), channel_id=1, source_target_pairs={{0,48},{1,49},{2,50},{3,51},{4,52},{5,53},{6,54},{7,55},{8,56},{9,... | collective-permute-start | bytes 196616 | tf_op jit(solution)/shard_map/ppermute | solution.py:37
  65.8 4.4 %copy-start = (bf16[1,256,8192]{2,1,0:T(8,128)(2,1)S(1)}, bf16[1,256,8192]{2,1,0:T(8,128)(2,1)}, u32[]{:S(2)}) copy-start(bf16[1,256,8192]{2,1,0:T(8,128)(2,1)} %param.17) | copy-start | bytes 12582916
  65.8 4.4 %copy-start.9 = (f32[64,512]{1,0:T(8,128)S(1)}, f32[64,512]{1,0:T(8,128)}, u32[]{:S(2)}) copy-start(f32[64,512]{1,0:T(8,128)} %constant.55.clone.cosine) | copy-start | bytes 393220
  65.8 4.4 %copy-start.10 = (f32[64,512]{1,0:T(8,128)S(1)}, f32[64,512]{1,0:T(8,128)}, u32[]{:S(2)}) copy-start(f32[64,512]{1,0:T(8,128)} %constant.56.clone.sine) | copy-start | bytes 393220
  72.7 14.9 %collective-permute-start.16 = (bf16[1024,512]{1,0:T(8,128)(2,1)S(1)}, bf16[1024,512]{1,0:T(8,128)(2,1)S(1)}, u32[]{:S(2)}, u32[]{:S(2)}) collective-permute-start(bf16[1024,512]{1,0:T(8,128)(2,1)S(1)} %get-tuple-element.46), channel_id=1, source_target_pairs={{0,192},{1,49},{2,194},{3,51},{4,196},{5,53},{6,198},{7,55},{8,200... | collective-permute-start | bytes 3145736 | tf_op jit(solution)/shard_map/ppermute | solution.py:37
  72.9 17.1 %collective-permute-start.12 = (bf16[1024,512]{1,0:T(8,128)(2,1)S(1)}, bf16[1024,512]{1,0:T(8,128)(2,1)S(1)}, u32[]{:S(2)}, u32[]{:S(2)}) collective-permute-start(bf16[1024,512]{1,0:T(8,128)(2,1)S(1)} %get-tuple-element.43), channel_id=1, source_target_pairs={{0,64},{1,17},{2,66},{3,19},{4,68},{5,21},{6,70},{7,23},{8,72},{9,... | collective-permute-start | bytes 3145736 | tf_op jit(solution)/shard_map/ppermute | solution.py:37
  76.1 22.7 %collective-permute-start.14 = (bf16[1024,512]{1,0:T(8,128)(2,1)S(1)}, bf16[1024,512]{1,0:T(8,128)(2,1)S(1)}, u32[]{:S(2)}, u32[]{:S(2)}) collective-permute-start(bf16[1024,512]{1,0:T(8,128)(2,1)S(1)} %get-tuple-element.44), channel_id=1, source_target_pairs={{0,192},{1,49},{2,194},{3,51},{4,196},{5,53},{6,198},{7,55},{8,200... | collective-permute-start | bytes 3145736 | tf_op jit(solution)/shard_map/ppermute | solution.py:37
  77.5 22.7 %collective-permute-start.15 = (bf16[1024,512]{1,0:T(8,128)(2,1)S(1)}, bf16[1024,512]{1,0:T(8,128)(2,1)S(1)}, u32[]{:S(2)}, u32[]{:S(2)}) collective-permute-start(bf16[1024,512]{1,0:T(8,128)(2,1)S(1)} %get-tuple-element.45), channel_id=1, source_target_pairs={{0,64},{1,17},{2,66},{3,19},{4,68},{5,21},{6,70},{7,23},{8,72},{9,... | collective-permute-start | bytes 3145736 | tf_op jit(solution)/shard_map/ppermute | solution.py:37
  88.6 21.5 %collective-permute-start.17 = (bf16[1024,512]{1,0:T(8,128)(2,1)S(1)}, bf16[1024,512]{1,0:T(8,128)(2,1)S(1)}, u32[]{:S(2)}, u32[]{:S(2)}) collective-permute-start(bf16[1024,512]{1,0:T(8,128)(2,1)S(1)} %shard_map.127), channel_id=1, source_target_pairs={{0,192},{1,49},{2,194},{3,51},{4,196},{5,53},{6,198},{7,55},{8,200... | collective-permute-start | bytes 3145736 | tf_op jit(solution)/shard_map/ppermute | solution.py:37
  90.9 20.4 %collective-permute-start.13 = (bf16[1024,512]{1,0:T(8,128)(2,1)S(1)}, bf16[1024,512]{1,0:T(8,128)(2,1)S(1)}, u32[]{:S(2)}, u32[]{:S(2)}) collective-permute-start(bf16[1024,512]{1,0:T(8,128)(2,1)S(1)} %shard_map.125), channel_id=1, source_target_pairs={{0,64},{1,17},{2,66},{3,19},{4,68},{5,21},{6,70},{7,23},{8,72},{9,... | collective-permute-start | bytes 3145736 | tf_op jit(solution)/shard_map/ppermute | solution.py:37
  112.9 9.3 %collective-permute-start.18 = (bf16[512,512]{1,0:T(8,128)(2,1)S(1)}, bf16[512,512]{1,0:T(8,128)(2,1)S(1)}, u32[]{:S(2)}, u32[]{:S(2)}) collective-permute-start(bf16[512,512]{1,0:T(8,128)(2,1)S(1)} %get-tuple-element.48), channel_id=1, source_target_pairs={{0,48},{1,193},{2,50},{3,195},{4,52},{5,197},{6,54},{7,199},{8,56}... | collective-permute-start | bytes 1572872 | tf_op jit(solution)/shard_map/ppermute | solution.py:37
  114.5 16.0 %collective-permute-start.19 = (bf16[512,512]{1,0:T(8,128)(2,1)S(1)}, bf16[512,512]{1,0:T(8,128)(2,1)S(1)}, u32[]{:S(2)}, u32[]{:S(2)}) collective-permute-start(bf16[512,512]{1,0:T(8,128)(2,1)S(1)} %get-tuple-element.49), channel_id=1, source_target_pairs={{0,16},{1,65},{2,18},{3,67},{4,20},{5,69},{6,22},{7,71},{8,24},{9,... | collective-permute-start | bytes 1572872 | tf_op jit(solution)/shard_map/ppermute | solution.py:37
  115.0 15.5 %collective-permute-start.20 = (bf16[512,512]{1,0:T(8,128)(2,1)S(1)}, bf16[512,512]{1,0:T(8,128)(2,1)S(1)}, u32[]{:S(2)}, u32[]{:S(2)}) collective-permute-start(bf16[512,512]{1,0:T(8,128)(2,1)S(1)} %get-tuple-element.50), channel_id=1, source_target_pairs={{0,32},{1,129},{2,34},{3,131},{4,36},{5,133},{6,38},{7,135},{8,40}... | collective-permute-start | bytes 1572872 | tf_op jit(solution)/shard_map/ppermute | solution.py:37
  130.8 9.8 %collective-permute-start.21 = (bf16[512,512]{1,0:T(8,128)(2,1)S(1)}, bf16[512,512]{1,0:T(8,128)(2,1)S(1)}, u32[]{:S(2)}, u32[]{:S(2)}) collective-permute-start(bf16[512,512]{1,0:T(8,128)(2,1)S(1)} %add_convert_fusion), channel_id=1, source_target_pairs={{0,1},{1,2},{2,3},{3,4},{4,5},{5,6},{6,7},{7,8},{8,9},{9,10},{10,1... | collective-permute-start | bytes 1572872 | tf_op jit(solution)/shard_map/ppermute | solution.py:301

commit v5 on v4

--- a/solution.py
+++ b/solution.py
@@ -213,8 +213,9 @@
                 continue
             if residual:
                 value = value + residual.pop()[...].astype(jnp.float32)
-            alone = refs.pop(0)
-            alone[...] = value.astype(alone.dtype)
+            for h in range(2):
+                alone = refs.pop(0)
+                alone[...] = value[h * rows // 2 : (h + 1) * rows // 2].astype(alone.dtype)
 
 
 def project(context, wo, table, jobs, base=None):
@@ -227,11 +228,11 @@
             specs.append(pl.BlockSpec((depth, width), lambda i, t, k=k: (0, t[k])))
         count = len(job["places"])
         if job["apart"]:
-            outs += [((rows, width), jnp.bfloat16)] * count
+            outs += [((rows // 2, width), jnp.bfloat16)] * (2 * count)
         else:
             outs.append(((rows * count, width), jnp.bfloat16))
     if base is not None:
-        outs[0] = (outs[0][0], jnp.float32)
+        outs[:2] = [(outs[0][0], jnp.float32)] * 2
     more = [a for job in jobs for a in job["adds"]] + ([] if base is None else [base])
     args += more
     specs += [whole(a.shape) for a in more]
@@ -294,11 +295,15 @@
     one_up = shift(run([job(1, one, [up])])[0], LONG, 1)
     two_down = shift(run([job(-1, two, [down])])[0], LONG, -1)
     jobs = [job(0, one, [one_up, one_down], True), job(0, two, [two_up, two_down], True)]
-    mine, *others = run(jobs, own)
-    for d, block in zip(OFFSETS[1:], others):
-        mine = mine + shift(block, SHORT, d).astype(jnp.float32)
+    pieces = run(jobs, own)
     step = [(p, (p + 1) % SECTIONS) for p in range(SECTIONS)]
-    return lax.ppermute(mine.astype(jnp.bfloat16), "pp", step).astype(jnp.float32)[None]
+    results = []
+    for h in range(2):
+        mine, *others = pieces[h::2]
+        for d, block in zip(OFFSETS[1:], others):
+            mine = mine + shift(block, SHORT, d).astype(jnp.float32)
+        results.append(lax.ppermute(mine.astype(jnp.bfloat16), "pp", step).astype(jnp.float32))
+    return jnp.concatenate(results)[None]
 
 
 def solution(mesh):

time: 142 us -> 139 us (0.979)
  waiting for transfers between devices: 87.1 us -> 80.5 us
  starting transfers between devices: 29.2 us -> 32.8 us
    ppermute x21 -> x24, waiting for transfers between devices: 77.3 us -> 73.5 us  [shift(): return lax.ppermute(block, ('ty', 'tx', 'pp'), route(axis_of_core, step))]
    ppermute x21 -> x24, starting transfers between devices: 29.2 us -> 32.7 us  [shift(): return lax.ppermute(block, ('ty', 'tx', 'pp'), route(axis_of_core, step))]
    ppermute x1 -> x2, waiting for transfers between devices: 9.8 us -> 6.99 us  [on_device(): lax.ppermute(mine.astype(jnp.bfloat16), 'pp', step).astype(jnp.float32)]
  transfers between devices with their start and end apart: 22 -> 26, of which waited for: 17 -> 20; matrix products, arithmetic and copies ran while one was open for 2% -> 2% of each run, Pallas kernels for 10% -> 10%
where the time goes in v5:
time: 139 us
  waiting for transfers between devices  80.5 us (58%)
  starting transfers between devices  32.8 us (24%)
  Pallas kernels  18.9 us (14%)
  local copies, waits for them, and re-layouts  3.9 us (3%)
  other arithmetic  2.57 us (2%)
    ppermute x24, waiting for transfers between devices, shift(): return lax.ppermute(block, ('ty', 'tx', 'pp'), route(axis_of_core, step))  73.5 us
    ppermute x24, starting transfers between devices, shift(): return lax.ppermute(block, ('ty', 'tx', 'pp'), route(axis_of_core, step))  32.7 us
    pallas_call x11, Pallas kernels, call(): pl.pallas_call(kernel, out_shape=[jax.ShapeDtypeStruct(s, d) for s, d in...  18.9 us
    ppermute x2, waiting for transfers between devices, on_device(): lax.ppermute(mine.astype(jnp.bfloat16), 'pp', step).astype(jnp.float32)  6.99 us
    unnamed x27, local copies, waits for them, and re-layouts  3.06 us
  transfers between devices with their start and end apart: 26, of which 20 were waited for; matrix products, arithmetic and copies ran while one was open for 2% of the time, Pallas kernels for 10%

profile of v5, /device:TPU:128, one launch (start us, length us, event | category | flops | bytes accessed | tf_op | source)
XLA Modules:
  0.0 138.8 jit_solution(18069718767126039261)
XLA Ops:
  0.0 2.8 %collective-permute-start.3 = (bf16[512,512]{1,0:T(8,128)(2,1)}, bf16[512,512]{1,0:T(8,128)(2,1)S(1)}, u32[]{:S(2)}, u32[]{:S(2)}) collective-permute-start(bf16[512,512]{1,0:T(8,128)(2,1)} %bitcast.79), channel_id=1, source_target_pairs={{0,48},{1,193},{2,50},{3,195},{4,52},{5,197},{6,54},{7,199},{8,56}... | collective-permute-start | bytes 1572872 | tf_op jit(solution)/shard_map/ppermute | solution.py:37
  2.9 0.8 collective-permute-start.4
  3.7 0.9 collective-permute-start
  4.6 11.0 %collective-permute-done.3.refs_2_ = bf16[512,512]{1,0:T(8,128)(2,1)S(1)} collective-permute-done((bf16[512,512]{1,0:T(8,128)(2,1)}, bf16[512,512]{1,0:T(8,128)(2,1)S(1)}, u32[]{:S(2)}, u32[]{:S(2)}) %collective-permute-start.3) | collective-permute-done | bytes 524320 | tf_op jit(solution)/shard_map/ppermute | solution.py:37
  15.5 0.8 constant_dynamic-update-slice_fusion.1
  16.4 0.8 constant_dynamic-update-slice_fusion
  17.2 3.0 %collective-permute-start.5 = (bf16[1024,512]{1,0:T(8,128)(2,1)}, bf16[1024,512]{1,0:T(8,128)(2,1)}, u32[]{:S(2)}, u32[]{:S(2)}) collective-permute-start(bf16[1024,512]{1,0:T(8,128)(2,1)} %constant_dynamic-update-slice_fusion), channel_id=1, source_target_pairs={{0,192},{1,49},{2,194},{3,51},{4,196},{5,53},{6,198},{7,55},{8,200... | collective-permute-start | bytes 3145736 | tf_op jit(solution)/shard_map/ppermute | solution.py:37
  20.2 1.0 pad_maximum_fusion
  21.3 0.7 collective-permute-start.1
  22.0 2.5 %collective-permute-start.8 = (bf16[1024,512]{1,0:T(8,128)(2,1)}, bf16[1024,512]{1,0:T(8,128)(2,1)}, u32[]{:S(2)}, u32[]{:S(2)}) collective-permute-start(bf16[1024,512]{1,0:T(8,128)(2,1)} %pad_maximum_fusion), channel_id=1, source_target_pairs={{0,192},{1,49},{2,194},{3,51},{4,196},{5,53},{6,198},{7,55},{8,200... | collective-permute-start | bytes 3145736 | tf_op jit(solution)/shard_map/ppermute | solution.py:37
  24.5 0.1 collective-permute-start.7
  24.6 0.1 pad_add_fusion.table.place
  24.7 8.2 %collective-permute-done.5.refs_1_ = bf16[1024,512]{1,0:T(8,128)(2,1)} collective-permute-done((bf16[1024,512]{1,0:T(8,128)(2,1)}, bf16[1024,512]{1,0:T(8,128)(2,1)}, u32[]{:S(2)}, u32[]{:S(2)}) %collective-permute-start.5) | collective-permute-done | bytes 1048608 | tf_op jit(solution)/shard_map/ppermute | solution.py:37
  32.9 3.7 %collective-permute-start.6 = (bf16[1024,512]{1,0:T(8,128)(2,1)}, bf16[1024,512]{1,0:T(8,128)(2,1)S(1)}, u32[]{:S(2)}, u32[]{:S(2)}) collective-permute-start(bf16[1024,512]{1,0:T(8,128)(2,1)} %collective-permute-done.5.refs_1_), channel_id=1, source_target_pairs={{0,192},{1,49},{2,194},{3,51},{4,196},{5,53},{6,198},{7,55},{8,200... | collective-permute-start | bytes 3145736 | tf_op jit(solution)/shard_map/ppermute | solution.py:37
  36.6 2.2 %copy-done.1 = bf16[1,8192,256]{2,1,0:T(8,128)(2,1)S(1)} copy-done((bf16[1,8192,256]{2,1,0:T(8,128)(2,1)S(1)}, bf16[1,8192,256]{2,1,0:T(8,128)(2,1)}, u32[]{:S(2)}) %copy-start.1) | copy-done | bytes 4194328
  38.7 1.8 %shard_map.118 = (f32[512,256]{1,0:T(8,128)S(1)}, f32[512,64]{1,0:T(8,128)S(1)}, f32[512,128]{1,0:T(8,128)S(1)}) custom-call(s32[17]{0:T(128)S(1)} %pad_add_fusion.table.place, bf16[512,512]{1,0:T(8,128)(2,1)S(1)} %bitcast.83, bf16[512,512]{1,0:T(8,128)(2,1)S(1)} %collective-permute-done.refs_1_, bf16[512,512]{1,0:T(8,128)(2,1)S(1)} %collective-permute-done.3.refs_2_, ...), custom_call_target="tpu_custom_call" | custom-call | flops 5368709120 | bytes 6823936 | tf_op jit(solution)/shard_map/pallas_call | solution.py:51
  40.6 0.1 collective-permute-start.2
  40.6 3.4 %collective-permute-done.8.refs_1_ = bf16[1024,512]{1,0:T(8,128)(2,1)} collective-permute-done((bf16[1024,512]{1,0:T(8,128)(2,1)}, bf16[1024,512]{1,0:T(8,128)(2,1)}, u32[]{:S(2)}, u32[]{:S(2)}) %collective-permute-start.8) | collective-permute-done | bytes 1048608 | tf_op jit(solution)/shard_map/ppermute | solution.py:37
  44.1 3.3 %shard_map.119 = (f32[512,256]{1,0:T(8,128)S(1)}, f32[512,64]{1,0:T(8,128)S(1)}, f32[512,128]{1,0:T(8,128)S(1)}) custom-call(s32[17]{0:T(128)S(1)} %pad_add_fusion.table.place, bf16[1024,512]{1,0:T(8,128)(2,1)} %collective-permute-done.1.refs_0_, bf16[1024,512]{1,0:T(8,128)(2,1)} %collective-permute-done.8.refs_1_, f32[1,8192]{1,0:T(1,128)S(1)} %copy-done.5, ...), custom_call_target="tpu_custom_call" | custom-call | flops 5368709120 | bytes 7741440 | tf_op jit(solution)/shard_map/pallas_call | solution.py:51
  47.4 1.3 collective-permute-done.7.refs_0_
  48.7 3.0 %shard_map.120 = (f32[512,256]{1,0:T(8,128)S(1)}, f32[512,64]{1,0:T(8,128)S(1)}, f32[512,128]{1,0:T(8,128)S(1)}) custom-call(s32[17]{0:T(128)S(1)} %pad_add_fusion.table.place, bf16[1024,512]{1,0:T(8,128)(2,1)S(1)} %collective-permute-done.7.refs_0_, bf16[1024,512]{1,0:T(8,128)(2,1)} %collective-permute-done.5.refs_1_, f32[1,8192]{1,0:T(1,128)S(1)} %copy-done.5, ...), custom_call_target="tpu_custom_call" | custom-call | flops 5368709120 | bytes 7741440 | tf_op jit(solution)/shard_map/pallas_call | solution.py:51
  51.8 3.6 %collective-permute-done.6.refs_0_ = bf16[1024,512]{1,0:T(8,128)(2,1)S(1)} collective-permute-done((bf16[1024,512]{1,0:T(8,128)(2,1)}, bf16[1024,512]{1,0:T(8,128)(2,1)S(1)}, u32[]{:S(2)}, u32[]{:S(2)}) %collective-permute-start.6) | collective-permute-done | bytes 1048608 | tf_op jit(solution)/shard_map/ppermute | solution.py:37
  55.3 1.3 shard_map.121
  56.6 3.4 %collective-permute-done.2.refs_0_ = bf16[1024,512]{1,0:T(8,128)(2,1)S(1)} collective-permute-done((bf16[1024,512]{1,0:T(8,128)(2,1)}, bf16[1024,512]{1,0:T(8,128)(2,1)S(1)}, u32[]{:S(2)}, u32[]{:S(2)}) %collective-permute-start.2) | collective-permute-done | bytes 1048608 | tf_op jit(solution)/shard_map/ppermute | solution.py:37
  60.0 1.1 shard_map.122
  61.1 0.3 collective-permute-start.10
  61.4 4.4 %collective-permute-start.11 = (bf16[64,512]{1,0:T(8,128)(2,1)S(1)}, bf16[64,512]{1,0:T(8,128)(2,1)S(1)}, u32[]{:S(2)}, u32[]{:S(2)}) collective-permute-start(bf16[64,512]{1,0:T(8,128)(2,1)S(1)} %get-tuple-element.45.own), channel_id=1, source_target_pairs={{0,16},{1,17},{2,18},{3,19},{4,20},{5,21},{6,22},{7,23},{8,24},{9,... | collective-permute-start | bytes 196616 | tf_op jit(solution)/shard_map/ppermute | solution.py:37
  65.8 1.1 shard_map.123.q
  66.9 0.3 collective-permute-done.10.two
  67.2 0.7 collective-permute-done.11.left
  67.8 2.4 %collective-permute-done.9.right = bf16[64,512]{1,0:T(8,128)(2,1)S(1)} collective-permute-done((bf16[64,512]{1,0:T(8,128)(2,1)S(1)}, bf16[64,512]{1,0:T(8,128)(2,1)S(1)}, u32[]{:S(2)}, u32[]{:S(2)}) %collective-permute-start.9) | collective-permute-done | bytes 65568 | tf_op jit(solution)/shard_map/ppermute | solution.py:37
  70.2 2.5 %shard_map.124 = (bf16[512,256]{1,0:T(8,128)(2,1)S(1)}, bf16[1024,512]{1,0:T(8,128)(2,1)S(1)}, bf16[1024,512]{1,0:T(8,128)(2,1)S(1)}) custom-call(s32[17]{0:T(128)S(1)} %pad_add_fusion.table.place, bf16[512,256]{1,0:T(8,128)(2,1)S(1)} %shard_map.123.q, bf16[64,512]{1,0:T(8,128)(2,1)S(1)} %get-tuple-element.45.own, ...), custom_call_target="tpu_custom_call" | custom-call | flops 402653184 | bytes 3407872 | tf_op jit(solution)/shard_map/pallas_call | solution.py:51
  72.7 0.2 collective-permute-start.16
  72.9 2.0 %collective-permute-start.12 = (bf16[1024,512]{1,0:T(8,128)(2,1)S(1)}, bf16[1024,512]{1,0:T(8,128)(2,1)S(1)}, u32[]{:S(2)}, u32[]{:S(2)}) collective-permute-start(bf16[1024,512]{1,0:T(8,128)(2,1)S(1)} %get-tuple-element.47), channel_id=1, source_target_pairs={{0,64},{1,17},{2,66},{3,19},{4,68},{5,21},{6,70},{7,23},{8,72},{9,... | collective-permute-start | bytes 3145736 | tf_op jit(solution)/shard_map/ppermute | solution.py:37
  74.8 1.3 shard_map.126
  76.1 1.4 collective-permute-start.14
  77.5 0.7 collective-permute-start.15
  78.2 9.4 %collective-permute-done.16.refs_2_ = bf16[1024,512]{1,0:T(8,128)(2,1)S(1)} collective-permute-done((bf16[1024,512]{1,0:T(8,128)(2,1)S(1)}, bf16[1024,512]{1,0:T(8,128)(2,1)S(1)}, u32[]{:S(2)}, u32[]{:S(2)}) %collective-permute-start.16) | collective-permute-done | bytes 1048608 | tf_op jit(solution)/shard_map/ppermute | solution.py:37
  87.6 1.0 shard_map.127
  88.6 1.4 collective-permute-start.17
  89.9 1.0 shard_map.125
  90.9 0.8 collective-permute-start.13
  91.7 7.1 %collective-permute-done.14.refs_5_ = bf16[1024,512]{1,0:T(8,128)(2,1)S(1)} collective-permute-done((bf16[1024,512]{1,0:T(8,128)(2,1)S(1)}, bf16[1024,512]{1,0:T(8,128)(2,1)S(1)}, u32[]{:S(2)}, u32[]{:S(2)}) %collective-permute-start.14) | collective-permute-done | bytes 1048608 | tf_op jit(solution)/shard_map/ppermute | solution.py:37
  98.8 1.3 collective-permute-done.15.refs_6_
  100.1 9.9 %collective-permute-done.17.refs_7_ = bf16[1024,512]{1,0:T(8,128)(2,1)S(1)} collective-permute-done((bf16[1024,512]{1,0:T(8,128)(2,1)S(1)}, bf16[1024,512]{1,0:T(8,128)(2,1)S(1)}, u32[]{:S(2)}, u32[]{:S(2)}) %collective-permute-start.17) | collective-permute-done | bytes 1048608 | tf_op jit(solution)/shard_map/ppermute | solution.py:37
  110.1 1.3 collective-permute-done.13.refs_4_
  111.4 1.5 %shard_map.128 = (f32[256,512]{1,0:T(8,128)S(1)}, f32[256,512]{1,0:T(8,128)S(1)}, bf16[256,512]{1,0:T(8,128)(2,1)S(1)}, bf16[256,512]{1,0:T(8,128)(2,1)S(1)}, bf...) custom-call(s32[17]{0:T(128)S(1)} %pad_add_fusion.table.place, ...), custom_call_target="tpu_custom_call" | custom-call | flops 536870912 | bytes 12058624 | tf_op jit(solution)/shard_map/pallas_call | solution.py:51
  112.9 1.6 %collective-permute-start.18 = (bf16[256,512]{1,0:T(8,128)(2,1)S(1)}, bf16[256,512]{1,0:T(8,128)(2,1)S(1)}, u32[]{:S(2)}, u32[]{:S(2)}) collective-permute-start(bf16[256,512]{1,0:T(8,128)(2,1)S(1)} %get-tuple-element.52), channel_id=1, source_target_pairs={{0,48},{1,193},{2,50},{3,195},{4,52},{5,197},{6,54},{7,199},{8,56}... | collective-permute-start | bytes 786440 | tf_op jit(solution)/shard_map/ppermute | solution.py:37
  114.5 0.5 collective-permute-start.19
  115.0 1.4 collective-permute-start.20
  116.4 1.4 collective-permute-start.22
  117.7 0.9 collective-permute-start.23
  118.6 0.8 collective-permute-done.18
  119.4 1.4 collective-permute-start.24
  120.7 4.2 %collective-permute-done.19 = bf16[256,512]{1,0:T(8,128)(2,1)S(1)} collective-permute-done((bf16[256,512]{1,0:T(8,128)(2,1)S(1)}, bf16[256,512]{1,0:T(8,128)(2,1)S(1)}, u32[]{:S(2)}, u32[]{:S(2)}) %collective-permute-start.19) | collective-permute-done | bytes 262176 | tf_op jit(solution)/shard_map/ppermute | solution.py:37
  124.9 0.2 add_convert_fusion.1
  125.1 0.0 collective-permute-start.21
  125.1 0.7 collective-permute-done.22
  125.8 4.7 %collective-permute-done.23 = bf16[256,512]{1,0:T(8,128)(2,1)S(1)} collective-permute-done((bf16[256,512]{1,0:T(8,128)(2,1)S(1)}, bf16[256,512]{1,0:T(8,128)(2,1)S(1)}, u32[]{:S(2)}, u32[]{:S(2)}) %collective-permute-start.23) | collective-permute-done | bytes 262176 | tf_op jit(solution)/shard_map/ppermute | solution.py:37
  130.5 0.2 add_convert_fusion
  130.7 0.0 collective-permute-start.25
  130.7 1.4 collective-permute-done.21
  132.1 5.6 %collective-permute-done.25 = bf16[256,512]{1,0:T(8,128)(2,1)S(1)} collective-permute-done((bf16[256,512]{1,0:T(8,128)(2,1)S(1)}, bf16[256,512]{1,0:T(8,128)(2,1)S(1)}, u32[]{:S(2)}, u32[]{:S(2)}) %collective-permute-start.25) | collective-permute-done | bytes 262176 | tf_op jit(solution)/shard_map/ppermute | solution.py:305
  137.7 1.1 fusion
  (33 shorter events, 0.1 us)
Async XLA Ops:
  0.0 20.2 %copy-start.6 = (bf16[1,512,512]{2,1,0:T(8,128)(2,1)S(1)}, bf16[1,512,512]{2,1,0:T(8,128)(2,1)}, u32[]{:S(2)}) copy-start(bf16[1,512,512]{2,1,0:T(8,128)(2,1)} %param.12) | copy-start | bytes 1572868
  0.0 24.5 %copy-start.11 = (s32[16]{0:T(128)S(1)}, s32[16]{0:T(128)}, u32[]{:S(2)}) copy-start(s32[16]{0:T(128)} %constant.51.clone) | copy-start | bytes 196
  0.0 24.5 %copy-start.12 = (s32[16]{0:T(128)S(1)}, s32[16]{0:T(128)}, u32[]{:S(2)}) copy-start(s32[16]{0:T(128)} %constant.52.clone) | copy-start | bytes 196
  0.0 36.5 %copy-start.3 = (bf16[1,8192,32]{1,2,0:T(8,128)(2,1)S(1)}, bf16[1,8192,32]{1,2,0:T(8,128)(2,1)}, u32[]{:S(2)}) copy-start(bf16[1,8192,32]{1,2,0:T(8,128)(2,1)} %param.15) | copy-start | bytes 1572868
  0.0 36.5 %copy-start.4 = (bf16[1,8192,32]{1,2,0:T(8,128)(2,1)S(1)}, bf16[1,8192,32]{1,2,0:T(8,128)(2,1)}, u32[]{:S(2)}) copy-start(bf16[1,8192,32]{1,2,0:T(8,128)(2,1)} %param.16) | copy-start | bytes 1572868
  0.0 36.5 %copy-start.5 = (f32[1,8192]{1,0:T(1,128)S(1)}, f32[1,8192]{1,0:T(1,128)}, u32[]{:S(2)}) copy-start(f32[1,8192]{1,0:T(1,128)} %refs_3_.1) | copy-start | bytes 98308
  0.0 15.5 %collective-permute-start.3 = (bf16[512,512]{1,0:T(8,128)(2,1)}, bf16[512,512]{1,0:T(8,128)(2,1)S(1)}, u32[]{:S(2)}, u32[]{:S(2)}) collective-permute-start(bf16[512,512]{1,0:T(8,128)(2,1)} %bitcast.79), channel_id=1, source_target_pairs={{0,48},{1,193},{2,50},{3,195},{4,52},{5,197},{6,54},{7,199},{8,56}... | collective-permute-start | bytes 1572872 | tf_op jit(solution)/shard_map/ppermute | solution.py:37
  2.9 13.5 %collective-permute-start.4 = (bf16[512,512]{1,0:T(8,128)(2,1)}, bf16[512,512]{1,0:T(8,128)(2,1)S(1)}, u32[]{:S(2)}, u32[]{:S(2)}) collective-permute-start(bf16[512,512]{1,0:T(8,128)(2,1)} %bitcast.80), channel_id=1, source_target_pairs={{0,32},{1,129},{2,34},{3,131},{4,36},{5,133},{6,38},{7,135},{8,40}... | collective-permute-start | bytes 1572872 | tf_op jit(solution)/shard_map/ppermute | solution.py:37
  3.7 16.5 %collective-permute-start = (bf16[512,512]{1,0:T(8,128)(2,1)}, bf16[512,512]{1,0:T(8,128)(2,1)S(1)}, u32[]{:S(2)}, u32[]{:S(2)}) collective-permute-start(bf16[512,512]{1,0:T(8,128)(2,1)} %bitcast.81), channel_id=1, source_target_pairs={{0,16},{1,65},{2,18},{3,67},{4,20},{5,69},{6,22},{7,71},{8,24},{9,... | collective-permute-start | bytes 1572872 | tf_op jit(solution)/shard_map/ppermute | solution.py:37
  17.2 15.6 %collective-permute-start.5 = (bf16[1024,512]{1,0:T(8,128)(2,1)}, bf16[1024,512]{1,0:T(8,128)(2,1)}, u32[]{:S(2)}, u32[]{:S(2)}) collective-permute-start(bf16[1024,512]{1,0:T(8,128)(2,1)} %constant_dynamic-update-slice_fusion), channel_id=1, source_target_pairs={{0,192},{1,49},{2,194},{3,51},{4,196},{5,53},{6,198},{7,55},{8,200... | collective-permute-start | bytes 3145736 | tf_op jit(solution)/shard_map/ppermute | solution.py:37
  21.3 19.3 %collective-permute-start.1 = (bf16[1024,512]{1,0:T(8,128)(2,1)}, bf16[1024,512]{1,0:T(8,128)(2,1)}, u32[]{:S(2)}, u32[]{:S(2)}) collective-permute-start(bf16[1024,512]{1,0:T(8,128)(2,1)} %pad_maximum_fusion), channel_id=1, source_target_pairs={{0,64},{1,17},{2,66},{3,19},{4,68},{5,21},{6,70},{7,23},{8,72},{9,... | collective-permute-start | bytes 3145736 | tf_op jit(solution)/shard_map/ppermute | solution.py:37
  22.0 22.1 %collective-permute-start.8 = (bf16[1024,512]{1,0:T(8,128)(2,1)}, bf16[1024,512]{1,0:T(8,128)(2,1)}, u32[]{:S(2)}, u32[]{:S(2)}) collective-permute-start(bf16[1024,512]{1,0:T(8,128)(2,1)} %pad_maximum_fusion), channel_id=1, source_target_pairs={{0,192},{1,49},{2,194},{3,51},{4,196},{5,53},{6,198},{7,55},{8,200... | collective-permute-start | bytes 3145736 | tf_op jit(solution)/shard_map/ppermute | solution.py:37
  24.5 24.2 %collective-permute-start.7 = (bf16[1024,512]{1,0:T(8,128)(2,1)}, bf16[1024,512]{1,0:T(8,128)(2,1)S(1)}, u32[]{:S(2)}, u32[]{:S(2)}) collective-permute-start(bf16[1024,512]{1,0:T(8,128)(2,1)} %constant_dynamic-update-slice_fusion), channel_id=1, source_target_pairs={{0,64},{1,17},{2,66},{3,19},{4,68},{5,21},{6,70},{7,23},{8,72},{9,... | collective-permute-start | bytes 3145736 | tf_op jit(solution)/shard_map/ppermute | solution.py:37
  32.9 22.5 %collective-permute-start.6 = (bf16[1024,512]{1,0:T(8,128)(2,1)}, bf16[1024,512]{1,0:T(8,128)(2,1)S(1)}, u32[]{:S(2)}, u32[]{:S(2)}) collective-permute-start(bf16[1024,512]{1,0:T(8,128)(2,1)} %collective-permute-done.5.refs_1_), channel_id=1, source_target_pairs={{0,192},{1,49},{2,194},{3,51},{4,196},{5,53},{6,198},{7,55},{8,200... | collective-permute-start | bytes 3145736 | tf_op jit(solution)/shard_map/ppermute | solution.py:37
  36.6 2.2 %copy-start.1 = (bf16[1,8192,256]{2,1,0:T(8,128)(2,1)S(1)}, bf16[1,8192,256]{2,1,0:T(8,128)(2,1)}, u32[]{:S(2)}) copy-start(bf16[1,8192,256]{2,1,0:T(8,128)(2,1)} %param.14) | copy-start | bytes 12582916
  38.7 5.3 %copy-start.2 = (bf16[1,8192,256]{2,1,0:T(8,128)(2,1)S(1)}, bf16[1,8192,256]{2,1,0:T(8,128)(2,1)}, u32[]{:S(2)}) copy-start(bf16[1,8192,256]{2,1,0:T(8,128)(2,1)} %param.14) | copy-start | bytes 12582916
  40.6 19.4 %collective-permute-start.2 = (bf16[1024,512]{1,0:T(8,128)(2,1)}, bf16[1024,512]{1,0:T(8,128)(2,1)S(1)}, u32[]{:S(2)}, u32[]{:S(2)}) collective-permute-start(bf16[1024,512]{1,0:T(8,128)(2,1)} %collective-permute-done.1.refs_0_), channel_id=1, source_target_pairs={{0,64},{1,17},{2,66},{3,19},{4,68},{5,21},{6,70},{7,23},{8,72},{9,... | collective-permute-start | bytes 3145736 | tf_op jit(solution)/shard_map/ppermute | solution.py:37
  60.0 5.8 %copy-start.7 = (f32[512,128]{1,0:T(8,128)S(1)}, f32[512,128]{1,0:T(8,128)}, u32[]{:S(2)}) copy-start(f32[512,128]{1,0:T(8,128)} %constant.53.clone.refs_7_) | copy-start | bytes 786436
  60.0 5.8 %copy-start.8 = (f32[512,128]{1,0:T(8,128)S(1)}, f32[512,128]{1,0:T(8,128)}, u32[]{:S(2)}) copy-start(f32[512,128]{1,0:T(8,128)} %constant.54.clone.refs_8_) | copy-start | bytes 786436
  61.1 6.1 %collective-permute-start.10 = (bf16[64,512]{1,0:T(8,128)(2,1)S(1)}, bf16[64,512]{1,0:T(8,128)(2,1)S(1)}, u32[]{:S(2)}, u32[]{:S(2)}) collective-permute-start(bf16[64,512]{1,0:T(8,128)(2,1)S(1)} %get-tuple-element.45.own), channel_id=1, source_target_pairs={{0,32},{1,33},{2,34},{3,35},{4,36},{5,37},{6,38},{7,39},{8,40},{9,... | collective-permute-start | bytes 196616 | tf_op jit(solution)/shard_map/ppermute | solution.py:37
  61.4 6.5 %collective-permute-start.11 = (bf16[64,512]{1,0:T(8,128)(2,1)S(1)}, bf16[64,512]{1,0:T(8,128)(2,1)S(1)}, u32[]{:S(2)}, u32[]{:S(2)}) collective-permute-start(bf16[64,512]{1,0:T(8,128)(2,1)S(1)} %get-tuple-element.45.own), channel_id=1, source_target_pairs={{0,16},{1,17},{2,18},{3,19},{4,20},{5,21},{6,22},{7,23},{8,24},{9,... | collective-permute-start | bytes 196616 | tf_op jit(solution)/shard_map/ppermute | solution.py:37
  65.8 4.4 %collective-permute-start.9 = (bf16[64,512]{1,0:T(8,128)(2,1)S(1)}, bf16[64,512]{1,0:T(8,128)(2,1)S(1)}, u32[]{:S(2)}, u32[]{:S(2)}) collective-permute-start(bf16[64,512]{1,0:T(8,128)(2,1)S(1)} %get-tuple-element.45.own), channel_id=1, source_target_pairs={{0,48},{1,49},{2,50},{3,51},{4,52},{5,53},{6,54},{7,55},{8,56},{9,... | collective-permute-start | bytes 196616 | tf_op jit(solution)/shard_map/ppermute | solution.py:37
  65.8 4.4 %copy-start = (bf16[1,256,8192]{2,1,0:T(8,128)(2,1)S(1)}, bf16[1,256,8192]{2,1,0:T(8,128)(2,1)}, u32[]{:S(2)}) copy-start(bf16[1,256,8192]{2,1,0:T(8,128)(2,1)} %param.17) | copy-start | bytes 12582916
  65.8 4.4 %copy-start.9 = (f32[64,512]{1,0:T(8,128)S(1)}, f32[64,512]{1,0:T(8,128)}, u32[]{:S(2)}) copy-start(f32[64,512]{1,0:T(8,128)} %constant.55.clone.cosine) | copy-start | bytes 393220
  65.8 4.4 %copy-start.10 = (f32[64,512]{1,0:T(8,128)S(1)}, f32[64,512]{1,0:T(8,128)}, u32[]{:S(2)}) copy-start(f32[64,512]{1,0:T(8,128)} %constant.56.clone.sine) | copy-start | bytes 393220
  72.7 14.9 %collective-permute-start.16 = (bf16[1024,512]{1,0:T(8,128)(2,1)S(1)}, bf16[1024,512]{1,0:T(8,128)(2,1)S(1)}, u32[]{:S(2)}, u32[]{:S(2)}) collective-permute-start(bf16[1024,512]{1,0:T(8,128)(2,1)S(1)} %get-tuple-element.50), channel_id=1, source_target_pairs={{0,192},{1,49},{2,194},{3,51},{4,196},{5,53},{6,198},{7,55},{8,200... | collective-permute-start | bytes 3145736 | tf_op jit(solution)/shard_map/ppermute | solution.py:37
  72.9 17.1 %collective-permute-start.12 = (bf16[1024,512]{1,0:T(8,128)(2,1)S(1)}, bf16[1024,512]{1,0:T(8,128)(2,1)S(1)}, u32[]{:S(2)}, u32[]{:S(2)}) collective-permute-start(bf16[1024,512]{1,0:T(8,128)(2,1)S(1)} %get-tuple-element.47), channel_id=1, source_target_pairs={{0,64},{1,17},{2,66},{3,19},{4,68},{5,21},{6,70},{7,23},{8,72},{9,... | collective-permute-start | bytes 3145736 | tf_op jit(solution)/shard_map/ppermute | solution.py:37
  76.1 22.7 %collective-permute-start.14 = (bf16[1024,512]{1,0:T(8,128)(2,1)S(1)}, bf16[1024,512]{1,0:T(8,128)(2,1)S(1)}, u32[]{:S(2)}, u32[]{:S(2)}) collective-permute-start(bf16[1024,512]{1,0:T(8,128)(2,1)S(1)} %get-tuple-element.48), channel_id=1, source_target_pairs={{0,192},{1,49},{2,194},{3,51},{4,196},{5,53},{6,198},{7,55},{8,200... | collective-permute-start | bytes 3145736 | tf_op jit(solution)/shard_map/ppermute | solution.py:37
  77.5 22.7 %collective-permute-start.15 = (bf16[1024,512]{1,0:T(8,128)(2,1)S(1)}, bf16[1024,512]{1,0:T(8,128)(2,1)S(1)}, u32[]{:S(2)}, u32[]{:S(2)}) collective-permute-start(bf16[1024,512]{1,0:T(8,128)(2,1)S(1)} %get-tuple-element.49), channel_id=1, source_target_pairs={{0,64},{1,17},{2,66},{3,19},{4,68},{5,21},{6,70},{7,23},{8,72},{9,... | collective-permute-start | bytes 3145736 | tf_op jit(solution)/shard_map/ppermute | solution.py:37
  88.6 21.5 %collective-permute-start.17 = (bf16[1024,512]{1,0:T(8,128)(2,1)S(1)}, bf16[1024,512]{1,0:T(8,128)(2,1)S(1)}, u32[]{:S(2)}, u32[]{:S(2)}) collective-permute-start(bf16[1024,512]{1,0:T(8,128)(2,1)S(1)} %shard_map.127), channel_id=1, source_target_pairs={{0,192},{1,49},{2,194},{3,51},{4,196},{5,53},{6,198},{7,55},{8,200... | collective-permute-start | bytes 3145736 | tf_op jit(solution)/shard_map/ppermute | solution.py:37
  90.9 20.4 %collective-permute-start.13 = (bf16[1024,512]{1,0:T(8,128)(2,1)S(1)}, bf16[1024,512]{1,0:T(8,128)(2,1)S(1)}, u32[]{:S(2)}, u32[]{:S(2)}) collective-permute-start(bf16[1024,512]{1,0:T(8,128)(2,1)S(1)} %shard_map.125), channel_id=1, source_target_pairs={{0,64},{1,17},{2,66},{3,19},{4,68},{5,21},{6,70},{7,23},{8,72},{9,... | collective-permute-start | bytes 3145736 | tf_op jit(solution)/shard_map/ppermute | solution.py:37
  112.9 6.5 %collective-permute-start.18 = (bf16[256,512]{1,0:T(8,128)(2,1)S(1)}, bf16[256,512]{1,0:T(8,128)(2,1)S(1)}, u32[]{:S(2)}, u32[]{:S(2)}) collective-permute-start(bf16[256,512]{1,0:T(8,128)(2,1)S(1)} %get-tuple-element.52), channel_id=1, source_target_pairs={{0,48},{1,193},{2,50},{3,195},{4,52},{5,197},{6,54},{7,199},{8,56}... | collective-permute-start | bytes 786440 | tf_op jit(solution)/shard_map/ppermute | solution.py:37
  114.5 10.4 %collective-permute-start.19 = (bf16[256,512]{1,0:T(8,128)(2,1)S(1)}, bf16[256,512]{1,0:T(8,128)(2,1)S(1)}, u32[]{:S(2)}, u32[]{:S(2)}) collective-permute-start(bf16[256,512]{1,0:T(8,128)(2,1)S(1)} %get-tuple-element.53), channel_id=1, source_target_pairs={{0,16},{1,65},{2,18},{3,67},{4,20},{5,69},{6,22},{7,71},{8,24},{9,... | collective-permute-start | bytes 786440 | tf_op jit(solution)/shard_map/ppermute | solution.py:37
  115.0 9.9 %collective-permute-start.20 = (bf16[256,512]{1,0:T(8,128)(2,1)S(1)}, bf16[256,512]{1,0:T(8,128)(2,1)S(1)}, u32[]{:S(2)}, u32[]{:S(2)}) collective-permute-start(bf16[256,512]{1,0:T(8,128)(2,1)S(1)} %get-tuple-element.54), channel_id=1, source_target_pairs={{0,32},{1,129},{2,34},{3,131},{4,36},{5,133},{6,38},{7,135},{8,40}... | collective-permute-start | bytes 786440 | tf_op jit(solution)/shard_map/ppermute | solution.py:37
  116.4 9.4 %collective-permute-start.22 = (bf16[256,512]{1,0:T(8,128)(2,1)S(1)}, bf16[256,512]{1,0:T(8,128)(2,1)S(1)}, u32[]{:S(2)}, u32[]{:S(2)}) collective-permute-start(bf16[256,512]{1,0:T(8,128)(2,1)S(1)} %get-tuple-element.56), channel_id=1, source_target_pairs={{0,48},{1,193},{2,50},{3,195},{4,52},{5,197},{6,54},{7,199},{8,56}... | collective-permute-start | bytes 786440 | tf_op jit(solution)/shard_map/ppermute | solution.py:37
  117.7 12.8 %collective-permute-start.23 = (bf16[256,512]{1,0:T(8,128)(2,1)S(1)}, bf16[256,512]{1,0:T(8,128)(2,1)S(1)}, u32[]{:S(2)}, u32[]{:S(2)}) collective-permute-start(bf16[256,512]{1,0:T(8,128)(2,1)S(1)} %get-tuple-element.57), channel_id=1, source_target_pairs={{0,16},{1,65},{2,18},{3,67},{4,20},{5,69},{6,22},{7,71},{8,24},{9,... | collective-permute-start | bytes 786440 | tf_op jit(solution)/shard_map/ppermute | solution.py:37
  119.4 11.2 %collective-permute-start.24 = (bf16[256,512]{1,0:T(8,128)(2,1)S(1)}, bf16[256,512]{1,0:T(8,128)(2,1)S(1)}, u32[]{:S(2)}, u32[]{:S(2)}) collective-permute-start(bf16[256,512]{1,0:T(8,128)(2,1)S(1)} %get-tuple-element.58), channel_id=1, source_target_pairs={{0,32},{1,129},{2,34},{3,131},{4,36},{5,133},{6,38},{7,135},{8,40}... | collective-permute-start | bytes 786440 | tf_op jit(solution)/shard_map/ppermute | solution.py:37
  125.1 7.0 %collective-permute-start.21 = (bf16[256,512]{1,0:T(8,128)(2,1)S(1)}, bf16[256,512]{1,0:T(8,128)(2,1)S(1)}, u32[]{:S(2)}, u32[]{:S(2)}) collective-permute-start(bf16[256,512]{1,0:T(8,128)(2,1)S(1)} %add_convert_fusion.1), channel_id=1, source_target_pairs={{0,1},{1,2},{2,3},{3,4},{4,5},{5,6},{6,7},{7,8},{8,9},{9,10},{10,1... | collective-permute-start | bytes 786440 | tf_op jit(solution)/shard_map/ppermute | solution.py:305
  130.7 7.0 %collective-permute-start.25 = (bf16[256,512]{1,0:T(8,128)(2,1)S(1)}, bf16[256,512]{1,0:T(8,128)(2,1)S(1)}, u32[]{:S(2)}, u32[]{:S(2)}) collective-permute-start(bf16[256,512]{1,0:T(8,128)(2,1)S(1)} %add_convert_fusion), channel_id=1, source_target_pairs={{0,1},{1,2},{2,3},{3,4},{4,5},{5,6},{6,7},{7,8},{8,9},{9,10},{10,1... | collective-permute-start | bytes 786440 | tf_op jit(solution)/shard_map/ppermute | solution.py:305

commit v6 on v5

--- a/solution.py
+++ b/solution.py
@@ -213,9 +213,12 @@
                 continue
             if residual:
                 value = value + residual.pop()[...].astype(jnp.float32)
-            for h in range(2):
+            begin = 0
+            for _ in range(2):
                 alone = refs.pop(0)
-                alone[...] = value[h * rows // 2 : (h + 1) * rows // 2].astype(alone.dtype)
+                end = begin + alone.shape[0]
+                alone[...] = value[begin:end].astype(alone.dtype)
+                begin = end
 
 
 def project(context, wo, table, jobs, base=None):
@@ -228,11 +231,12 @@
             specs.append(pl.BlockSpec((depth, width), lambda i, t, k=k: (0, t[k])))
         count = len(job["places"])
         if job["apart"]:
-            outs += [((rows // 2, width), jnp.bfloat16)] * (2 * count)
+            cuts = (rows * 5 // 8, rows * 3 // 8)
+            outs += [((cut, width), jnp.bfloat16) for cut in cuts] * count
         else:
             outs.append(((rows * count, width), jnp.bfloat16))
     if base is not None:
-        outs[:2] = [(outs[0][0], jnp.float32)] * 2
+        outs[:2] = [(shape, jnp.float32) for shape, _ in outs[:2]]
     more = [a for job in jobs for a in job["adds"]] + ([] if base is None else [base])
     args += more
     specs += [whole(a.shape) for a in more]

time: 139 us -> 138 us (level)
  transfers between devices with their start and end apart: 26 -> 26, of which waited for: 20 -> 18; matrix products, arithmetic and copies ran while one was open for 2% -> 2% of each run, Pallas kernels for 10% -> 10%
where the time goes in v6:
time: 138 us
  waiting for transfers between devices  79.8 us (58%)
  starting transfers between devices  32.8 us (24%)
  Pallas kernels  18.9 us (14%)
  local copies, waits for them, and re-layouts  3.9 us (3%)
  other arithmetic  2.51 us (2%)
    ppermute x24, waiting for transfers between devices, shift(): return lax.ppermute(block, ('ty', 'tx', 'pp'), route(axis_of_core, step))  73.5 us
    ppermute x24, starting transfers between devices, shift(): return lax.ppermute(block, ('ty', 'tx', 'pp'), route(axis_of_core, step))  32.7 us
    pallas_call x11, Pallas kernels, call(): pl.pallas_call(kernel, out_shape=[jax.ShapeDtypeStruct(s, d) for s, d in...  18.9 us
    ppermute x2, waiting for transfers between devices, on_device(): lax.ppermute(mine.astype(jnp.bfloat16), 'pp', step).astype(jnp.float32)  6.29 us
    unnamed x27, local copies, waits for them, and re-layouts  3.06 us
  transfers between devices with their start and end apart: 26, of which 18 were waited for; matrix products, arithmetic and copies ran while one was open for 2% of the time, Pallas kernels for 10%

profile of v6, /device:TPU:128, one launch (start us, length us, event | category | flops | bytes accessed | tf_op | source)
XLA Modules:
  0.0 138.0 jit_solution(6073231092485880938)
XLA Ops:
  0.0 2.8 %collective-permute-start.3 = (bf16[512,512]{1,0:T(8,128)(2,1)}, bf16[512,512]{1,0:T(8,128)(2,1)S(1)}, u32[]{:S(2)}, u32[]{:S(2)}) collective-permute-start(bf16[512,512]{1,0:T(8,128)(2,1)} %bitcast.79), channel_id=1, source_target_pairs={{0,48},{1,193},{2,50},{3,195},{4,52},{5,197},{6,54},{7,199},{8,56}... | collective-permute-start | bytes 1572872 | tf_op jit(solution)/shard_map/ppermute | solution.py:37
  2.9 0.8 collective-permute-start.4
  3.7 0.9 collective-permute-start
  4.6 11.0 %collective-permute-done.3.refs_2_ = bf16[512,512]{1,0:T(8,128)(2,1)S(1)} collective-permute-done((bf16[512,512]{1,0:T(8,128)(2,1)}, bf16[512,512]{1,0:T(8,128)(2,1)S(1)}, u32[]{:S(2)}, u32[]{:S(2)}) %collective-permute-start.3) | collective-permute-done | bytes 524320 | tf_op jit(solution)/shard_map/ppermute | solution.py:37
  15.5 0.8 constant_dynamic-update-slice_fusion.1
  16.4 0.8 constant_dynamic-update-slice_fusion
  17.2 3.0 %collective-permute-start.5 = (bf16[1024,512]{1,0:T(8,128)(2,1)}, bf16[1024,512]{1,0:T(8,128)(2,1)}, u32[]{:S(2)}, u32[]{:S(2)}) collective-permute-start(bf16[1024,512]{1,0:T(8,128)(2,1)} %constant_dynamic-update-slice_fusion), channel_id=1, source_target_pairs={{0,192},{1,49},{2,194},{3,51},{4,196},{5,53},{6,198},{7,55},{8,200... | collective-permute-start | bytes 3145736 | tf_op jit(solution)/shard_map/ppermute | solution.py:37
  20.2 1.0 pad_maximum_fusion
  21.3 0.7 collective-permute-start.1
  22.0 2.5 %collective-permute-start.8 = (bf16[1024,512]{1,0:T(8,128)(2,1)}, bf16[1024,512]{1,0:T(8,128)(2,1)}, u32[]{:S(2)}, u32[]{:S(2)}) collective-permute-start(bf16[1024,512]{1,0:T(8,128)(2,1)} %pad_maximum_fusion), channel_id=1, source_target_pairs={{0,192},{1,49},{2,194},{3,51},{4,196},{5,53},{6,198},{7,55},{8,200... | collective-permute-start | bytes 3145736 | tf_op jit(solution)/shard_map/ppermute | solution.py:37
  24.5 0.1 collective-permute-start.7
  24.6 0.1 pad_add_fusion.table.place
  24.7 8.2 %collective-permute-done.5.refs_1_ = bf16[1024,512]{1,0:T(8,128)(2,1)} collective-permute-done((bf16[1024,512]{1,0:T(8,128)(2,1)}, bf16[1024,512]{1,0:T(8,128)(2,1)}, u32[]{:S(2)}, u32[]{:S(2)}) %collective-permute-start.5) | collective-permute-done | bytes 1048608 | tf_op jit(solution)/shard_map/ppermute | solution.py:37
  32.9 3.7 %collective-permute-start.6 = (bf16[1024,512]{1,0:T(8,128)(2,1)}, bf16[1024,512]{1,0:T(8,128)(2,1)S(1)}, u32[]{:S(2)}, u32[]{:S(2)}) collective-permute-start(bf16[1024,512]{1,0:T(8,128)(2,1)} %collective-permute-done.5.refs_1_), channel_id=1, source_target_pairs={{0,192},{1,49},{2,194},{3,51},{4,196},{5,53},{6,198},{7,55},{8,200... | collective-permute-start | bytes 3145736 | tf_op jit(solution)/shard_map/ppermute | solution.py:37
  36.6 2.2 %copy-done.1 = bf16[1,8192,256]{2,1,0:T(8,128)(2,1)S(1)} copy-done((bf16[1,8192,256]{2,1,0:T(8,128)(2,1)S(1)}, bf16[1,8192,256]{2,1,0:T(8,128)(2,1)}, u32[]{:S(2)}) %copy-start.1) | copy-done | bytes 4194328
  38.7 1.8 %shard_map.118 = (f32[512,256]{1,0:T(8,128)S(1)}, f32[512,64]{1,0:T(8,128)S(1)}, f32[512,128]{1,0:T(8,128)S(1)}) custom-call(s32[17]{0:T(128)S(1)} %pad_add_fusion.table.place, bf16[512,512]{1,0:T(8,128)(2,1)S(1)} %bitcast.83, bf16[512,512]{1,0:T(8,128)(2,1)S(1)} %collective-permute-done.refs_1_, bf16[512,512]{1,0:T(8,128)(2,1)S(1)} %collective-permute-done.3.refs_2_, ...), custom_call_target="tpu_custom_call" | custom-call | flops 5368709120 | bytes 6823936 | tf_op jit(solution)/shard_map/pallas_call | solution.py:51
  40.6 0.1 collective-permute-start.2
  40.6 3.4 %collective-permute-done.8.refs_1_ = bf16[1024,512]{1,0:T(8,128)(2,1)} collective-permute-done((bf16[1024,512]{1,0:T(8,128)(2,1)}, bf16[1024,512]{1,0:T(8,128)(2,1)}, u32[]{:S(2)}, u32[]{:S(2)}) %collective-permute-start.8) | collective-permute-done | bytes 1048608 | tf_op jit(solution)/shard_map/ppermute | solution.py:37
  44.1 3.3 %shard_map.119 = (f32[512,256]{1,0:T(8,128)S(1)}, f32[512,64]{1,0:T(8,128)S(1)}, f32[512,128]{1,0:T(8,128)S(1)}) custom-call(s32[17]{0:T(128)S(1)} %pad_add_fusion.table.place, bf16[1024,512]{1,0:T(8,128)(2,1)} %collective-permute-done.1.refs_0_, bf16[1024,512]{1,0:T(8,128)(2,1)} %collective-permute-done.8.refs_1_, f32[1,8192]{1,0:T(1,128)S(1)} %copy-done.5, ...), custom_call_target="tpu_custom_call" | custom-call | flops 5368709120 | bytes 7741440 | tf_op jit(solution)/shard_map/pallas_call | solution.py:51
  47.4 1.3 collective-permute-done.7.refs_0_
  48.7 3.0 %shard_map.120 = (f32[512,256]{1,0:T(8,128)S(1)}, f32[512,64]{1,0:T(8,128)S(1)}, f32[512,128]{1,0:T(8,128)S(1)}) custom-call(s32[17]{0:T(128)S(1)} %pad_add_fusion.table.place, bf16[1024,512]{1,0:T(8,128)(2,1)S(1)} %collective-permute-done.7.refs_0_, bf16[1024,512]{1,0:T(8,128)(2,1)} %collective-permute-done.5.refs_1_, f32[1,8192]{1,0:T(1,128)S(1)} %copy-done.5, ...), custom_call_target="tpu_custom_call" | custom-call | flops 5368709120 | bytes 7741440 | tf_op jit(solution)/shard_map/pallas_call | solution.py:51
  51.8 3.6 %collective-permute-done.6.refs_0_ = bf16[1024,512]{1,0:T(8,128)(2,1)S(1)} collective-permute-done((bf16[1024,512]{1,0:T(8,128)(2,1)}, bf16[1024,512]{1,0:T(8,128)(2,1)S(1)}, u32[]{:S(2)}, u32[]{:S(2)}) %collective-permute-start.6) | collective-permute-done | bytes 1048608 | tf_op jit(solution)/shard_map/ppermute | solution.py:37
  55.3 1.3 shard_map.121
  56.6 3.4 %collective-permute-done.2.refs_0_ = bf16[1024,512]{1,0:T(8,128)(2,1)S(1)} collective-permute-done((bf16[1024,512]{1,0:T(8,128)(2,1)}, bf16[1024,512]{1,0:T(8,128)(2,1)S(1)}, u32[]{:S(2)}, u32[]{:S(2)}) %collective-permute-start.2) | collective-permute-done | bytes 1048608 | tf_op jit(solution)/shard_map/ppermute | solution.py:37
  60.0 1.1 shard_map.122
  61.1 0.3 collective-permute-start.10
  61.4 4.4 %collective-permute-start.11 = (bf16[64,512]{1,0:T(8,128)(2,1)S(1)}, bf16[64,512]{1,0:T(8,128)(2,1)S(1)}, u32[]{:S(2)}, u32[]{:S(2)}) collective-permute-start(bf16[64,512]{1,0:T(8,128)(2,1)S(1)} %get-tuple-element.45.own), channel_id=1, source_target_pairs={{0,16},{1,17},{2,18},{3,19},{4,20},{5,21},{6,22},{7,23},{8,24},{9,... | collective-permute-start | bytes 196616 | tf_op jit(solution)/shard_map/ppermute | solution.py:37
  65.8 0.0 copy-start.9
  65.8 0.0 copy-start.10
  65.8 1.1 shard_map.123.q
  66.9 0.3 collective-permute-done.10.two
  67.2 0.7 collective-permute-done.11.left
  67.8 2.4 %collective-permute-done.9.right = bf16[64,512]{1,0:T(8,128)(2,1)S(1)} collective-permute-done((bf16[64,512]{1,0:T(8,128)(2,1)S(1)}, bf16[64,512]{1,0:T(8,128)(2,1)S(1)}, u32[]{:S(2)}, u32[]{:S(2)}) %collective-permute-start.9) | collective-permute-done | bytes 65568 | tf_op jit(solution)/shard_map/ppermute | solution.py:37
  70.2 2.5 %shard_map.124 = (bf16[512,256]{1,0:T(8,128)(2,1)S(1)}, bf16[1024,512]{1,0:T(8,128)(2,1)S(1)}, bf16[1024,512]{1,0:T(8,128)(2,1)S(1)}) custom-call(s32[17]{0:T(128)S(1)} %pad_add_fusion.table.place, bf16[512,256]{1,0:T(8,128)(2,1)S(1)} %shard_map.123.q, bf16[64,512]{1,0:T(8,128)(2,1)S(1)} %get-tuple-element.45.own, ...), custom_call_target="tpu_custom_call" | custom-call | flops 402653184 | bytes 3407872 | tf_op jit(solution)/shard_map/pallas_call | solution.py:51
  72.7 0.2 collective-permute-start.16
  72.9 2.0 %collective-permute-start.12 = (bf16[1024,512]{1,0:T(8,128)(2,1)S(1)}, bf16[1024,512]{1,0:T(8,128)(2,1)S(1)}, u32[]{:S(2)}, u32[]{:S(2)}) collective-permute-start(bf16[1024,512]{1,0:T(8,128)(2,1)S(1)} %get-tuple-element.47), channel_id=1, source_target_pairs={{0,64},{1,17},{2,66},{3,19},{4,68},{5,21},{6,70},{7,23},{8,72},{9,... | collective-permute-start | bytes 3145736 | tf_op jit(solution)/shard_map/ppermute | solution.py:37
  74.8 1.3 shard_map.126
  76.1 1.4 collective-permute-start.14
  77.5 0.7 collective-permute-start.15
  78.2 9.4 %collective-permute-done.16.refs_2_ = bf16[1024,512]{1,0:T(8,128)(2,1)S(1)} collective-permute-done((bf16[1024,512]{1,0:T(8,128)(2,1)S(1)}, bf16[1024,512]{1,0:T(8,128)(2,1)S(1)}, u32[]{:S(2)}, u32[]{:S(2)}) %collective-permute-start.16) | collective-permute-done | bytes 1048608 | tf_op jit(solution)/shard_map/ppermute | solution.py:37
  87.6 1.0 shard_map.127
  88.6 1.4 collective-permute-start.17
  89.9 1.0 shard_map.125
  90.9 0.8 collective-permute-start.13
  91.7 7.1 %collective-permute-done.14.refs_5_ = bf16[1024,512]{1,0:T(8,128)(2,1)S(1)} collective-permute-done((bf16[1024,512]{1,0:T(8,128)(2,1)S(1)}, bf16[1024,512]{1,0:T(8,128)(2,1)S(1)}, u32[]{:S(2)}, u32[]{:S(2)}) %collective-permute-start.14) | collective-permute-done | bytes 1048608 | tf_op jit(solution)/shard_map/ppermute | solution.py:37
  98.8 1.3 collective-permute-done.15.refs_6_
  100.1 9.9 %collective-permute-done.17.refs_7_ = bf16[1024,512]{1,0:T(8,128)(2,1)S(1)} collective-permute-done((bf16[1024,512]{1,0:T(8,128)(2,1)S(1)}, bf16[1024,512]{1,0:T(8,128)(2,1)S(1)}, u32[]{:S(2)}, u32[]{:S(2)}) %collective-permute-start.17) | collective-permute-done | bytes 1048608 | tf_op jit(solution)/shard_map/ppermute | solution.py:37
  110.1 1.3 collective-permute-done.13.refs_4_
  111.4 1.5 %shard_map.128 = (f32[320,512]{1,0:T(8,128)S(1)}, f32[192,512]{1,0:T(8,128)S(1)}, bf16[320,512]{1,0:T(8,128)(2,1)S(1)}, bf16[192,512]{1,0:T(8,128)(2,1)S(1)}, bf...) custom-call(s32[17]{0:T(128)S(1)} %pad_add_fusion.table.place, ...), custom_call_target="tpu_custom_call" | custom-call | flops 536870912 | bytes 12058624 | tf_op jit(solution)/shard_map/pallas_call | solution.py:51
  112.9 1.6 %collective-permute-start.18 = (bf16[320,512]{1,0:T(8,128)(2,1)S(1)}, bf16[320,512]{1,0:T(8,128)(2,1)S(1)}, u32[]{:S(2)}, u32[]{:S(2)}) collective-permute-start(bf16[320,512]{1,0:T(8,128)(2,1)S(1)} %get-tuple-element.52), channel_id=1, source_target_pairs={{0,48},{1,193},{2,50},{3,195},{4,52},{5,197},{6,54},{7,199},{8,56}... | collective-permute-start | bytes 983048 | tf_op jit(solution)/shard_map/ppermute | solution.py:37
  114.5 0.5 collective-permute-start.19
  115.0 1.4 collective-permute-start.20
  116.4 1.4 collective-permute-start.22
  117.7 0.9 collective-permute-start.23
  118.6 1.5 %collective-permute-done.18 = bf16[320,512]{1,0:T(8,128)(2,1)S(1)} collective-permute-done((bf16[320,512]{1,0:T(8,128)(2,1)S(1)}, bf16[320,512]{1,0:T(8,128)(2,1)S(1)}, u32[]{:S(2)}, u32[]{:S(2)}) %collective-permute-start.18) | collective-permute-done | bytes 327712 | tf_op jit(solution)/shard_map/ppermute | solution.py:37
  120.1 1.4 collective-permute-start.24
  121.4 4.9 %collective-permute-done.19 = bf16[320,512]{1,0:T(8,128)(2,1)S(1)} collective-permute-done((bf16[320,512]{1,0:T(8,128)(2,1)S(1)}, bf16[320,512]{1,0:T(8,128)(2,1)S(1)}, u32[]{:S(2)}, u32[]{:S(2)}) %collective-permute-start.19) | collective-permute-done | bytes 327712 | tf_op jit(solution)/shard_map/ppermute | solution.py:37
  126.3 0.2 add_convert_fusion
  126.5 0.0 collective-permute-start.21
  126.5 4.0 %collective-permute-done.23 = bf16[192,512]{1,0:T(8,128)(2,1)S(1)} collective-permute-done((bf16[192,512]{1,0:T(8,128)(2,1)S(1)}, bf16[192,512]{1,0:T(8,128)(2,1)S(1)}, u32[]{:S(2)}, u32[]{:S(2)}) %collective-permute-start.23) | collective-permute-done | bytes 196640 | tf_op jit(solution)/shard_map/ppermute | solution.py:37
  130.5 0.1 add_convert_fusion.1
  130.6 0.0 collective-permute-start.25
  130.6 6.3 %collective-permute-done.25 = bf16[192,512]{1,0:T(8,128)(2,1)S(1)} collective-permute-done((bf16[192,512]{1,0:T(8,128)(2,1)S(1)}, bf16[192,512]{1,0:T(8,128)(2,1)S(1)}, u32[]{:S(2)}, u32[]{:S(2)}) %collective-permute-start.25) | collective-permute-done | bytes 196640 | tf_op jit(solution)/shard_map/ppermute | solution.py:309
  136.9 1.1 fusion
  (33 shorter events, 0.1 us)
Async XLA Ops:
  0.0 20.2 %copy-start.6 = (bf16[1,512,512]{2,1,0:T(8,128)(2,1)S(1)}, bf16[1,512,512]{2,1,0:T(8,128)(2,1)}, u32[]{:S(2)}) copy-start(bf16[1,512,512]{2,1,0:T(8,128)(2,1)} %param.12) | copy-start | bytes 1572868
  0.0 24.5 %copy-start.11 = (s32[16]{0:T(128)S(1)}, s32[16]{0:T(128)}, u32[]{:S(2)}) copy-start(s32[16]{0:T(128)} %constant.51.clone) | copy-start | bytes 196
  0.0 24.5 %copy-start.12 = (s32[16]{0:T(128)S(1)}, s32[16]{0:T(128)}, u32[]{:S(2)}) copy-start(s32[16]{0:T(128)} %constant.52.clone) | copy-start | bytes 196
  0.0 36.5 %copy-start.3 = (bf16[1,8192,32]{1,2,0:T(8,128)(2,1)S(1)}, bf16[1,8192,32]{1,2,0:T(8,128)(2,1)}, u32[]{:S(2)}) copy-start(bf16[1,8192,32]{1,2,0:T(8,128)(2,1)} %param.15) | copy-start | bytes 1572868
  0.0 36.5 %copy-start.4 = (bf16[1,8192,32]{1,2,0:T(8,128)(2,1)S(1)}, bf16[1,8192,32]{1,2,0:T(8,128)(2,1)}, u32[]{:S(2)}) copy-start(bf16[1,8192,32]{1,2,0:T(8,128)(2,1)} %param.16) | copy-start | bytes 1572868
  0.0 36.5 %copy-start.5 = (f32[1,8192]{1,0:T(1,128)S(1)}, f32[1,8192]{1,0:T(1,128)}, u32[]{:S(2)}) copy-start(f32[1,8192]{1,0:T(1,128)} %refs_3_.1) | copy-start | bytes 98308
  0.0 15.5 %collective-permute-start.3 = (bf16[512,512]{1,0:T(8,128)(2,1)}, bf16[512,512]{1,0:T(8,128)(2,1)S(1)}, u32[]{:S(2)}, u32[]{:S(2)}) collective-permute-start(bf16[512,512]{1,0:T(8,128)(2,1)} %bitcast.79), channel_id=1, source_target_pairs={{0,48},{1,193},{2,50},{3,195},{4,52},{5,197},{6,54},{7,199},{8,56}... | collective-permute-start | bytes 1572872 | tf_op jit(solution)/shard_map/ppermute | solution.py:37
  2.9 13.5 %collective-permute-start.4 = (bf16[512,512]{1,0:T(8,128)(2,1)}, bf16[512,512]{1,0:T(8,128)(2,1)S(1)}, u32[]{:S(2)}, u32[]{:S(2)}) collective-permute-start(bf16[512,512]{1,0:T(8,128)(2,1)} %bitcast.80), channel_id=1, source_target_pairs={{0,32},{1,129},{2,34},{3,131},{4,36},{5,133},{6,38},{7,135},{8,40}... | collective-permute-start | bytes 1572872 | tf_op jit(solution)/shard_map/ppermute | solution.py:37
  3.7 16.5 %collective-permute-start = (bf16[512,512]{1,0:T(8,128)(2,1)}, bf16[512,512]{1,0:T(8,128)(2,1)S(1)}, u32[]{:S(2)}, u32[]{:S(2)}) collective-permute-start(bf16[512,512]{1,0:T(8,128)(2,1)} %bitcast.81), channel_id=1, source_target_pairs={{0,16},{1,65},{2,18},{3,67},{4,20},{5,69},{6,22},{7,71},{8,24},{9,... | collective-permute-start | bytes 1572872 | tf_op jit(solution)/shard_map/ppermute | solution.py:37
  17.2 15.6 %collective-permute-start.5 = (bf16[1024,512]{1,0:T(8,128)(2,1)}, bf16[1024,512]{1,0:T(8,128)(2,1)}, u32[]{:S(2)}, u32[]{:S(2)}) collective-permute-start(bf16[1024,512]{1,0:T(8,128)(2,1)} %constant_dynamic-update-slice_fusion), channel_id=1, source_target_pairs={{0,192},{1,49},{2,194},{3,51},{4,196},{5,53},{6,198},{7,55},{8,200... | collective-permute-start | bytes 3145736 | tf_op jit(solution)/shard_map/ppermute | solution.py:37
  21.3 19.3 %collective-permute-start.1 = (bf16[1024,512]{1,0:T(8,128)(2,1)}, bf16[1024,512]{1,0:T(8,128)(2,1)}, u32[]{:S(2)}, u32[]{:S(2)}) collective-permute-start(bf16[1024,512]{1,0:T(8,128)(2,1)} %pad_maximum_fusion), channel_id=1, source_target_pairs={{0,64},{1,17},{2,66},{3,19},{4,68},{5,21},{6,70},{7,23},{8,72},{9,... | collective-permute-start | bytes 3145736 | tf_op jit(solution)/shard_map/ppermute | solution.py:37
  22.0 22.1 %collective-permute-start.8 = (bf16[1024,512]{1,0:T(8,128)(2,1)}, bf16[1024,512]{1,0:T(8,128)(2,1)}, u32[]{:S(2)}, u32[]{:S(2)}) collective-permute-start(bf16[1024,512]{1,0:T(8,128)(2,1)} %pad_maximum_fusion), channel_id=1, source_target_pairs={{0,192},{1,49},{2,194},{3,51},{4,196},{5,53},{6,198},{7,55},{8,200... | collective-permute-start | bytes 3145736 | tf_op jit(solution)/shard_map/ppermute | solution.py:37
  24.5 24.2 %collective-permute-start.7 = (bf16[1024,512]{1,0:T(8,128)(2,1)}, bf16[1024,512]{1,0:T(8,128)(2,1)S(1)}, u32[]{:S(2)}, u32[]{:S(2)}) collective-permute-start(bf16[1024,512]{1,0:T(8,128)(2,1)} %constant_dynamic-update-slice_fusion), channel_id=1, source_target_pairs={{0,64},{1,17},{2,66},{3,19},{4,68},{5,21},{6,70},{7,23},{8,72},{9,... | collective-permute-start | bytes 3145736 | tf_op jit(solution)/shard_map/ppermute | solution.py:37
  32.9 22.5 %collective-permute-start.6 = (bf16[1024,512]{1,0:T(8,128)(2,1)}, bf16[1024,512]{1,0:T(8,128)(2,1)S(1)}, u32[]{:S(2)}, u32[]{:S(2)}) collective-permute-start(bf16[1024,512]{1,0:T(8,128)(2,1)} %collective-permute-done.5.refs_1_), channel_id=1, source_target_pairs={{0,192},{1,49},{2,194},{3,51},{4,196},{5,53},{6,198},{7,55},{8,200... | collective-permute-start | bytes 3145736 | tf_op jit(solution)/shard_map/ppermute | solution.py:37
  36.6 2.2 %copy-start.1 = (bf16[1,8192,256]{2,1,0:T(8,128)(2,1)S(1)}, bf16[1,8192,256]{2,1,0:T(8,128)(2,1)}, u32[]{:S(2)}) copy-start(bf16[1,8192,256]{2,1,0:T(8,128)(2,1)} %param.14) | copy-start | bytes 12582916
  38.7 5.3 %copy-start.2 = (bf16[1,8192,256]{2,1,0:T(8,128)(2,1)S(1)}, bf16[1,8192,256]{2,1,0:T(8,128)(2,1)}, u32[]{:S(2)}) copy-start(bf16[1,8192,256]{2,1,0:T(8,128)(2,1)} %param.14) | copy-start | bytes 12582916
  40.6 19.4 %collective-permute-start.2 = (bf16[1024,512]{1,0:T(8,128)(2,1)}, bf16[1024,512]{1,0:T(8,128)(2,1)S(1)}, u32[]{:S(2)}, u32[]{:S(2)}) collective-permute-start(bf16[1024,512]{1,0:T(8,128)(2,1)} %collective-permute-done.1.refs_0_), channel_id=1, source_target_pairs={{0,64},{1,17},{2,66},{3,19},{4,68},{5,21},{6,70},{7,23},{8,72},{9,... | collective-permute-start | bytes 3145736 | tf_op jit(solution)/shard_map/ppermute | solution.py:37
  60.0 5.8 %copy-start.7 = (f32[512,128]{1,0:T(8,128)S(1)}, f32[512,128]{1,0:T(8,128)}, u32[]{:S(2)}) copy-start(f32[512,128]{1,0:T(8,128)} %constant.53.clone.refs_7_) | copy-start | bytes 786436
  60.0 5.8 %copy-start.8 = (f32[512,128]{1,0:T(8,128)S(1)}, f32[512,128]{1,0:T(8,128)}, u32[]{:S(2)}) copy-start(f32[512,128]{1,0:T(8,128)} %constant.54.clone.refs_8_) | copy-start | bytes 786436
  61.1 6.1 %collective-permute-start.10 = (bf16[64,512]{1,0:T(8,128)(2,1)S(1)}, bf16[64,512]{1,0:T(8,128)(2,1)S(1)}, u32[]{:S(2)}, u32[]{:S(2)}) collective-permute-start(bf16[64,512]{1,0:T(8,128)(2,1)S(1)} %get-tuple-element.45.own), channel_id=1, source_target_pairs={{0,32},{1,33},{2,34},{3,35},{4,36},{5,37},{6,38},{7,39},{8,40},{9,... | collective-permute-start | bytes 196616 | tf_op jit(solution)/shard_map/ppermute | solution.py:37
  61.4 6.5 %collective-permute-start.11 = (bf16[64,512]{1,0:T(8,128)(2,1)S(1)}, bf16[64,512]{1,0:T(8,128)(2,1)S(1)}, u32[]{:S(2)}, u32[]{:S(2)}) collective-permute-start(bf16[64,512]{1,0:T(8,128)(2,1)S(1)} %get-tuple-element.45.own), channel_id=1, source_target_pairs={{0,16},{1,17},{2,18},{3,19},{4,20},{5,21},{6,22},{7,23},{8,24},{9,... | collective-permute-start | bytes 196616 | tf_op jit(solution)/shard_map/ppermute | solution.py:37
  65.8 4.4 %collective-permute-start.9 = (bf16[64,512]{1,0:T(8,128)(2,1)S(1)}, bf16[64,512]{1,0:T(8,128)(2,1)S(1)}, u32[]{:S(2)}, u32[]{:S(2)}) collective-permute-start(bf16[64,512]{1,0:T(8,128)(2,1)S(1)} %get-tuple-element.45.own), channel_id=1, source_target_pairs={{0,48},{1,49},{2,50},{3,51},{4,52},{5,53},{6,54},{7,55},{8,56},{9,... | collective-permute-start | bytes 196616 | tf_op jit(solution)/shard_map/ppermute | solution.py:37
  65.8 4.4 %copy-start = (bf16[1,256,8192]{2,1,0:T(8,128)(2,1)S(1)}, bf16[1,256,8192]{2,1,0:T(8,128)(2,1)}, u32[]{:S(2)}) copy-start(bf16[1,256,8192]{2,1,0:T(8,128)(2,1)} %param.17) | copy-start | bytes 12582916
  65.8 4.4 %copy-start.9 = (f32[64,512]{1,0:T(8,128)S(1)}, f32[64,512]{1,0:T(8,128)}, u32[]{:S(2)}) copy-start(f32[64,512]{1,0:T(8,128)} %constant.55.clone.cosine) | copy-start | bytes 393220
  65.8 4.4 %copy-start.10 = (f32[64,512]{1,0:T(8,128)S(1)}, f32[64,512]{1,0:T(8,128)}, u32[]{:S(2)}) copy-start(f32[64,512]{1,0:T(8,128)} %constant.56.clone.sine) | copy-start | bytes 393220
  72.7 14.9 %collective-permute-start.16 = (bf16[1024,512]{1,0:T(8,128)(2,1)S(1)}, bf16[1024,512]{1,0:T(8,128)(2,1)S(1)}, u32[]{:S(2)}, u32[]{:S(2)}) collective-permute-start(bf16[1024,512]{1,0:T(8,128)(2,1)S(1)} %get-tuple-element.50), channel_id=1, source_target_pairs={{0,192},{1,49},{2,194},{3,51},{4,196},{5,53},{6,198},{7,55},{8,200... | collective-permute-start | bytes 3145736 | tf_op jit(solution)/shard_map/ppermute | solution.py:37
  72.9 17.1 %collective-permute-start.12 = (bf16[1024,512]{1,0:T(8,128)(2,1)S(1)}, bf16[1024,512]{1,0:T(8,128)(2,1)S(1)}, u32[]{:S(2)}, u32[]{:S(2)}) collective-permute-start(bf16[1024,512]{1,0:T(8,128)(2,1)S(1)} %get-tuple-element.47), channel_id=1, source_target_pairs={{0,64},{1,17},{2,66},{3,19},{4,68},{5,21},{6,70},{7,23},{8,72},{9,... | collective-permute-start | bytes 3145736 | tf_op jit(solution)/shard_map/ppermute | solution.py:37
  76.1 22.7 %collective-permute-start.14 = (bf16[1024,512]{1,0:T(8,128)(2,1)S(1)}, bf16[1024,512]{1,0:T(8,128)(2,1)S(1)}, u32[]{:S(2)}, u32[]{:S(2)}) collective-permute-start(bf16[1024,512]{1,0:T(8,128)(2,1)S(1)} %get-tuple-element.48), channel_id=1, source_target_pairs={{0,192},{1,49},{2,194},{3,51},{4,196},{5,53},{6,198},{7,55},{8,200... | collective-permute-start | bytes 3145736 | tf_op jit(solution)/shard_map/ppermute | solution.py:37
  77.5 22.7 %collective-permute-start.15 = (bf16[1024,512]{1,0:T(8,128)(2,1)S(1)}, bf16[1024,512]{1,0:T(8,128)(2,1)S(1)}, u32[]{:S(2)}, u32[]{:S(2)}) collective-permute-start(bf16[1024,512]{1,0:T(8,128)(2,1)S(1)} %get-tuple-element.49), channel_id=1, source_target_pairs={{0,64},{1,17},{2,66},{3,19},{4,68},{5,21},{6,70},{7,23},{8,72},{9,... | collective-permute-start | bytes 3145736 | tf_op jit(solution)/shard_map/ppermute | solution.py:37
  88.6 21.5 %collective-permute-start.17 = (bf16[1024,512]{1,0:T(8,128)(2,1)S(1)}, bf16[1024,512]{1,0:T(8,128)(2,1)S(1)}, u32[]{:S(2)}, u32[]{:S(2)}) collective-permute-start(bf16[1024,512]{1,0:T(8,128)(2,1)S(1)} %shard_map.127), channel_id=1, source_target_pairs={{0,192},{1,49},{2,194},{3,51},{4,196},{5,53},{6,198},{7,55},{8,200... | collective-permute-start | bytes 3145736 | tf_op jit(solution)/shard_map/ppermute | solution.py:37
  90.9 20.4 %collective-permute-start.13 = (bf16[1024,512]{1,0:T(8,128)(2,1)S(1)}, bf16[1024,512]{1,0:T(8,128)(2,1)S(1)}, u32[]{:S(2)}, u32[]{:S(2)}) collective-permute-start(bf16[1024,512]{1,0:T(8,128)(2,1)S(1)} %shard_map.125), channel_id=1, source_target_pairs={{0,64},{1,17},{2,66},{3,19},{4,68},{5,21},{6,70},{7,23},{8,72},{9,... | collective-permute-start | bytes 3145736 | tf_op jit(solution)/shard_map/ppermute | solution.py:37
  112.9 7.2 %collective-permute-start.18 = (bf16[320,512]{1,0:T(8,128)(2,1)S(1)}, bf16[320,512]{1,0:T(8,128)(2,1)S(1)}, u32[]{:S(2)}, u32[]{:S(2)}) collective-permute-start(bf16[320,512]{1,0:T(8,128)(2,1)S(1)} %get-tuple-element.52), channel_id=1, source_target_pairs={{0,48},{1,193},{2,50},{3,195},{4,52},{5,197},{6,54},{7,199},{8,56}... | collective-permute-start | bytes 983048 | tf_op jit(solution)/shard_map/ppermute | solution.py:37
  114.5 11.8 %collective-permute-start.19 = (bf16[320,512]{1,0:T(8,128)(2,1)S(1)}, bf16[320,512]{1,0:T(8,128)(2,1)S(1)}, u32[]{:S(2)}, u32[]{:S(2)}) collective-permute-start(bf16[320,512]{1,0:T(8,128)(2,1)S(1)} %get-tuple-element.53), channel_id=1, source_target_pairs={{0,16},{1,65},{2,18},{3,67},{4,20},{5,69},{6,22},{7,71},{8,24},{9,... | collective-permute-start | bytes 983048 | tf_op jit(solution)/shard_map/ppermute | solution.py:37
  115.0 11.3 %collective-permute-start.20 = (bf16[320,512]{1,0:T(8,128)(2,1)S(1)}, bf16[320,512]{1,0:T(8,128)(2,1)S(1)}, u32[]{:S(2)}, u32[]{:S(2)}) collective-permute-start(bf16[320,512]{1,0:T(8,128)(2,1)S(1)} %get-tuple-element.54), channel_id=1, source_target_pairs={{0,32},{1,129},{2,34},{3,131},{4,36},{5,133},{6,38},{7,135},{8,40}... | collective-permute-start | bytes 983048 | tf_op jit(solution)/shard_map/ppermute | solution.py:37
  116.4 10.1 %collective-permute-start.22 = (bf16[192,512]{1,0:T(8,128)(2,1)S(1)}, bf16[192,512]{1,0:T(8,128)(2,1)S(1)}, u32[]{:S(2)}, u32[]{:S(2)}) collective-permute-start(bf16[192,512]{1,0:T(8,128)(2,1)S(1)} %get-tuple-element.56), channel_id=1, source_target_pairs={{0,48},{1,193},{2,50},{3,195},{4,52},{5,197},{6,54},{7,199},{8,56}... | collective-permute-start | bytes 589832 | tf_op jit(solution)/shard_map/ppermute | solution.py:37
  117.7 12.8 %collective-permute-start.23 = (bf16[192,512]{1,0:T(8,128)(2,1)S(1)}, bf16[192,512]{1,0:T(8,128)(2,1)S(1)}, u32[]{:S(2)}, u32[]{:S(2)}) collective-permute-start(bf16[192,512]{1,0:T(8,128)(2,1)S(1)} %get-tuple-element.57), channel_id=1, source_target_pairs={{0,16},{1,65},{2,18},{3,67},{4,20},{5,69},{6,22},{7,71},{8,24},{9,... | collective-permute-start | bytes 589832 | tf_op jit(solution)/shard_map/ppermute | solution.py:37
  120.1 10.4 %collective-permute-start.24 = (bf16[192,512]{1,0:T(8,128)(2,1)S(1)}, bf16[192,512]{1,0:T(8,128)(2,1)S(1)}, u32[]{:S(2)}, u32[]{:S(2)}) collective-permute-start(bf16[192,512]{1,0:T(8,128)(2,1)S(1)} %get-tuple-element.58), channel_id=1, source_target_pairs={{0,32},{1,129},{2,34},{3,131},{4,36},{5,133},{6,38},{7,135},{8,40}... | collective-permute-start | bytes 589832 | tf_op jit(solution)/shard_map/ppermute | solution.py:37
  126.5 10.5 %collective-permute-start.21 = (bf16[320,512]{1,0:T(8,128)(2,1)S(1)}, bf16[320,512]{1,0:T(8,128)(2,1)S(1)}, u32[]{:S(2)}, u32[]{:S(2)}) collective-permute-start(bf16[320,512]{1,0:T(8,128)(2,1)S(1)} %add_convert_fusion), channel_id=1, source_target_pairs={{0,1},{1,2},{2,3},{3,4},{4,5},{5,6},{6,7},{7,8},{8,9},{9,10},{10,1... | collective-permute-start | bytes 983048 | tf_op jit(solution)/shard_map/ppermute | solution.py:309
  130.6 6.3 %collective-permute-start.25 = (bf16[192,512]{1,0:T(8,128)(2,1)S(1)}, bf16[192,512]{1,0:T(8,128)(2,1)S(1)}, u32[]{:S(2)}, u32[]{:S(2)}) collective-permute-start(bf16[192,512]{1,0:T(8,128)(2,1)S(1)} %add_convert_fusion.1), channel_id=1, source_target_pairs={{0,1},{1,2},{2,3},{3,4},{4,5},{5,6},{6,7},{7,8},{8,9},{9,10},{10,1... | collective-permute-start | bytes 589832 | tf_op jit(solution)/shard_map/ppermute | solution.py:309
